TPU v7x, 128 devices: a whole 4x4x4 slice. The times are simulated.
128 devices in a mesh: ctx: 32 (over y, x_hi, z), tp: 4 (over x_lo, core).
Axes of the slice: x: 4 (x_hi: 2, x_lo: 2; x = x_hi * 2 + x_lo), y: 4, z: 4, core: 2. Of those that a mesh axis runs over, the one named last changes fastest.
Arguments:
- prefill_queries: bfloat16 [6144, 8192], P('ctx', 'tp'), may hold values from -440 to 440, as said below
- prefill_key_values: bfloat16 [2, 6144, 1024], P(None, 'ctx', 'tp'), may hold values from -6 to 6
- fill_doc: int32 [6144], P('ctx'), may hold values from 0 to 3, never falling along the last dimension, each value on 1 to 3072 neighbouring positions
- decode_queries: bfloat16 [4, 32, 8192], P(None, None, 'tp'), may hold values from -440 to 440, as said below
- step_key_values: bfloat16 [4, 2, 32, 1024], P(None, None, None, 'tp'), may hold values from -6 to 6
- stored_key_values: bfloat16 [2, 32, 4096, 1024], P(None, None, 'ctx', 'tp'), may hold values from -6 to 6
- cached_len: int32 [32], replicated, may hold values from 1 to 4096, as said below
Outputs:
- fill_out: bfloat16 [6144, 8192], P('ctx', 'tp')
- step_out: bfloat16 [4, 32, 8192], P(None, None, 'tp')
Inputs may be any that keep to these rules, and one draw needn't show every extreme that they name: `prefill_queries`: queries of order one or larger. `decode_queries`: queries of order one or larger. `fill_doc`: document ids never fall; each document holds at most 3072 positions. `cached_len`: some sequence has all 4096 positions cached.
All inputs are finite; a program needn't handle non-finite values.
Results may differ from a plain program's by a relative error of at most 0.006.
Values may be sent and summed in bfloat16 or wider, within the bound.
No kernel may reach another device: no remote copies, remote signals or barrier semaphores. Data moves between devices by JAX's collectives and lax.ppermute only.
A program may use at most 192 MiB of HBM per device.

v0:
```python
import jax
import jax.numpy as jnp
from jax import lax
from jax.sharding import PartitionSpec as P

QUERY_HEADS = 64
KEY_VALUE_HEADS = 8
HEAD_DIM = 128


NEG = -1e30


def combined_all(value, axis, join):
    pieces = jax.tree.map(lambda part: lax.all_gather(part, axis), value)
    head = jax.tree.map(lambda part: part[0], pieces)
    tail = jax.tree.map(lambda part: part[1:], pieces)
    subtotal, _ = lax.scan(lambda subtotal, share: (join(subtotal, share), None), head, tail)
    return subtotal


def join_partials(first, second):
    peak = jnp.maximum(first[0], second[0])
    left = jnp.exp(first[0] - peak)
    right = jnp.exp(second[0] - peak)
    total = first[1] * left + second[1] * right
    summed = first[2] * left[..., None] + second[2] * right[..., None]
    return (peak, total, summed)


def reduce_context(peak, total, summed):
    return combined_all((peak, total, summed), "ctx", join_partials)


def local(
    prefill_queries,
    prefill_key_values,
    fill_doc,
    decode_queries,
    step_key_values,
    stored_key_values,
    cached_len,
):
    head_size = HEAD_DIM
    scale = head_size ** (-0.5)
    query_group = QUERY_HEADS // KEY_VALUE_HEADS
    rows = prefill_queries.shape[0]
    kv_heads = prefill_key_values.shape[2] // head_size
    all_docs = lax.all_gather(fill_doc, "ctx", axis=0, tiled=True)
    q_pos = lax.axis_index("ctx") * rows + jnp.arange(rows, dtype=jnp.int32)
    q_heads = prefill_queries.reshape(rows, kv_heads, query_group, head_size).transpose(1, 2, 0, 3)
    start_state = (
        jnp.full((kv_heads, query_group, rows), NEG, jnp.float32),
        jnp.zeros((kv_heads, query_group, rows), jnp.float32),
        jnp.zeros((kv_heads, query_group, rows, head_size), jnp.float32),
    )
    fold_piece = lax.all_gather(prefill_key_values, "ctx", axis=1, tiled=True)
    count = fold_piece.shape[1]
    k_pos = jnp.arange(count, dtype=jnp.int32)
    visible = (all_docs[None, :] == fill_doc[:, None]) & (k_pos[None, :] <= q_pos[:, None])
    visible = visible & (k_pos[None, :] >= 0)
    key_rows = fold_piece[0].reshape(count, kv_heads, head_size).transpose(1, 0, 2)
    value_rows = fold_piece[1].reshape(count, kv_heads, head_size).transpose(1, 0, 2)

    def one_head(item):
        single_query, key_head, value_head, peak, total, summed = item
        scores = (
            jnp.einsum("gqd,kd->gqk", single_query, key_head, preferred_element_type=jnp.float32)
            * scale
        )
        scores = jnp.where(visible[None], scores, NEG)
        new_peak = jnp.maximum(peak, jnp.max(scores, axis=-1))
        factor = jnp.exp(peak - new_peak)
        weights = jnp.where(visible[None], jnp.exp(scores - new_peak[..., None]), 0.0)
        total = total * factor + jnp.sum(weights, axis=-1)
        added = jnp.einsum(
            "gqk,kd->gqd",
            weights.astype(jnp.bfloat16),
            value_head,
            preferred_element_type=jnp.float32,
        )
        return (new_peak, total, summed * factor[..., None] + added)

    def compute(operand):
        return lax.map(
            one_head,
            (q_heads, key_rows, value_rows, start_state[0], start_state[1], start_state[2]),
        )

    def keep(operand):
        return start_state

    final = lax.cond(jnp.any(visible), compute, keep, 0)
    fill_out = (
        (final[2] / final[1][..., None])
        .transpose(2, 0, 1, 3)
        .reshape(rows, kv_heads * query_group * head_size)
    )
    fill_out = fill_out.astype(jnp.bfloat16)
    steps, seqs = (decode_queries.shape[0], decode_queries.shape[1])
    cache_rows = stored_key_values.shape[2]
    c_pos = lax.axis_index("ctx") * cache_rows + jnp.arange(cache_rows, dtype=jnp.int32)
    live = c_pos[None, :] < cached_len[:, None]
    query_rows = decode_queries.reshape(steps, seqs, kv_heads, query_group, head_size)
    stored_keys = stored_key_values[0].reshape(seqs, cache_rows, kv_heads, head_size)
    stored_values = stored_key_values[1].reshape(seqs, cache_rows, kv_heads, head_size)
    scores = (
        jnp.einsum("tshgd,schd->tshgc", query_rows, stored_keys, preferred_element_type=jnp.float32)
        * scale
    )
    mask = live[None, :, None, None, :]
    scores = jnp.where(mask, scores, NEG)
    peak = jnp.max(scores, axis=-1)
    weights = jnp.where(mask, jnp.exp(scores - peak[..., None]), 0.0)
    total = jnp.sum(weights, axis=-1)
    summed = jnp.einsum(
        "tshgc,schd->tshgd",
        weights.astype(jnp.bfloat16),
        stored_values,
        preferred_element_type=jnp.float32,
    )
    pieces = [
        reduce_context(peak[decode_index], total[decode_index], summed[decode_index])
        for decode_index in range(steps)
    ]
    peak = jnp.stack([piece[0] for piece in pieces])
    total = jnp.stack([piece[1] for piece in pieces])
    summed = jnp.stack([piece[2] for piece in pieces])
    step_keys = step_key_values[:, 0].reshape(steps, seqs, kv_heads, head_size)
    step_values = step_key_values[:, 1].reshape(steps, seqs, kv_heads, head_size)
    fresh = (
        jnp.einsum("tshgd,ushd->tshgu", query_rows, step_keys, preferred_element_type=jnp.float32)
        * scale
    )
    seen = jnp.arange(steps)[None, :] <= jnp.arange(steps)[:, None]
    seen = seen[:, None, None, None, :]
    fresh = jnp.where(seen, fresh, NEG)
    top = jnp.maximum(peak, jnp.max(fresh, axis=-1))
    factor = jnp.exp(peak - top)
    fresh_w = jnp.where(seen, jnp.exp(fresh - top[..., None]), 0.0)
    total = total * factor + jnp.sum(fresh_w, axis=-1)
    added = jnp.einsum(
        "tshgu,ushd->tshgd",
        fresh_w.astype(jnp.bfloat16),
        step_values,
        preferred_element_type=jnp.float32,
    )
    summed = summed * factor[..., None] + added
    step_out = (
        (summed / total[..., None])
        .reshape(steps, seqs, kv_heads * query_group * head_size)
        .astype(jnp.bfloat16)
    )
    return (fill_out, step_out)


def solution(mesh):
    placed = (
        P("ctx", "tp"),
        P(None, "ctx", "tp"),
        P("ctx"),
        P(None, None, "tp"),
        P(None, None, None, "tp"),
        P(None, None, "ctx", "tp"),
        P(),
    )
    return jax.shard_map(
        local,
        mesh=mesh,
        in_specs=placed,
        out_specs=(P("ctx", "tp"), P(None, None, "tp")),
        check_vma=False,
    )
```

profile of v0, /device:TPU:4, one launch (start us, length us, event | category | flops | bytes accessed | tf_op | source)
XLA Modules:
  0.0 1413.6 jit_solution(15682053109479662096)
XLA Ops:
  7.2 1.8 copy.149
  9.1 4.0 fusion.78
  13.1 4.1 copy.203
  17.4 3.0 copy.204
  20.4 2.4 fusion.83
  22.8 2.9 convolution_bitcast_fusion
  29.6 87.8 %all_gather.53 = f32[32,32,2,8]{1,3,2,0:T(8,128)S(1)} all-gather(f32[1,32,2,8]{1,3,2,0:T(8,128)S(1)} %copy.170), channel_id=1, replica_groups=mesh['ctx'=32,'tp'=4] {'ctx'}, dimensions={0}, use_global_device_ids=true | all-gather | bytes 67584 | tf_op jit(solution)/shard_map/all_gather | solution.py:15
  118.9 90.1 %all_gather.54 = f32[32,32,2,8]{1,3,2,0:T(8,128)S(1)} all-gather(f32[1,32,2,8]{1,3,2,0:T(8,128)S(1)} %copy.171), channel_id=1, replica_groups=mesh['ctx'=32,'tp'=4] {'ctx'}, dimensions={0}, use_global_device_ids=true | all-gather | bytes 67584 | tf_op jit(solution)/shard_map/all_gather | solution.py:15
  210.4 91.4 %all_gather.50 = f32[32,32,2,8]{1,3,2,0:T(8,128)S(1)} all-gather(f32[1,32,2,8]{1,3,2,0:T(8,128)S(1)} %copy.167), channel_id=1, replica_groups=mesh['ctx'=32,'tp'=4] {'ctx'}, dimensions={0}, use_global_device_ids=true | all-gather | bytes 67584 | tf_op jit(solution)/shard_map/all_gather | solution.py:15
  303.3 89.6 %all_gather.51 = f32[32,32,2,8]{1,3,2,0:T(8,128)S(1)} all-gather(f32[1,32,2,8]{1,3,2,0:T(8,128)S(1)} %copy.168), channel_id=1, replica_groups=mesh['ctx'=32,'tp'=4] {'ctx'}, dimensions={0}, use_global_device_ids=true | all-gather | bytes 67584 | tf_op jit(solution)/shard_map/all_gather | solution.py:15
  394.3 92.0 %all_gather.47 = f32[32,32,2,8]{1,3,2,0:T(8,128)S(1)} all-gather(f32[1,32,2,8]{1,3,2,0:T(8,128)S(1)} %copy.164), channel_id=1, replica_groups=mesh['ctx'=32,'tp'=4] {'ctx'}, dimensions={0}, use_global_device_ids=true | all-gather | bytes 67584 | tf_op jit(solution)/shard_map/all_gather | solution.py:15
  487.7 89.0 %all_gather.48 = f32[32,32,2,8]{1,3,2,0:T(8,128)S(1)} all-gather(f32[1,32,2,8]{1,3,2,0:T(8,128)S(1)} %copy.165), channel_id=1, replica_groups=mesh['ctx'=32,'tp'=4] {'ctx'}, dimensions={0}, use_global_device_ids=true | all-gather | bytes 67584 | tf_op jit(solution)/shard_map/all_gather | solution.py:15
  578.0 90.4 %all_gather.44 = f32[32,32,2,8]{1,3,2,0:T(8,128)S(1)} all-gather(f32[1,32,2,8]{1,3,2,0:T(8,128)S(1)} %copy.159), channel_id=1, replica_groups=mesh['ctx'=32,'tp'=4] {'ctx'}, dimensions={0}, use_global_device_ids=true | all-gather | bytes 67584 | tf_op jit(solution)/shard_map/all_gather | solution.py:15
  669.8 88.9 %all_gather.45 = f32[32,32,2,8]{1,3,2,0:T(8,128)S(1)} all-gather(f32[1,32,2,8]{1,3,2,0:T(8,128)S(1)} %copy.160), channel_id=1, replica_groups=mesh['ctx'=32,'tp'=4] {'ctx'}, dimensions={0}, use_global_device_ids=true | all-gather | bytes 67584 | tf_op jit(solution)/shard_map/all_gather | solution.py:15
  761.6 177.8 %all-reduce = s32[6144]{0:T(1024)S(1)} all-reduce(s32[6144]{0:T(1024)S(1)} %dynamic-update-slice), channel_id=1, replica_groups=mesh['ctx'=32,'tp'=4] {'ctx'}, use_global_device_ids=true, to_apply=%add | all-reduce | flops 6144 | bytes 49152
  939.5 3.3 fusion.43
  944.5 3.3 fusion.84
  949.1 13.6 fusion.77
  962.7 13.5 copy.201
  976.3 13.5 copy.202
  989.8 112.2 %conditional.1 = (f32[2,8,192]{2,1,0:T(8,128)}, f32[2,8,192,128]{3,2,1,0:T(8,128)}) conditional(s32[]{:T(128)} %convert_element_type.27, () %tuple.36, (pred[192,6144]{1,0:T(8,128)(4,1)}, bf16[2,8,192,128]{3,1,0,2:T(8,128)(2,1)}, bf16[2,6144,128]{1,2,0:T(8,128)(2,1)}, bf16[2,6144,128]{1,2,0:T(8,128)(2,1)}) %tuple.178), branch_computations={%region_1.0_spmd, %region_2.7_spmd} | conditional | flops 4954725888 | bytes 126686432 | solution.py:93
  989.8 112.2 %while.67 = (s32[]{:T(128)}, f32[2,8,192]{2,1,0:T(8,128)}, f32[2,8,192,128]{3,2,1,0:T(8,128)}, pred[192,6144]{1,0:T(8,128)(4,1)}, bf16[2,8,192,128]{3,1,0,2:T(8,...) while((s32[]{:T(128)}, f32[2,8,192]{2,1,0:T(8,128)}, ...), condition=%wide.region_6.6_spmd, body=%wide.region_3.5_spmd.sunk | while | flops 4954725888 | bytes 126686344 | solution.py:85
  990.9 17.8 %fusion.110 = (f32[8,192]{1,0:T(8,128)S(1)}, f32[8,192,6144]{2,1,0:T(8,128)}) fusion(pred[192,6144]{1,0:T(8,128)(4,1)} %get-tuple-element.770, bf16[2,6144,128]{1,2,0:T(8,128)(2,1)} %get-tuple-element.772, s32[]{:T(128)S(6)} %copy.251, bf16[1,8,192,128]{3,1,0,2:T(8,128)(2,1)S(1)} %constant_dynamic-slice_fusion.2), kind=kOutput, calls=%fused_computation.2.clone.1 | convolution fusion | flops 2444229120 | bytes 40900612 | tf_op jit(solution)/shard_map/cond/branch_1_fun/while/body/eval_jaxpr/gqd,kd->gqk/dot_general | solution.py:68
  1008.7 18.6 %fusion.111 = f32[8,192]{1,0:T(8,128)S(1)} fusion(f32[8,192,6144]{2,1,0:T(8,128)} %get-tuple-element.747, f32[8,192]{1,0:T(8,128)S(1)} %get-tuple-element.749, pred[192,6144]{1,0:T(8,128)(4,1)S(1)} %copy-done), kind=kLoop, calls=%fused_computation.4.clone.1 | loop fusion | flops 47184384 | bytes 38940672 | tf_op jit(solution)/shard_map/cond/branch_1_fun/while/body/eval_jaxpr/reduce_sum | solution.py:75
  1027.9 18.0 %fusion.112 = f32[2,8,192,128]{3,2,1,0:T(8,128)} fusion(f32[2,8,192,128]{3,2,1,0:T(8,128)} %get-tuple-element.761, s32[]{:T(128)S(6)} %copy.251, bf16[2,6144,128]{1,2,0:T(8,128)(2,1)} %get-tuple-element.773, f32[8,192,6144]{2,1,0:T(8,128)} %get-tuple-element.747, f32[8,192]{1,0:T(8,128)S(1)} %get-tuple-element.749, ...), kind=kOutput, calls=%fused_computation.14.clone.1 | convolution fusion | flops 2463301632 | bytes 41300992 | tf_op jit(solution)/shard_map/cond/branch_1_fun/while/body/eval_jaxpr/gqk,kd->gqd/dot_general | solution.py:76
  1047.0 17.8 %fusion.110 = (f32[8,192]{1,0:T(8,128)S(1)}, f32[8,192,6144]{2,1,0:T(8,128)}) fusion(pred[192,6144]{1,0:T(8,128)(4,1)} %get-tuple-element.770, bf16[2,6144,128]{1,2,0:T(8,128)(2,1)} %get-tuple-element.772, s32[]{:T(128)S(6)} %copy.251, bf16[1,8,192,128]{3,1,0,2:T(8,128)(2,1)S(1)} %constant_dynamic-slice_fusion.2), kind=kOutput, calls=%fused_computation.2.clone.1 | convolution fusion | flops 2444229120 | bytes 40900612 | tf_op jit(solution)/shard_map/cond/branch_1_fun/while/body/eval_jaxpr/gqd,kd->gqk/dot_general | solution.py:68
  1064.8 18.6 %fusion.111 = f32[8,192]{1,0:T(8,128)S(1)} fusion(f32[8,192,6144]{2,1,0:T(8,128)} %get-tuple-element.747, f32[8,192]{1,0:T(8,128)S(1)} %get-tuple-element.749, pred[192,6144]{1,0:T(8,128)(4,1)S(1)} %copy-done), kind=kLoop, calls=%fused_computation.4.clone.1 | loop fusion | flops 47184384 | bytes 38940672 | tf_op jit(solution)/shard_map/cond/branch_1_fun/while/body/eval_jaxpr/reduce_sum | solution.py:75
  1084.0 18.0 %fusion.112 = f32[2,8,192,128]{3,2,1,0:T(8,128)} fusion(f32[2,8,192,128]{3,2,1,0:T(8,128)} %get-tuple-element.761, s32[]{:T(128)S(6)} %copy.251, bf16[2,6144,128]{1,2,0:T(8,128)(2,1)} %get-tuple-element.773, f32[8,192,6144]{2,1,0:T(8,128)} %get-tuple-element.747, f32[8,192]{1,0:T(8,128)S(1)} %get-tuple-element.749, ...), kind=kOutput, calls=%fused_computation.14.clone.1 | convolution fusion | flops 2463301632 | bytes 41300992 | tf_op jit(solution)/shard_map/cond/branch_1_fun/while/body/eval_jaxpr/gqk,kd->gqd/dot_general | solution.py:76
  1102.0 1.9 fusion.53
  1106.5 7.0 slice.205
  1113.5 66.5 %while.71 = (s32[]{:T(128)}, f32[32,2,8]{0,2,1:T(8,128)S(1)}, f32[32,2,8]{0,2,1:T(8,128)S(1)}, f32[32,2,8,128]{3,2,1,0:T(8,128)S(1)}, f32[31,32,2,8]{1,3,2,0:T(8...) while((s32[]{:T(128)}, f32[32,2,8]{0,2,1:T(8,128)S(1)}, ...), condition=%wide.region_16.17_spmd, body=%wide.region_15.16_spmd.sunk | while | flops 199682 | bytes 815205 | solution.py:18
  1114.4 1.2 fusion.107
  1116.6 1.2 fusion.107
  1118.7 1.2 fusion.107
  1123.0 1.2 fusion.107
  1127.3 1.2 fusion.107
  1133.7 1.2 fusion.107
  1138.0 1.2 fusion.107
  1142.3 1.2 fusion.107
  1146.6 1.2 fusion.107
  1150.9 1.2 fusion.107
  1153.0 1.2 fusion.107
  1155.2 1.2 fusion.107
  1157.3 1.2 fusion.107
  1159.5 1.2 fusion.107
  1161.6 1.2 fusion.107
  1163.7 1.2 fusion.107
  1165.9 1.2 fusion.107
  1168.0 1.2 fusion.107
  1170.2 1.2 fusion.107
  1172.3 1.2 fusion.107
  1174.5 1.2 fusion.107
  1176.6 1.2 fusion.107
  1181.0 7.0 slice.196
  1188.0 66.5 %while.70 = (s32[]{:T(128)}, f32[32,2,8]{0,2,1:T(8,128)S(1)}, f32[32,2,8]{0,2,1:T(8,128)S(1)}, f32[32,2,8,128]{3,2,1,0:T(8,128)S(1)}, f32[31,32,2,8]{1,3,2,0:T(8...) while((s32[]{:T(128)}, f32[32,2,8]{0,2,1:T(8,128)S(1)}, ...), condition=%wide.region_14.15_spmd, body=%wide.region_13.14_spmd.sunk | while | flops 199682 | bytes 815205 | solution.py:18
  1188.9 1.2 fusion.105
  1191.1 1.2 fusion.105
  1193.2 1.2 fusion.105
  1195.4 1.2 fusion.105
  1199.7 1.2 fusion.105
  1254.6 7.0 slice.187
  1262.6 66.5 %while.69 = (s32[]{:T(128)}, f32[32,2,8]{0,2,1:T(8,128)S(1)}, f32[32,2,8]{0,2,1:T(8,128)S(1)}, f32[32,2,8,128]{3,2,1,0:T(8,128)S(1)}, f32[31,32,2,8]{1,3,2,0:T(8...) while((s32[]{:T(128)}, f32[32,2,8]{0,2,1:T(8,128)S(1)}, ...), condition=%wide.region_12.13_spmd, body=%wide.region_11.12_spmd.sunk | while | flops 199682 | bytes 815205 | solution.py:18
  1330.1 7.1 slice.178
  1337.2 66.5 %while.68 = (s32[]{:T(128)}, f32[32,2,8]{0,2,1:T(8,128)S(1)}, f32[32,2,8]{0,2,1:T(8,128)S(1)}, f32[32,2,8,128]{3,2,1,0:T(8,128)S(1)}, f32[31,32,2,8]{1,3,2,0:T(8...) while((s32[]{:T(128)}, f32[32,2,8]{0,2,1:T(8,128)S(1)}, ...), condition=%wide.region_10.11_spmd, body=%wide.region_9.10_spmd.sunk | while | flops 199682 | bytes 815205 | solution.py:18
  (591 shorter events, 260.3 us)
Async XLA Ops:
  7.2 942.0 %all-gather.6.cloned.1.call-start = ((), (), s32[]{:S(2)}) async-start(), calls=%async_computation | async-start | bytes 6488064 | tf_op jit(solution)/shard_map/all_gather | solution.py:57
  9.0 1096.5 %all-gather.14.cloned.1.call-start = ((), (), s32[]{:S(2)}) async-start(), calls=%async_computation.4 | async-start | bytes 8650752 | tf_op jit(solution)/shard_map/all_gather | solution.py:15
  9.1 8.2 copy-start.2
  13.1 7.2 copy-start.16
  25.7 734.4 %copy-start.19 = (u32[128]{0:T(128)S(1)}, u32[128]{0:T(128)}, u32[]{:S(2)}) copy-start(u32[128]{0:T(128)} %constant.99) | copy-start | bytes 1540
  25.7 735.6 %copy-start.15 = (s32[192]{0:T(256)S(1)}, s32[192]{0:T(256)}, u32[]{:S(2)}) copy-start(s32[192]{0:T(256)} %param.21) | copy-start | bytes 2308
  25.7 917.7 %copy-start.1 = (bf16[192,2048]{1,0:T(8,128)(2,1)S(1)}, bf16[192,2048]{1,0:T(8,128)(2,1)}, u32[]{:S(2)}) copy-start(bf16[192,2048]{1,0:T(8,128)(2,1)} %param.19) | copy-start | bytes 2359300
  26.7 917.7 %copy-start.13 = (bf16[4,2,32,256]{3,2,1,0:T(8,128)(2,1)S(1)}, bf16[4,2,32,256]{3,2,1,0:T(8,128)(2,1)}, u32[]{:S(2)}) copy-start(bf16[4,2,32,256]{3,2,1,0:T(8,128)(2,1)} %param.23) | copy-start | bytes 393220
  26.8 1153.2 %all-gather.12.cloned.1.call-start = ((), (), s32[]{:S(2)}) async-start(), calls=%async_computation.3 | async-start | bytes 8650752 | tf_op jit(solution)/shard_map/all_gather | solution.py:15
  27.5 1227.1 %all-gather.10.cloned.1.call-start = ((), (), s32[]{:S(2)}) async-start(), calls=%async_computation.2 | async-start | bytes 8650752 | tf_op jit(solution)/shard_map/all_gather | solution.py:15
  28.1 1301.0 %all-gather.8.cloned.1.call-start = ((), (), s32[]{:S(2)}) async-start(), calls=%async_computation.1 | async-start | bytes 8650752 | tf_op jit(solution)/shard_map/all_gather | solution.py:15
  760.1 202.7 %copy-start.17 = (pred[4,4]{1,0:T(4,128)(4,1)}, pred[4,4]{1,0:T(4,128)(4,1)S(1)}, u32[]{:S(2)}) copy-start(pred[4,4]{1,0:T(4,128)(4,1)S(1)} %iota_compare_fusion.1) | copy-start | bytes 52
  990.9 17.8 %copy-start = (pred[192,6144]{1,0:T(8,128)(4,1)S(1)}, pred[192,6144]{1,0:T(8,128)(4,1)}, u32[]{:S(2)}) copy-start(pred[192,6144]{1,0:T(8,128)(4,1)} %get-tuple-element.770) | copy-start | bytes 3538948 | tf_op jit(solution)/shard_map/cond/branch_1_fun/while
  1047.0 17.8 %copy-start = (pred[192,6144]{1,0:T(8,128)(4,1)S(1)}, pred[192,6144]{1,0:T(8,128)(4,1)}, u32[]{:S(2)}) copy-start(pred[192,6144]{1,0:T(8,128)(4,1)} %get-tuple-element.770) | copy-start | bytes 3538948 | tf_op jit(solution)/shard_map/cond/branch_1_fun/while
  1106.5 7.0 copy-start.7
  1106.5 7.0 copy-start.11
  1181.0 7.0 copy-start.6
  1181.0 7.0 copy-start.10
  1254.5 8.0 copy-start.5
  1254.5 8.0 copy-start.9
  1330.1 7.1 copy-start.4
  1330.1 7.1 copy-start.8
  1330.1 73.6 %copy-start.12 = (f32[4,32,2,8]{1,3,2,0:T(8,128)S(1)}, f32[4,32,2,8]{1,3,2,0:T(8,128)}, u32[]{:S(2)}) copy-start(f32[4,32,2,8]{1,3,2,0:T(8,128)} %copy.175) | copy-start | bytes 24580
  1330.1 73.8 %copy-start.3 = (f32[4,32,2,8,4]{3,4,0,2,1:T(4,128)S(1)}, f32[4,32,2,8,4]{3,4,0,2,1:T(4,128)}, u32[]{:S(2)}) copy-start(f32[4,32,2,8,4]{3,4,0,2,1:T(4,128)} %get-tuple-element.495) | copy-start | bytes 98308
  1330.1 73.8 %copy-start.18 = (pred[4,4]{1,0:T(4,128)(4,1)S(1)}, pred[4,4]{1,0:T(4,128)(4,1)}, u32[]{:S(2)}) copy-start(pred[4,4]{1,0:T(4,128)(4,1)} %copy-done.17) | copy-start | bytes 52
  1337.2 67.6 %copy-start.14 = (bf16[4,32,2,128]{3,2,1,0:T(2,128)(2,1)S(1)}, bf16[4,32,2,128]{3,2,1,0:T(2,128)(2,1)}, u32[]{:S(2)}) copy-start(bf16[4,32,2,128]{3,2,1,0:T(2,128)(2,1)} %reshape_squeeze.23) | copy-start | bytes 196612
Sparse Core Ops, SparseCore 0:
  11.1 93.0 all-gather.5
  106.9 100.3 all-gather.13
  210.1 100.9 all-gather.11
  313.8 100.7 all-gather.9
  417.1 100.8 all-gather.7
where the time goes:
time: 1440 us; the launch traced here: 1410 us
  blocking collectives  897 us (62%)
  other arithmetic  286 us (20%)
  local copies, waits for them, and re-layouts  128 us (9%)
  matrix products  81.3 us (6%)
  between operations  15.5 us (1%)
    all_gather x8, blocking collectives, combined_all(): pieces = jax.tree.map(lambda part: lax.all_gather(part, axis), value)  719 us
    unnamed x1, blocking collectives  178 us
    add x124, other arithmetic, join_partials(): summed = first[2] * left[..., None] + second[2] * right[..., None]  151 us
    add x124, other arithmetic, join_partials(): total = first[1] * left + second[1] * right  90.7 us
    unnamed x49, local copies, waits for them, and re-layouts  39.2 us
    reduce_sum x2, other arithmetic, one_head(): total = total * factor + jnp.sum(weights, axis=-1)  37.2 us
    dot_general x2, matrix products, one_head(): jnp.einsum('gqk,kd->gqd', weights.astype(jnp.bfloat16), value_head, prefe...  36 us
    dot_general x2, matrix products, one_head(): jnp.einsum('gqd,kd->gqk', single_query, key_head, preferred_element_type=...  35.6 us
  transfers between devices with their start and end apart: 5, of which 0 were waited for; matrix products, arithmetic and copies ran while one was open for 29% of the time, Pallas kernels for 0%

commit v1 on v0

v1 whole, which is shorter than its diff:
```python
import functools

import jax
import jax.numpy as jnp
from jax import lax
from jax.experimental import pallas as pl
from jax.experimental.pallas import tpu as pltpu
from jax.sharding import Mesh
from jax.sharding import PartitionSpec as P

HEAD_DIM = 128
GROUP = 8
STEPS = 4
SEQS = 32
SLOTS = 128
ROWS = 192
KV_HEADS = 2
HEADS = KV_HEADS * GROUP
PER_SEQ = STEPS * HEADS
PACKED = PER_SEQ + 16
BLOCK = 2 * ROWS + 16
FUSED = 4
LANES = FUSED * ROWS
CHUNK = 256
STATE = HEAD_DIM + 16
HIDDEN = -1e30
FLOOR = -1e20
TO_LOG2 = HEAD_DIM**-0.5 * 1.4426950408889634
CTX = ("y", "xh", "z")
PLANE = ("xh", "z")

NT = (((1,), (1,)), ((), ()))
TN = (((0,), (0,)), ((), ()))


def dot(a, b, dims):
    return lax.dot_general(a, b, dims, preferred_element_type=jnp.float32)


def decode_kernel(len_ref, me_ref, q_ref, kv_ref, fresh_ref, out_ref, *, per_step):
    base = pl.program_id(0) * per_step
    me = me_ref[0]
    lane = lax.broadcasted_iota(jnp.int32, (STEPS * GROUP, SLOTS), 1)
    stat_lane = lax.broadcasted_iota(jnp.int32, (STEPS * GROUP, HEAD_DIM), 1)
    pick = (
        lax.broadcasted_iota(jnp.int32, (16, HEAD_DIM), 0)
        == lax.broadcasted_iota(jnp.int32, (16, HEAD_DIM), 1)
    ).astype(jnp.bfloat16)
    row_step = lax.broadcasted_iota(jnp.int32, (STEPS * GROUP, 16), 0) // GROUP
    fresh_step = lax.broadcasted_iota(jnp.int32, (STEPS * GROUP, 16), 1)
    fresh_mask = fresh_step <= row_step

    def one(i, with_fresh):
        seq = base + i
        stats = []
        for h in range(KV_HEADS):
            at = pl.ds(h * HEAD_DIM, HEAD_DIM)
            rows = pl.ds(h * STEPS * GROUP, STEPS * GROUP)
            q = q_ref[i, rows, :]
            s = dot(q, kv_ref[0, i, :, at], NT) * TO_LOG2
            s = jnp.where(lane < len_ref[seq] - me * SLOTS, s, HIDDEN)
            m = jnp.maximum(jnp.max(s, axis=1, keepdims=True), FLOOR)
            if with_fresh:
                f = dot(q, fresh_ref[0, :, at], NT) * TO_LOG2
                f = jnp.where(fresh_mask, f, HIDDEN)
                m = jnp.maximum(m, jnp.max(f, axis=1, keepdims=True))
            m_hi = m.astype(jnp.bfloat16).astype(jnp.float32)
            m_lo = (m - m_hi).astype(jnp.bfloat16).astype(jnp.float32)
            m = m_hi + m_lo
            p = jnp.exp2(s - m)
            total = jnp.sum(p, axis=1, keepdims=True)
            o = dot(p.astype(jnp.bfloat16), kv_ref[1, i, :, at], (((1,), (0,)), ((), ())))
            if with_fresh:
                pf = jnp.exp2(f - m)
                total = total + jnp.sum(pf, axis=1, keepdims=True)
                o = o + dot(pf.astype(jnp.bfloat16), fresh_ref[1, :, at], (((1,), (0,)), ((), ())))
            l_hi = total.astype(jnp.bfloat16).astype(jnp.float32)
            l_lo = total - l_hi
            out_ref[i, rows, :] = o.astype(jnp.bfloat16)
            st = jnp.where(
                stat_lane == 0, m_hi, jnp.where(stat_lane == 1, m_lo, jnp.where(stat_lane == 2, l_hi, l_lo))
            )
            stats.append(st.astype(jnp.bfloat16))
        stats = jnp.concatenate(stats + [jnp.zeros((HEAD_DIM - PER_SEQ, HEAD_DIM), jnp.bfloat16)], axis=0)
        out_ref[i, PER_SEQ:, :] = dot(pick, stats, NT).astype(jnp.bfloat16)

    for i in range(per_step):
        one(i, False)
    for i in range(per_step):

        @pl.when(base + i == me)
        def _():
            one(i, True)


def decode_partials(lens, me, queries, cache, fresh):
    per_step = 4
    return pl.pallas_call(
        functools.partial(decode_kernel, per_step=per_step),
        grid_spec=pltpu.PrefetchScalarGridSpec(
            num_scalar_prefetch=2,
            grid=(SEQS // per_step,),
            in_specs=[
                pl.BlockSpec((per_step, PER_SEQ, HEAD_DIM), lambda i, *_: (i, 0, 0)),
                pl.BlockSpec((2, per_step, SLOTS, KV_HEADS * HEAD_DIM), lambda i, *_: (0, i, 0, 0)),
                pl.BlockSpec((2, 16, KV_HEADS * HEAD_DIM), lambda i, *_: (0, 0, 0)),
            ],
            out_specs=pl.BlockSpec((per_step, PACKED, HEAD_DIM), lambda i, *_: (i, 0, 0)),
        ),
        out_shape=jax.ShapeDtypeStruct((SEQS, PACKED, HEAD_DIM), jnp.bfloat16),
        compiler_params=pltpu.CompilerParams(vmem_limit_bytes=32 * 1024 * 1024),
        cost_estimate=pl.CostEstimate(flops=70_000_000, bytes_accessed=5_500_000, transcendentals=262144),
        name="decode_partials",
    )(lens, me, queries, cache, fresh)


def join_kernel(in_ref, out_ref, coef):
    peaks, totals = [], []
    for i in range(SEQS):
        st = in_ref[i, PER_SEQ:, :].astype(jnp.float32)
        peaks.append(st[0:1] + st[1:2])
        totals.append(st[2:3] + st[3:4])
    top = functools.reduce(jnp.maximum, peaks)
    scales = [jnp.exp2(m - top) for m in peaks]
    total = functools.reduce(jnp.add, [a * b for a, b in zip(scales, totals)])
    coef[...] = jnp.zeros_like(coef)
    for i in range(SEQS):
        coef[i : i + 1, :] = scales[i] / total
    columns = jnp.transpose(coef[...])
    acc = jnp.zeros((PER_SEQ, HEAD_DIM), jnp.float32)
    for i in range(SEQS):
        acc = acc + in_ref[i, :PER_SEQ, :].astype(jnp.float32) * columns[:PER_SEQ, i : i + 1]
    out_ref[...] = acc.astype(jnp.bfloat16)


def join_shares(shares):
    return pl.pallas_call(
        join_kernel,
        out_shape=jax.ShapeDtypeStruct((PER_SEQ, HEAD_DIM), jnp.bfloat16),
        in_specs=[pl.BlockSpec(memory_space=pltpu.VMEM)],
        out_specs=pl.BlockSpec(memory_space=pltpu.VMEM),
        scratch_shapes=[pltpu.VMEM((HEAD_DIM, HEAD_DIM), jnp.float32)],
        cost_estimate=pl.CostEstimate(flops=1_000_000, bytes_accessed=700_000, transcendentals=4096),
        name="join_shares",
    )(shares)


def prefill_kernel(valid_ref, info_ref, q_ref, *refs, counts, first, last):
    n_in = len(counts)
    blocks = refs[:n_in]
    rest = refs[n_in:]
    if first:
        state_in, rest = None, rest
    else:
        state_in, rest = rest[0], rest[1:]
    out_ref, rest = rest[0], rest[1:]
    if last:
        state, rest = rest[0], rest[1:]
    else:
        state = out_ref.at[0]
    low_ref, flag_ref = rest
    step = pl.program_id(0)
    places = [(r, b) for r, n in enumerate(counts) for b in range(n)]

    @pl.when(step == 0)
    def _():
        doc = info_ref[0:1, :]
        for at, (r, b) in enumerate(places):
            t = blocks[r][b, 2 * ROWS :, :].astype(jnp.float32)[0:1, :].astype(jnp.int32)
            low = jnp.where(doc == 1, t[:, 0:1], jnp.where(doc == 2, t[:, 1:2], jnp.where(doc == 3, t[:, 2:3], 0)))
            low_ref[at, 0:1, :] = low
            lowest, highest = jnp.min(low), jnp.max(low)
            seen = (valid_ref[at] > 0) & (lowest < ROWS)
            flag_ref[at] = jnp.where(seen, jnp.where(highest == 0, 1, 2), 0)

    if first:
        state[0:HEAD_DIM, :] = jnp.zeros((HEAD_DIM, LANES), jnp.float32)
        state[HEAD_DIM : HEAD_DIM + 8, :] = jnp.full((8, LANES), FLOOR, jnp.float32)
        state[HEAD_DIM + 8 :, :] = jnp.zeros((8, LANES), jnp.float32)
    else:
        state[...] = state_in[0]
    queries = jnp.concatenate([q_ref[:, j * HEAD_DIM : (j + 1) * HEAD_DIM] for j in range(FUSED)], axis=0)

    def attend(at, r, b, masked, own):
        keys = blocks[r][b, 0:ROWS, :]
        values = blocks[r][b, ROWS : 2 * ROWS, :]
        for c in range(LANES // CHUNK):
            on = slice(c * CHUNK, (c + 1) * CHUNK)
            s = dot(keys, queries[on], NT)
            if masked:
                j = lax.broadcasted_iota(jnp.int32, (ROWS, CHUNK), 0)
                sees = j >= low_ref[at, 0:1, on]
                if own:
                    sees = sees & (j <= info_ref[1:2, on])
                s = jnp.where(sees, s, HIDDEN)
            old = state[HEAD_DIM : HEAD_DIM + 1, on]
            peak = jnp.maximum(old, jnp.max(s, axis=0, keepdims=True))
            factor = jnp.exp2((old - peak) * TO_LOG2)
            p = jnp.exp2((s - peak) * TO_LOG2)
            total = state[HEAD_DIM + 8 : HEAD_DIM + 9, on] * factor + jnp.sum(p, axis=0, keepdims=True)
            state[HEAD_DIM : HEAD_DIM + 1, on] = peak
            state[HEAD_DIM + 8 : HEAD_DIM + 9, on] = total
            state[0:HEAD_DIM, on] = state[0:HEAD_DIM, on] * factor + dot(values, p.astype(jnp.bfloat16), TN)

    for at, (r, b) in enumerate(places):
        if first and at == 0:
            attend(at, r, b, True, True)
            continue

        @pl.when(flag_ref[at] == 1)
        def _():
            attend(at, r, b, False, False)

        @pl.when(flag_ref[at] == 2)
        def _():
            attend(at, r, b, True, False)

    if last:
        out = state[0:HEAD_DIM, :] / state[HEAD_DIM + 8 : HEAD_DIM + 9, :]
        out = jnp.transpose(out).astype(jnp.bfloat16)
        for j in range(FUSED):
            out_ref[:, j * HEAD_DIM : (j + 1) * HEAD_DIM] = out[j * ROWS : (j + 1) * ROWS]


def prefill_part(valid, info, queries, blocks, state, last, name):
    first = state is None
    counts = [b.shape[0] for b in blocks]
    n = sum(counts)
    steps = HEADS // FUSED
    q_spec = pl.BlockSpec((ROWS, FUSED * HEAD_DIM), lambda i, *_: (0, i))
    state_spec = pl.BlockSpec((1, STATE, LANES), lambda i, *_: (i, 0, 0))
    per_kv = steps // KV_HEADS
    in_specs = [pl.BlockSpec((8, LANES), lambda i, *_: (0, 0)), q_spec]
    in_specs += [pl.BlockSpec((c, BLOCK, HEAD_DIM), lambda i, *_: (0, 0, i // per_kv)) for c in counts]
    operands = [valid, info, queries, *blocks]
    if not first:
        in_specs.append(state_spec)
        operands.append(state)
    scratch = []
    if last:
        out_shape = jax.ShapeDtypeStruct((ROWS, HEADS * HEAD_DIM), jnp.bfloat16)
        out_spec = q_spec
        scratch.append(pltpu.VMEM((STATE, LANES), jnp.float32))
    else:
        out_shape = jax.ShapeDtypeStruct((steps, STATE, LANES), jnp.float32)
        out_spec = state_spec
    scratch += [pltpu.VMEM((n, 8, LANES), jnp.int32), pltpu.SMEM((n,), jnp.int32)]
    return pl.pallas_call(
        functools.partial(prefill_kernel, counts=counts, first=first, last=last),
        grid_spec=pltpu.PrefetchScalarGridSpec(
            num_scalar_prefetch=1,
            grid=(steps,),
            in_specs=in_specs,
            out_specs=out_spec,
            scratch_shapes=scratch,
        ),
        out_shape=out_shape,
        compiler_params=pltpu.CompilerParams(vmem_limit_bytes=48 * 1024 * 1024),
        cost_estimate=pl.CostEstimate(
            flops=4 * n * ROWS * ROWS * HEADS * HEAD_DIM,
            bytes_accessed=n * BLOCK * 512 + 4_000_000,
            transcendentals=n * ROWS * ROWS * HEADS,
        ),
        name=name,
    )(*operands)


def local(prefill_queries, prefill_key_values, fill_doc, decode_queries, step_key_values, stored_key_values, cached_len):
    y = lax.axis_index("y")
    place = lax.axis_index(PLANE)
    me = lax.axis_index(CTX).astype(jnp.int32)

    starts = jnp.sum(fill_doc[None, :] < jnp.arange(1, 4, dtype=jnp.int32)[:, None], axis=1)
    starts = jnp.pad(starts.astype(jnp.bfloat16), (0, HEAD_DIM - 3))
    starts = jnp.pad(jnp.concatenate([starts, starts])[None], ((0, 15), (0, 0)))
    own = jnp.concatenate([prefill_key_values[0], prefill_key_values[1], starts], axis=0)[None]
    back1 = lax.ppermute(own, "y", [(i, i + 1) for i in range(3)])
    back2 = lax.ppermute(own, "y", [(i, i + 2) for i in range(2)])

    queries = decode_queries.reshape(STEPS, SEQS, KV_HEADS, GROUP, HEAD_DIM)
    queries = queries.transpose(1, 2, 0, 3, 4).reshape(SEQS, PER_SEQ, HEAD_DIM)
    fresh = lax.dynamic_index_in_dim(step_key_values, me, axis=2, keepdims=False)
    fresh = jnp.pad(fresh.transpose(1, 0, 2), ((0, 0), (0, 16 - STEPS), (0, 0)))
    shares = decode_partials(cached_len, me[None], queries, stored_key_values, fresh)

    got, flags = [], []
    for k in range(1, 8):
        bit = 1 << (k.bit_length() - 1)
        to_later = (place & bit) == 0
        other = jnp.where(to_later, own, back2)
        packed = jnp.concatenate([back1, other], axis=0)
        got.append(lax.ppermute(packed, PLANE, [(i, i ^ k) for i in range(8)]))
        from_earlier = (place & bit) != 0
        flags.append(jnp.stack([y >= 1, from_earlier | (y >= 2)]).astype(jnp.int32))

    shares = lax.all_to_all(shares, CTX, 0, 0)
    mine = join_shares(shares)
    spread = lax.all_to_all(jnp.broadcast_to(mine[None], (SEQS,) + mine.shape), CTX, 0, 0)
    step_out = spread.reshape(SEQS, KV_HEADS, STEPS, GROUP, HEAD_DIM).transpose(2, 0, 1, 3, 4)
    step_out = step_out.reshape(STEPS, SEQS, HEADS * HEAD_DIM)

    info = jnp.stack([fill_doc, jnp.arange(ROWS, dtype=jnp.int32)])
    info = jnp.pad(jnp.tile(info, (1, FUSED)), ((0, 6), (0, 0)))
    valid0 = jnp.stack([y >= 0, y >= 1, y >= 2]).astype(jnp.int32)
    state = prefill_part(valid0, info, prefill_queries, [own, back1, back2], None, False, "prefill_own")
    for at, (a, b) in enumerate(((0, 2), (2, 4), (4, 7))):
        state = prefill_part(
            jnp.concatenate(flags[a:b]), info, prefill_queries, got[a:b], state, b == 7, "prefill_%d" % at
        )
    return state, step_out


def solution(mesh):
    fine = Mesh(mesh.devices.reshape(4, 2, 4, 2, 2), ("y", "xh", "z", "xl", "c"))
    tp = ("xl", "c")
    placed = (
        P(CTX, tp),
        P(None, CTX, tp),
        P(CTX),
        P(None, None, tp),
        P(None, None, None, tp),
        P(None, None, CTX, tp),
        P(),
    )
    return jax.shard_map(
        local,
        mesh=fine,
        in_specs=placed,
        out_specs=(P(CTX, tp), P(None, None, tp)),
        check_vma=False,
    )
```

time: 1440 us -> 148 us (0.10)
  the two profiles are of different devices: /device:TPU:4 before, /device:TPU:120 now
where the time goes in v1:
time: 148 us; the launch traced here: 150 us
  Pallas kernels  77.7 us (52%)
  starting transfers between devices  42.7 us (29%)
  waiting for transfers between devices  17.8 us (12%)
  local copies, waits for them, and re-layouts  8.42 us (6%)
  other arithmetic  2.54 us (2%)
    pallas_call x4, Pallas kernels, prefill_part(): pl.pallas_call(functools.partial(prefill_kernel, counts=counts, first=fir...  59.3 us
    ppermute x7, waiting for transfers between devices, local(): got.append(lax.ppermute(packed, PLANE, [(i, i ^ k) for i in range(8)]))  16.3 us
    pallas_call x1, Pallas kernels, decode_partials(): pl.pallas_call(functools.partial(decode_kernel, per_step=per_step), grid_...  16.1 us
    ppermute x7, starting transfers between devices, local(): got.append(lax.ppermute(packed, PLANE, [(i, i ^ k) for i in range(8)]))  14.9 us
    all_to_all x1, starting transfers between devices, local(): lax.all_to_all(jnp.broadcast_to(mine[None], (SEQS,) + mine.shape), CTX, 0...  13.2 us
    all_to_all x1, starting transfers between devices, local(): shares = lax.all_to_all(shares, CTX, 0, 0)  12 us
    unnamed x11, local copies, waits for them, and re-layouts  3.36 us
  transfers between devices with their start and end apart: 11, of which 2 were waited for; matrix products, arithmetic and copies ran while one was open for 3% of the time, Pallas kernels for 52%

profile of v1, /device:TPU:120, one launch (start us, length us, event | category | flops | bytes accessed | tf_op | source)
XLA Modules:
  0.0 150.1 jit_solution(2910325814118717181)
XLA Ops:
  0.6 0.0 copy-start
  0.6 0.0 copy-start.3
  0.7 1.0 slice_bitcast_fusion.1
  1.7 0.9 convert_reduce_fusion
  2.6 1.3 collective-permute-start.1
  3.9 1.3 collective-permute-start
  5.2 0.0 copy-done
  5.3 1.1 copy.19
  6.4 0.1 copy.16
  6.6 0.0 copy-done.3
  6.6 0.0 copy-start.1
  6.6 2.2 %copy-done.1 = bf16[2,32,128,256]{3,2,1,0:T(8,128)(2,1)S(1)} copy-done((bf16[2,32,128,256]{3,2,1,0:T(8,128)(2,1)S(1)}, bf16[2,32,128,256]{3,2,1,0:T(8,128)(2,1)}, u32[]{:S(2)}) %copy-start.1) | copy-done | bytes 4194328
  8.8 16.1 %decode_partials.1 = bf16[32,80,128]{2,1,0:T(8,128)(2,1)} custom-call(s32[32]{0:T(128)S(1)} %copy-done.3, s32[1]{0:T(128)} %bitcast.10.me_ref, bf16[32,64,128]{2,1,0:T(8,128)(2,1)S(1)} %bitcast.37, bf16[2,32,128,256]{3,2,1,0:T(8,128)(2,1)S(1)} %copy-done.1, bf16[2,16,256]{2,1,0:T(8,128)(2,1)S(1)} %pad.19.fresh_ref), custom_call_target="tpu_custom_call" | custom-call | flops 70000000 | bytes 5500000 | tf_op jit(solution)/shard_map/decode_partials/pallas_call | solution.py:98
  24.9 12.0 %all-to-all-start = ((bf16[32,80,128]{2,1,0:T(8,128)(2,1)}), bf16[32,80,128]{2,1,0:T(8,128)(2,1)}, u32[]{:S(2)}, u32[]{:S(2)}) async-start(bf16[32,80,128]{2,1,0:T(8,128)(2,1)} %decode_partials.1), calls=%async_computation | async-start | bytes 1310720 | tf_op jit(solution)/shard_map/all_to_all | solution.py:296
  36.9 0.0 copy-start.4
  37.0 0.1 add_convert_fusion.1
  37.0 0.0 collective-permute-done.1.refs_2_
  37.0 0.1 broadcast_select_fusion
  37.2 0.0 collective-permute-done.refs_1_
  37.2 0.0 copy-start.2
  37.2 1.1 pad_maximum_fusion
  38.3 1.4 collective-permute-start.8
  39.8 0.0 collective-permute-start.7
  39.8 0.1 add_convert_fusion
  39.8 0.1 pad_add_fusion.3
  39.9 0.0 copy-done.4
  39.9 2.7 %collective-permute-start.5 = (bf16[2,400,256]{2,1,0:T(8,128)(2,1)}, bf16[2,400,256]{2,1,0:T(8,128)(2,1)S(1)}, u32[]{:S(2)}, u32[]{:S(2)}) collective-permute-start(bf16[2,400,256]{2,1,0:T(8,128)(2,1)} %get-tuple-element.6), channel_id=1, source_target_pairs={{0,12},{4,8},{8,4},{12,0},{16,28},{20,24},{24,20},{28,16},{1,13},{... | collective-permute-start | bytes 1228808 | tf_op jit(solution)/shard_map/ppermute | solution.py:292
  42.7 3.0 %collective-permute-start.6 = (bf16[2,400,256]{2,1,0:T(8,128)(2,1)}, bf16[2,400,256]{2,1,0:T(8,128)(2,1)S(1)}, u32[]{:S(2)}, u32[]{:S(2)}) collective-permute-start(bf16[2,400,256]{2,1,0:T(8,128)(2,1)} %get-tuple-element.7), channel_id=1, source_target_pairs={{0,16},{4,20},{8,24},{12,28},{16,0},{20,4},{24,8},{28,12},{1,17},{... | collective-permute-start | bytes 1228808 | tf_op jit(solution)/shard_map/ppermute | solution.py:292
  45.7 0.1 pad_add_fusion.1.valid_ref
  45.7 0.8 collective-permute-start.2
  46.6 1.5 %all-to-all-done.in_ref = bf16[32,80,128]{2,1,0:T(8,128)(2,1)} async-done(((bf16[32,80,128]{2,1,0:T(8,128)(2,1)}), bf16[32,80,128]{2,1,0:T(8,128)(2,1)}, u32[]{:S(2)}, u32[]{:S(2)}) %all-to-all-start) | async-done | bytes 655392 | tf_op jit(solution)/shard_map/all_to_all | solution.py:296
  48.1 2.3 %join_shares.1 = bf16[64,128]{1,0:T(8,128)(2,1)} custom-call(bf16[32,80,128]{2,1,0:T(8,128)(2,1)} %all-to-all-done.in_ref), custom_call_target="tpu_custom_call" | custom-call | flops 1000000 | bytes 700000 | tf_op jit(solution)/shard_map/join_shares/pallas_call | solution.py:137
  50.4 1.6 %broadcast_in_dim.20 = bf16[32,64,128]{2,1,0:T(8,128)(2,1)} broadcast(bf16[64,128]{1,0:T(8,128)(2,1)} %join_shares.1), dimensions={1,2} | broadcast | bytes 540672 | tf_op jit(solution)/shard_map/broadcast_in_dim | solution.py:298
  52.0 13.2 %all-to-all-start.1 = ((bf16[32,64,128]{2,1,0:T(8,128)(2,1)}), bf16[32,64,128]{2,1,0:T(8,128)(2,1)}, u32[]{:S(2)}, u32[]{:S(2)}) async-start(bf16[32,64,128]{2,1,0:T(8,128)(2,1)} %broadcast_in_dim.20), calls=%async_computation.1 | async-start | bytes 1048576 | tf_op jit(solution)/shard_map/all_to_all | solution.py:298
  65.2 0.0 collective-permute-done.8.refs_1_
  65.2 4.0 %collective-permute-start.3 = (bf16[2,400,256]{2,1,0:T(8,128)(2,1)}, bf16[2,400,256]{2,1,0:T(8,128)(2,1)}, u32[]{:S(2)}, u32[]{:S(2)}) collective-permute-start(bf16[2,400,256]{2,1,0:T(8,128)(2,1)} %get-tuple-element.7), channel_id=1, source_target_pairs={{0,24},{4,28},{8,16},{12,20},{16,8},{20,12},{24,0},{28,4},{1,25},{... | collective-permute-start | bytes 1228808 | tf_op jit(solution)/shard_map/ppermute | solution.py:292
  69.2 16.3 %collective-permute-done.7.refs_0_ = bf16[2,400,256]{2,1,0:T(8,128)(2,1)S(1)} collective-permute-done((bf16[2,400,256]{2,1,0:T(8,128)(2,1)}, bf16[2,400,256]{2,1,0:T(8,128)(2,1)S(1)}, u32[]{:S(2)}, u32[]{:S(2)}) %collective-permute-start.7) | collective-permute-done | bytes 409632 | tf_op jit(solution)/shard_map/ppermute | solution.py:292
  85.5 2.9 %collective-permute-start.4 = (bf16[2,400,256]{2,1,0:T(8,128)(2,1)}, bf16[2,400,256]{2,1,0:T(8,128)(2,1)}, u32[]{:S(2)}, u32[]{:S(2)}) collective-permute-start(bf16[2,400,256]{2,1,0:T(8,128)(2,1)} %get-tuple-element.7), channel_id=1, source_target_pairs={{0,28},{4,24},{8,20},{12,16},{16,12},{20,8},{24,4},{28,0},{1,29},{... | collective-permute-start | bytes 1228808 | tf_op jit(solution)/shard_map/ppermute | solution.py:292
  88.4 0.1 add_convert_fusion.3.valid_ref
  88.5 0.1 tile.10
  88.6 0.0 copy-done.2
  88.6 10.4 %prefill_own.1.refs_2_ = f32[4,144,768]{2,1,0:T(8,128)S(1)} custom-call(s32[3]{0:T(128)S(1)} %add_convert_fusion.3.valid_ref, s32[8,768]{1,0:T(8,128)S(1)} %pad.16.info_ref, bf16[192,2048]{1,0:T(8,128)(2,1)S(1)} %copy-done.2, bf16[1,400,256]{2,1,0:T(8,128)(2,1)S(1)} %fusion.2.refs_0_, bf16[1,400,256]{2,1,0:T(8,128)(2,1)S(1)} %collective-permute-done.refs_1_, ...), custom_call_target="tpu_custom_call" | custom-call | flops 905969664 | bytes 4614400 | tf_op jit(solution)/shard_map/prefill_own/pallas_call | solution.py:248
  98.9 13.5 %prefill_0.1.refs_2_ = f32[4,144,768]{2,1,0:T(8,128)S(1)} custom-call(s32[4]{0:T(128)S(1)} %get-tuple-element.10.valid_ref, s32[8,768]{1,0:T(8,128)S(1)} %pad.16.info_ref, bf16[192,2048]{1,0:T(8,128)(2,1)S(1)} %copy-done.2, bf16[2,400,256]{2,1,0:T(8,128)(2,1)S(1)} %collective-permute-done.7.refs_0_, bf16[2,400,256]{2,1,0:T(8,128)(2,1)S(1)} %collective-permute-done.8.refs_1_, ...), custom_call_target="tpu_custom_call" | custom-call | flops 1207959552 | bytes 4819200 | tf_op jit(solution)/shard_map/prefill_0/pallas_call | solution.py:248
  112.4 0.0 collective-permute-done.6.refs_1_
  112.4 0.0 collective-permute-done.5.refs_0_
  112.4 13.5 %prefill_1.1.refs_3_ = f32[4,144,768]{2,1,0:T(8,128)S(1)} custom-call(s32[4]{0:T(128)S(1)} %get-tuple-element.11.valid_ref, s32[8,768]{1,0:T(8,128)S(1)} %pad.16.info_ref, bf16[192,2048]{1,0:T(8,128)(2,1)S(1)} %copy-done.2, bf16[2,400,256]{2,1,0:T(8,128)(2,1)S(1)} %collective-permute-done.5.refs_0_, bf16[2,400,256]{2,1,0:T(8,128)(2,1)S(1)} %collective-permute-done.6.refs_1_, ...), custom_call_target="tpu_custom_call" | custom-call | flops 1207959552 | bytes 4819200 | tf_op jit(solution)/shard_map/prefill_1/pallas_call | solution.py:248
  125.9 0.0 collective-permute-done.2.refs_0_
  125.9 0.0 collective-permute-done.3.refs_1_
  125.9 0.0 collective-permute-done.4.refs_2_
  125.9 22.0 %prefill_2.1 = bf16[192,2048]{1,0:T(8,128)(2,1)} custom-call(s32[6]{0:T(128)S(1)} %pad_add_fusion.1.valid_ref, s32[8,768]{1,0:T(8,128)S(1)} %pad.16.info_ref, bf16[192,2048]{1,0:T(8,128)(2,1)S(1)} %copy-done.2, bf16[2,400,256]{2,1,0:T(8,128)(2,1)} %collective-permute-done.2.refs_0_, bf16[2,400,256]{2,1,0:T(8,128)(2,1)} %collective-permute-done.3.refs_1_, ...), custom_call_target="tpu_custom_call" | custom-call | flops 1811939328 | bytes 5228800 | tf_op jit(solution)/shard_map/prefill_2/pallas_call | solution.py:248
  148.0 0.0 all-to-all-done.1
  148.0 1.1 copy.18
  149.1 1.0 reshape.29
  (13 shorter events, 0.1 us)
Async XLA Ops:
  0.6 4.6 %copy-start = (bf16[4,2,32,256]{3,2,1,0:T(8,128)(2,1)S(1)}, bf16[4,2,32,256]{3,2,1,0:T(8,128)(2,1)}, u32[]{:S(2)}) copy-start(bf16[4,2,32,256]{3,2,1,0:T(8,128)(2,1)} %param.11) | copy-start | bytes 393220
  0.6 5.9 %copy-start.3 = (s32[32]{0:T(128)S(1)}, s32[32]{0:T(128)}, u32[]{:S(2)}) copy-start(s32[32]{0:T(128)} %len_ref.1) | copy-start | bytes 388
  2.6 34.4 %collective-permute-start.1 = (bf16[1,400,256]{2,1,0:T(8,128)(2,1)S(1)}, bf16[1,400,256]{2,1,0:T(8,128)(2,1)S(1)}, u32[]{:S(2)}, u32[]{:S(2)}) collective-permute-start(bf16[1,400,256]{2,1,0:T(8,128)(2,1)S(1)} %fusion.2.refs_0_), channel_id=1, source_target_pairs={{0,64},{32,96},{1,65},{33,97},{2,66},{34,98},{3,67},{35,99},{4,68}... | collective-permute-start | bytes 614408 | tf_op jit(solution)/shard_map/ppermute | solution.py:278
  3.9 33.3 %collective-permute-start = (bf16[1,400,256]{2,1,0:T(8,128)(2,1)S(1)}, bf16[1,400,256]{2,1,0:T(8,128)(2,1)S(1)}, u32[]{:S(2)}, u32[]{:S(2)}) collective-permute-start(bf16[1,400,256]{2,1,0:T(8,128)(2,1)S(1)} %fusion.2.refs_0_), channel_id=1, source_target_pairs={{0,32},{32,64},{64,96},{1,33},{33,65},{65,97},{2,34},{34,66},{66,9... | collective-permute-start | bytes 614408 | tf_op jit(solution)/shard_map/ppermute | solution.py:277
  6.6 2.2 %copy-start.1 = (bf16[2,32,128,256]{3,2,1,0:T(8,128)(2,1)S(1)}, bf16[2,32,128,256]{3,2,1,0:T(8,128)(2,1)}, u32[]{:S(2)}) copy-start(bf16[2,32,128,256]{3,2,1,0:T(8,128)(2,1)} %kv_ref.1) | copy-start | bytes 12582916
  24.9 23.2 %all-to-all-start = ((bf16[32,80,128]{2,1,0:T(8,128)(2,1)}), bf16[32,80,128]{2,1,0:T(8,128)(2,1)}, u32[]{:S(2)}, u32[]{:S(2)}) async-start(bf16[32,80,128]{2,1,0:T(8,128)(2,1)} %decode_partials.1), calls=%async_computation | async-start | bytes 1310720 | tf_op jit(solution)/shard_map/all_to_all | solution.py:296
  36.9 3.0 %copy-start.4 = (s32[192]{0:T(256)S(1)}, s32[192]{0:T(256)}, u32[]{:S(2)}) copy-start(s32[192]{0:T(256)} %param.9) | copy-start | bytes 2308
  37.2 51.4 %copy-start.2 = (bf16[192,2048]{1,0:T(8,128)(2,1)S(1)}, bf16[192,2048]{1,0:T(8,128)(2,1)}, u32[]{:S(2)}) copy-start(bf16[192,2048]{1,0:T(8,128)(2,1)} %q_ref.7) | copy-start | bytes 2359300
  38.3 26.9 %collective-permute-start.8 = (bf16[2,400,256]{2,1,0:T(8,128)(2,1)}, bf16[2,400,256]{2,1,0:T(8,128)(2,1)S(1)}, u32[]{:S(2)}, u32[]{:S(2)}) collective-permute-start(bf16[2,400,256]{2,1,0:T(8,128)(2,1)} %get-tuple-element.6), channel_id=1, source_target_pairs={{0,8},{4,12},{8,0},{12,4},{16,24},{20,28},{24,16},{28,20},{1,9},{5... | collective-permute-start | bytes 1228808 | tf_op jit(solution)/shard_map/ppermute | solution.py:292
  39.8 45.7 %collective-permute-start.7 = (bf16[2,400,256]{2,1,0:T(8,128)(2,1)}, bf16[2,400,256]{2,1,0:T(8,128)(2,1)S(1)}, u32[]{:S(2)}, u32[]{:S(2)}) collective-permute-start(bf16[2,400,256]{2,1,0:T(8,128)(2,1)} %get-tuple-element.5), channel_id=1, source_target_pairs={{0,4},{4,0},{8,12},{12,8},{16,20},{20,16},{24,28},{28,24},{1,5},{5... | collective-permute-start | bytes 1228808 | tf_op jit(solution)/shard_map/ppermute | solution.py:292
  39.9 72.5 %collective-permute-start.5 = (bf16[2,400,256]{2,1,0:T(8,128)(2,1)}, bf16[2,400,256]{2,1,0:T(8,128)(2,1)S(1)}, u32[]{:S(2)}, u32[]{:S(2)}) collective-permute-start(bf16[2,400,256]{2,1,0:T(8,128)(2,1)} %get-tuple-element.6), channel_id=1, source_target_pairs={{0,12},{4,8},{8,4},{12,0},{16,28},{20,24},{24,20},{28,16},{1,13},{... | collective-permute-start | bytes 1228808 | tf_op jit(solution)/shard_map/ppermute | solution.py:292
  42.7 69.8 %collective-permute-start.6 = (bf16[2,400,256]{2,1,0:T(8,128)(2,1)}, bf16[2,400,256]{2,1,0:T(8,128)(2,1)S(1)}, u32[]{:S(2)}, u32[]{:S(2)}) collective-permute-start(bf16[2,400,256]{2,1,0:T(8,128)(2,1)} %get-tuple-element.7), channel_id=1, source_target_pairs={{0,16},{4,20},{8,24},{12,28},{16,0},{20,4},{24,8},{28,12},{1,17},{... | collective-permute-start | bytes 1228808 | tf_op jit(solution)/shard_map/ppermute | solution.py:292
  45.7 80.2 %collective-permute-start.2 = (bf16[2,400,256]{2,1,0:T(8,128)(2,1)}, bf16[2,400,256]{2,1,0:T(8,128)(2,1)}, u32[]{:S(2)}, u32[]{:S(2)}) collective-permute-start(bf16[2,400,256]{2,1,0:T(8,128)(2,1)} %get-tuple-element.7), channel_id=1, source_target_pairs={{0,20},{4,16},{8,28},{12,24},{16,4},{20,0},{24,12},{28,8},{1,21},{... | collective-permute-start | bytes 1228808 | tf_op jit(solution)/shard_map/ppermute | solution.py:292
  52.0 95.9 %all-to-all-start.1 = ((bf16[32,64,128]{2,1,0:T(8,128)(2,1)}), bf16[32,64,128]{2,1,0:T(8,128)(2,1)}, u32[]{:S(2)}, u32[]{:S(2)}) async-start(bf16[32,64,128]{2,1,0:T(8,128)(2,1)} %broadcast_in_dim.20), calls=%async_computation.1 | async-start | bytes 1048576 | tf_op jit(solution)/shard_map/all_to_all | solution.py:298
  65.2 60.7 %collective-permute-start.3 = (bf16[2,400,256]{2,1,0:T(8,128)(2,1)}, bf16[2,400,256]{2,1,0:T(8,128)(2,1)}, u32[]{:S(2)}, u32[]{:S(2)}) collective-permute-start(bf16[2,400,256]{2,1,0:T(8,128)(2,1)} %get-tuple-element.7), channel_id=1, source_target_pairs={{0,24},{4,28},{8,16},{12,20},{16,8},{20,12},{24,0},{28,4},{1,25},{... | collective-permute-start | bytes 1228808 | tf_op jit(solution)/shard_map/ppermute | solution.py:292
  85.5 40.5 %collective-permute-start.4 = (bf16[2,400,256]{2,1,0:T(8,128)(2,1)}, bf16[2,400,256]{2,1,0:T(8,128)(2,1)}, u32[]{:S(2)}, u32[]{:S(2)}) collective-permute-start(bf16[2,400,256]{2,1,0:T(8,128)(2,1)} %get-tuple-element.7), channel_id=1, source_target_pairs={{0,28},{4,24},{8,20},{12,16},{16,12},{20,8},{24,4},{28,0},{1,29},{... | collective-permute-start | bytes 1228808 | tf_op jit(solution)/shard_map/ppermute | solution.py:292

commit v2 on v1

v2 whole, which is shorter than its diff:
```python
import functools

import jax
import jax.numpy as jnp
from jax import lax
from jax.experimental import pallas as pl
from jax.experimental.pallas import tpu as pltpu
from jax.sharding import Mesh
from jax.sharding import PartitionSpec as P

HEAD_DIM = 128
GROUP = 8
STEPS = 4
SEQS = 32
SLOTS = 128
ROWS = 192
KV_HEADS = 2
HEADS = KV_HEADS * GROUP
PER_KV = STEPS * GROUP
PER_SEQ = STEPS * HEADS
PACKED = PER_SEQ + 16
FUSED = 4
LANES = FUSED * ROWS
STATE = HEAD_DIM + 16
HIDDEN = -1e30
FLOOR = -1e20
NOWHERE = -1000000
TO_LOG2 = HEAD_DIM**-0.5 * 1.4426950408889634
CTX = ("y", "xh", "z")
PLANE = ("xh", "z")

NT = (((1,), (1,)), ((), ()))
TN = (((0,), (0,)), ((), ()))
NN = (((1,), (0,)), ((), ()))


def dot(a, b, dims):
    return lax.dot_general(a, b, dims, preferred_element_type=jnp.float32)


def halves(value):
    high = value.astype(jnp.bfloat16).astype(jnp.float32)
    return high, (value - high).astype(jnp.bfloat16).astype(jnp.float32)


def decode_kernel(len_ref, me_ref, q_ref, kv_ref, step_ref, doc_ref, out_ref, *, per_step):
    base = pl.program_id(0) * per_step
    me = me_ref[0]
    lane = lax.broadcasted_iota(jnp.int32, (PER_SEQ, SLOTS), 1)
    tile_row = lax.broadcasted_iota(jnp.int32, (16, HEAD_DIM), 0)
    tile_lane = lax.broadcasted_iota(jnp.int32, (16, HEAD_DIM), 1)
    pick = ((tile_row == tile_lane) & (tile_row < 4)).astype(jnp.bfloat16)

    doc = doc_ref[...]
    counts = jnp.zeros((16, HEAD_DIM), jnp.float32)
    for d in range(1, 4):
        below = jnp.sum((doc < d).astype(jnp.float32), axis=1, keepdims=True)
        counts = jnp.where((tile_row == 4) & (tile_lane == d - 1), below, counts)

    def pack_stats(m_hi, m_lo, total):
        l_hi, l_lo = halves(total)
        at = lax.broadcasted_iota(jnp.int32, (total.shape[0], HEAD_DIM), 1)
        st = jnp.where(at == 0, m_hi, jnp.where(at == 1, m_lo, jnp.where(at == 2, l_hi, l_lo)))
        return dot(pick, st.astype(jnp.bfloat16), NT)

    def scores(i):
        return jnp.concatenate(
            [
                dot(
                    q_ref[i, h * PER_KV : (h + 1) * PER_KV, :],
                    kv_ref[0, i, :, h * HEAD_DIM : (h + 1) * HEAD_DIM],
                    NT,
                )
                for h in range(KV_HEADS)
            ],
            axis=0,
        )

    s = jnp.concatenate(
        [jnp.where(lane < len_ref[base + i] - me * SLOTS, scores(i) * TO_LOG2, HIDDEN) for i in range(per_step)],
        axis=0,
    )
    m_hi, m_lo = halves(jnp.maximum(jnp.max(s, axis=1, keepdims=True), FLOOR))
    p = jnp.exp2(s - (m_hi + m_lo))
    tile = pack_stats(m_hi, m_lo, jnp.sum(p, axis=1, keepdims=True))
    p = p.astype(jnp.bfloat16)
    for i in range(per_step):
        for h in range(KV_HEADS):
            r = i * PER_SEQ + h * PER_KV
            o = dot(p[r : r + PER_KV], kv_ref[1, i, :, h * HEAD_DIM : (h + 1) * HEAD_DIM], NN)
            out_ref[i, h * PER_KV : (h + 1) * PER_KV, :] = o.astype(jnp.bfloat16)
    for i in range(0, per_step, 2):
        pair = tile[:, i * PER_SEQ : (i + 2) * PER_SEQ]
        out_ref[i, PER_SEQ:, :] = (pair + counts).astype(jnp.bfloat16)
        swapped = jnp.concatenate([pair[:, PER_SEQ:], pair[:, :PER_SEQ]], axis=1)
        out_ref[i + 1, PER_SEQ:, :] = (swapped + counts).astype(jnp.bfloat16)

    for i in range(per_step):

        @pl.when(base + i == me)
        def _():
            row = lax.broadcasted_iota(jnp.int32, (16, KV_HEADS * HEAD_DIM), 0) == lax.rem(me, 16)

            def fresh(kind):
                rows = [
                    jnp.sum(jnp.where(row, step_ref[t, kind].astype(jnp.float32), 0.0), axis=0, keepdims=True)
                    for t in range(STEPS)
                ]
                rows.append(jnp.zeros((16 - STEPS, KV_HEADS * HEAD_DIM), jnp.float32))
                return jnp.concatenate(rows, axis=0).astype(jnp.bfloat16)

            keys, values = fresh(0), fresh(1)
            t = lax.rem(lax.broadcasted_iota(jnp.int32, (PER_SEQ, 16), 0), PER_KV) // GROUP
            sees = lax.broadcasted_iota(jnp.int32, (PER_SEQ, 16), 1) <= t
            s = jnp.where(lane < len_ref[me] - me * SLOTS, scores(i) * TO_LOG2, HIDDEN)
            f = jnp.concatenate(
                [
                    dot(q_ref[i, h * PER_KV : (h + 1) * PER_KV, :], keys[:, h * HEAD_DIM : (h + 1) * HEAD_DIM], NT)
                    for h in range(KV_HEADS)
                ],
                axis=0,
            )
            f = jnp.where(sees, f * TO_LOG2, HIDDEN)
            m_hi, m_lo = halves(
                jnp.maximum(jnp.max(s, axis=1, keepdims=True), jnp.max(f, axis=1, keepdims=True))
            )
            p = jnp.exp2(s - (m_hi + m_lo))
            pf = jnp.exp2(f - (m_hi + m_lo))
            total = jnp.sum(p, axis=1, keepdims=True) + jnp.sum(pf, axis=1, keepdims=True)
            stats = [jnp.broadcast_to(x, (PER_SEQ, 1)) for x in (m_hi, m_lo, total)]
            stats = [jnp.concatenate([x, jnp.zeros_like(x)], axis=0) for x in stats]
            out_ref[i, PER_SEQ:, :] = (pack_stats(*stats) + counts).astype(jnp.bfloat16)
            p, pf = p.astype(jnp.bfloat16), pf.astype(jnp.bfloat16)
            for h in range(KV_HEADS):
                on, at = slice(h * PER_KV, (h + 1) * PER_KV), slice(h * HEAD_DIM, (h + 1) * HEAD_DIM)
                o = dot(p[on], kv_ref[1, i, :, at], NN) + dot(pf[on], values[:, at], NN)
                out_ref[i, on, :] = o.astype(jnp.bfloat16)


def decode_partials(lens, me, queries, cache, fresh, doc):
    per_step = 16
    return pl.pallas_call(
        functools.partial(decode_kernel, per_step=per_step),
        grid_spec=pltpu.PrefetchScalarGridSpec(
            num_scalar_prefetch=2,
            grid=(SEQS // per_step,),
            in_specs=[
                pl.BlockSpec((per_step, PER_SEQ, HEAD_DIM), lambda i, *_: (i, 0, 0)),
                pl.BlockSpec((2, per_step, SLOTS, KV_HEADS * HEAD_DIM), lambda i, *_: (0, i, 0, 0)),
                pl.BlockSpec((STEPS, 2, 16, KV_HEADS * HEAD_DIM), lambda i, lens, me: (0, 0, me[0] // 16, 0)),
                pl.BlockSpec((1, ROWS), lambda i, *_: (0, 0)),
            ],
            out_specs=pl.BlockSpec((per_step, PACKED, HEAD_DIM), lambda i, *_: (i, 0, 0)),
        ),
        out_shape=jax.ShapeDtypeStruct((SEQS, PACKED, HEAD_DIM), jnp.bfloat16),
        compiler_params=pltpu.CompilerParams(vmem_limit_bytes=56 * 1024 * 1024),
        cost_estimate=pl.CostEstimate(flops=70_000_000, bytes_accessed=5_500_000, transcendentals=262144),
        name="decode_partials",
    )(lens, me, queries, cache, fresh, doc)


def join_kernel(in_ref, out_ref, starts_ref, coef):
    peaks, totals, starts = [], [], jnp.zeros((1, HEAD_DIM), jnp.float32)
    for i in range(SEQS):
        st = in_ref[i, PER_SEQ:, :].astype(jnp.float32)
        peaks.append(st[0:1] + st[1:2])
        totals.append(st[2:3] + st[3:4])
        starts = starts + st[4:5]
    starts_ref[...] = jnp.broadcast_to(starts, (8, HEAD_DIM))
    top = functools.reduce(jnp.maximum, peaks)
    scales = [jnp.exp2(m - top) for m in peaks]
    total = functools.reduce(jnp.add, [a * b for a, b in zip(scales, totals)])
    coef[...] = jnp.zeros_like(coef)
    for i in range(SEQS):
        coef[i : i + 1, :] = scales[i] / total
    columns = jnp.transpose(coef[...])
    acc = jnp.zeros((PER_SEQ, HEAD_DIM), jnp.float32)
    for i in range(SEQS):
        acc = acc + in_ref[i, :PER_SEQ, :].astype(jnp.float32) * columns[:PER_SEQ, i : i + 1]
    acc = acc.astype(jnp.bfloat16)
    for i in range(SEQS):
        out_ref[i] = acc


def join_shares(shares):
    return pl.pallas_call(
        join_kernel,
        out_shape=(
            jax.ShapeDtypeStruct((SEQS, PER_SEQ, HEAD_DIM), jnp.bfloat16),
            jax.ShapeDtypeStruct((8, HEAD_DIM), jnp.float32),
        ),
        in_specs=[pl.BlockSpec(memory_space=pltpu.VMEM)],
        out_specs=(pl.BlockSpec(memory_space=pltpu.VMEM), pl.BlockSpec(memory_space=pltpu.VMEM)),
        scratch_shapes=[pltpu.VMEM((HEAD_DIM, HEAD_DIM), jnp.float32)],
        cost_estimate=pl.CostEstimate(flops=1_000_000, bytes_accessed=1_200_000, transcendentals=4096),
        name="join_shares",
    )(shares)


def prefill_kernel(base_ref, info_ref, starts_ref, q_ref, *refs, counts, first, last):
    blocks, rest = refs[: len(counts)], refs[len(counts) :]
    state_in = None
    if not first:
        state_in, rest = rest[0], rest[1:]
    out_ref, keys_ref, values_ref, since_ref, flag_ref = rest
    step = pl.program_id(0)
    places = [(r, b) for r, n in enumerate(counts) for b in range(n)]
    n = len(places)

    @pl.when(step == 0)
    def _():
        doc, starts = info_ref[0:1, :], starts_ref[0:1, :].astype(jnp.int32)
        since = jnp.where(
            doc == 1, starts[:, 0:1], jnp.where(doc == 2, starts[:, 1:2], jnp.where(doc == 3, starts[:, 2:3], 0))
        )
        since_ref[0:1, :] = since
        lowest, highest = jnp.min(since), jnp.max(since)
        some, whole = lowest - base_ref[0] < ROWS, highest <= base_ref[0]
        for at in range(1, n):
            some = some | (lowest - base_ref[at] < ROWS)
            whole = whole & (highest <= base_ref[at])
        flag_ref[0] = jnp.where(some, jnp.where(whole, 1, 2), 0)

    @pl.when(lax.rem(step, HEADS // FUSED // KV_HEADS) == 0)
    def _():
        for at, (r, b) in enumerate(places):
            on = slice(at * ROWS, (at + 1) * ROWS)
            keys_ref[on, :] = blocks[r][0, b]
            values_ref[on, :] = blocks[r][1, b]

    def attend(masked):
        queries = jnp.concatenate([q_ref[:, j * HEAD_DIM : (j + 1) * HEAD_DIM] for j in range(FUSED)], axis=0)
        s = dot(keys_ref[...], queries, NT)
        if masked:
            row = lax.broadcasted_iota(jnp.int32, (ROWS, LANES), 0)
            parts = []
            for at in range(n):
                sees = row >= since_ref[0:1, :] - base_ref[at]
                if first and at == 0:
                    sees = sees & (row <= info_ref[1:2, :])
                parts.append(jnp.where(sees, s[at * ROWS : (at + 1) * ROWS], HIDDEN))
            s = jnp.concatenate(parts, axis=0)
        peak = jnp.max(s, axis=0, keepdims=True)
        if first:
            peak = jnp.maximum(peak, FLOOR)
        else:
            old = state_in[0, HEAD_DIM : HEAD_DIM + 1, :]
            peak = jnp.maximum(old, peak)
            factor = jnp.exp2((old - peak) * TO_LOG2)
        p = jnp.exp2((s - peak) * TO_LOG2)
        total = jnp.sum(p, axis=0, keepdims=True)
        summed = dot(values_ref[...], p.astype(jnp.bfloat16), TN)
        if not first:
            total = total + state_in[0, HEAD_DIM + 8 : HEAD_DIM + 9, :] * factor
            summed = summed + state_in[0, 0:HEAD_DIM, :] * factor
        finish(peak, total, summed)

    def finish(peak, total, summed):
        if last:
            out = jnp.transpose(summed / total).astype(jnp.bfloat16)
            for j in range(FUSED):
                out_ref[:, j * HEAD_DIM : (j + 1) * HEAD_DIM] = out[j * ROWS : (j + 1) * ROWS]
        else:
            out_ref[0, 0:HEAD_DIM, :] = summed
            out_ref[0, HEAD_DIM : HEAD_DIM + 8, :] = jnp.broadcast_to(peak, (8, LANES))
            out_ref[0, HEAD_DIM + 8 :, :] = jnp.broadcast_to(total, (8, LANES))

    if first:
        attend(True)
        return

    @pl.when(flag_ref[0] == 0)
    def _():
        finish(
            state_in[0, HEAD_DIM : HEAD_DIM + 1, :],
            state_in[0, HEAD_DIM + 8 : HEAD_DIM + 9, :],
            state_in[0, 0:HEAD_DIM, :],
        )

    @pl.when(flag_ref[0] == 1)
    def _():
        attend(False)

    @pl.when(flag_ref[0] == 2)
    def _():
        attend(True)


def prefill_part(bases, info, starts, queries, blocks, state, last, name):
    first = state is None
    counts = [b.shape[1] for b in blocks]
    n = sum(counts)
    steps = HEADS // FUSED
    per_kv = steps // KV_HEADS
    q_spec = pl.BlockSpec((ROWS, FUSED * HEAD_DIM), lambda i, *_: (0, i))
    state_spec = pl.BlockSpec((1, STATE, LANES), lambda i, *_: (i, 0, 0))
    in_specs = [
        pl.BlockSpec((8, LANES), lambda i, *_: (0, 0)),
        pl.BlockSpec((8, HEAD_DIM), lambda i, *_: (0, 0)),
        q_spec,
    ]
    in_specs += [pl.BlockSpec((2, c, ROWS, HEAD_DIM), lambda i, *_: (0, 0, 0, i // per_kv)) for c in counts]
    operands = [bases, info, starts, queries, *blocks]
    if not first:
        in_specs.append(state_spec)
        operands.append(state)
    if last:
        out_shape = jax.ShapeDtypeStruct((ROWS, HEADS * HEAD_DIM), jnp.bfloat16)
        out_spec = q_spec
    else:
        out_shape = jax.ShapeDtypeStruct((steps, STATE, LANES), jnp.float32)
        out_spec = state_spec
    return pl.pallas_call(
        functools.partial(prefill_kernel, counts=counts, first=first, last=last),
        grid_spec=pltpu.PrefetchScalarGridSpec(
            num_scalar_prefetch=1,
            grid=(steps,),
            in_specs=in_specs,
            out_specs=out_spec,
            scratch_shapes=[
                pltpu.VMEM((n * ROWS, HEAD_DIM), jnp.bfloat16),
                pltpu.VMEM((n * ROWS, HEAD_DIM), jnp.bfloat16),
                pltpu.VMEM((8, LANES), jnp.int32),
                pltpu.SMEM((1,), jnp.int32),
            ],
        ),
        out_shape=out_shape,
        compiler_params=pltpu.CompilerParams(vmem_limit_bytes=48 * 1024 * 1024),
        cost_estimate=pl.CostEstimate(
            flops=4 * n * ROWS * ROWS * HEADS * HEAD_DIM,
            bytes_accessed=n * ROWS * 1024 + 4_000_000,
            transcendentals=n * ROWS * ROWS * HEADS,
        ),
        name=name,
    )(*operands)


ORDER = (4, 1, 3, 5, 2, 6, 7)
CALLS = ((0, 2), (2, 4), (4, 7))


def local(prefill_queries, prefill_key_values, fill_doc, decode_queries, step_key_values, stored_key_values, cached_len):
    y = lax.axis_index("y").astype(jnp.int32)
    place = lax.axis_index(PLANE).astype(jnp.int32)
    me = y * 8 + place

    own = prefill_key_values[:, None]
    back1 = lax.ppermute(own, "y", [(i, i + 1) for i in range(3)])
    back2 = lax.ppermute(own, "y", [(i, i + 2) for i in range(2)])

    queries = decode_queries.reshape(STEPS, SEQS, KV_HEADS, GROUP, HEAD_DIM)
    queries = queries.transpose(1, 2, 0, 3, 4).reshape(SEQS, PER_SEQ, HEAD_DIM)
    shares = decode_partials(cached_len, me[None], queries, stored_key_values, step_key_values, fill_doc[None])

    packs = {}
    for bit in (1, 2, 4):
        other = jnp.where((place & bit) == 0, own, back2)
        packs[bit] = jnp.concatenate([back1, other], axis=1)
    shares, packs = lax.optimization_barrier((shares, packs))
    got, bases = [], []
    for k in ORDER:
        bit = 1 << (k.bit_length() - 1)
        got.append(lax.ppermute(packs[bit], PLANE, [(i, i ^ k) for i in range(8)]))
        from_row = jnp.where((place & bit) != 0, y, y - 2)
        for row in (y - 1, from_row):
            bases.append(jnp.where(row >= 0, (row * 8 + (place ^ k)) * ROWS, NOWHERE))
    bases = jnp.stack(bases)

    shares = lax.all_to_all(shares, CTX, 0, 0)
    spread, starts = join_shares(shares)
    spread = lax.all_to_all(spread, CTX, 0, 0)
    step_out = spread.reshape(SEQS, KV_HEADS, STEPS, GROUP, HEAD_DIM).transpose(2, 0, 1, 3, 4)
    step_out = step_out.reshape(STEPS, SEQS, HEADS * HEAD_DIM)

    info = jnp.stack([fill_doc, jnp.arange(ROWS, dtype=jnp.int32)])
    info = jnp.pad(jnp.tile(info, (1, FUSED)), ((0, 6), (0, 0)))
    rows = [jnp.where(y >= d, (me - 8 * d) * ROWS, NOWHERE) for d in range(3)]
    state = None
    for at, (a, b) in enumerate(CALLS):
        blocks, base = got[a:b], bases[2 * a : 2 * b]
        if at == 0:
            blocks, base = [own, back1, back2] + blocks, jnp.concatenate([jnp.stack(rows), base])
        state = prefill_part(base, info, starts, prefill_queries, blocks, state, b == 7, "prefill_%d" % at)
    return state, step_out


def solution(mesh):
    fine = Mesh(mesh.devices.reshape(4, 2, 4, 2, 2), ("y", "xh", "z", "xl", "c"))
    tp = ("xl", "c")
    placed = (
        P(CTX, tp),
        P(None, CTX, tp),
        P(CTX),
        P(None, None, tp),
        P(None, None, None, tp),
        P(None, None, CTX, tp),
        P(),
    )
    return jax.shard_map(
        local,
        mesh=fine,
        in_specs=placed,
        out_specs=(P(CTX, tp), P(None, None, tp)),
        check_vma=False,
    )
```

time: 148 us -> 98.7 us (0.67)
  the two profiles are of different devices: /device:TPU:120 before, /device:TPU:4 now
where the time goes in v2:
time: 98.7 us; the launch traced here: 98.1 us
  starting transfers between devices  36.2 us (37%)
  Pallas kernels  34.8 us (35%)
  waiting for transfers between devices  19.9 us (20%)
  local copies, waits for them, and re-layouts  5.21 us (5%)
  other arithmetic  1.22 us (1%)
    pallas_call x3, Pallas kernels, prefill_part(): pl.pallas_call(functools.partial(prefill_kernel, counts=counts, first=fir...  25.9 us
    ppermute x7, waiting for transfers between devices, local(): got.append(lax.ppermute(packs[bit], PLANE, [(i, i ^ k) for i in range(8)]))  16.1 us
    ppermute x7, starting transfers between devices, local(): got.append(lax.ppermute(packs[bit], PLANE, [(i, i ^ k) for i in range(8)]))  11.7 us
    all_to_all x1, starting transfers between devices, local(): shares = lax.all_to_all(shares, CTX, 0, 0)  9.41 us
    all_to_all x1, starting transfers between devices, local(): spread = lax.all_to_all(spread, CTX, 0, 0)  7.36 us
    pallas_call x1, Pallas kernels, decode_partials(): pl.pallas_call(functools.partial(decode_kernel, per_step=per_step), grid_...  6.37 us
    ppermute x1, starting transfers between devices, local(): back2 = lax.ppermute(own, 'y', [(i, i + 2) for i in range(2)])  5.11 us
    all_to_all x1, waiting for transfers between devices, local(): shares = lax.all_to_all(shares, CTX, 0, 0)  3.79 us
  transfers between devices with their start and end apart: 11, of which 3 were waited for; matrix products, arithmetic and copies ran while one was open for 3% of the time, Pallas kernels for 35%

profile of v2, /device:TPU:4, one launch (start us, length us, event | category | flops | bytes accessed | tf_op | source)
XLA Modules:
  0.0 98.1 jit_solution(806321351672622417)
XLA Ops:
  0.6 5.1 %collective-permute-start.1 = (bf16[2,1,192,256]{3,2,1,0:T(8,128)(2,1)}, bf16[2,1,192,256]{3,2,1,0:T(8,128)(2,1)S(1)}, u32[]{:S(2)}, u32[]{:S(2)}) collective-permute-start(bf16[2,1,192,256]{3,2,1,0:T(8,128)(2,1)} %bitcast.35), channel_id=1, source_target_pairs={{0,64},{32,96},{1,65},{33,97},{2,66},{34,98},{3,67},{35,99},{4,68}... | collective-permute-start | bytes 589832 | tf_op jit(solution)/shard_map/ppermute | solution.py:349
  5.7 2.6 %collective-permute-start = (bf16[2,1,192,256]{3,2,1,0:T(8,128)(2,1)}, bf16[2,1,192,256]{3,2,1,0:T(8,128)(2,1)S(1)}, u32[]{:S(2)}, u32[]{:S(2)}) collective-permute-start(bf16[2,1,192,256]{3,2,1,0:T(8,128)(2,1)} %bitcast.36), channel_id=1, source_target_pairs={{0,32},{32,64},{64,96},{1,33},{33,65},{65,97},{2,34},{34,66},{66,9... | collective-permute-start | bytes 589832 | tf_op jit(solution)/shard_map/ppermute | solution.py:348
  8.4 1.1 %copy.11 = bf16[16,8,16,128]{3,2,1,0:T(8,128)(2,1)S(1)} copy(bf16[16,8,16,128]{3,1,2,0:T(8,128)(2,1)} %bitcast.40) | data formatting | bytes 1048576
  9.5 0.9 copy.9
  10.5 0.0 copy-start.1
  10.5 6.4 %decode_partials.1 = bf16[32,80,128]{2,1,0:T(8,128)(2,1)} custom-call(s32[32]{0:T(128)} %len_ref.1, s32[1]{0:T(128)} %bitcast.7.me_ref, bf16[32,64,128]{2,1,0:T(8,128)(2,1)} %bitcast.38, bf16[2,32,128,256]{3,2,1,0:T(8,128)(2,1)} %kv_ref.1, bf16[4,2,32,256]{3,2,1,0:T(8,128)(2,1)} %step_ref.1, s32[1,192]{1,0:T(1,128)} %bitcast.41), custom_call_target="tpu_custom_call" | custom-call | flops 70000000 | bytes 5500000 | tf_op jit(solution)/shard_map/decode_partials/pallas_call | solution.py:142
  16.8 0.0 collective-permute-done.1.refs_2_
  16.8 0.0 copy-done.1
  16.9 0.1 broadcast_select_fusion
  16.9 0.0 copy-start.3
  16.9 0.0 collective-permute-done.refs_1_
  16.9 1.1 %pad_maximum_fusion = (bf16[2,2,192,256]{3,2,1,0:T(8,128)(2,1)}, bf16[2,2,192,256]{3,2,1,0:T(8,128)(2,1)}, bf16[2,2,192,256]{3,2,1,0:T(8,128)(2,1)}) fusion(bf16[2,1,192,256]{3,2,1,0:T(8,128)(2,1)S(1)} %collective-permute-done.refs_1_, bf16[2,1,192,256]{3,2,1,0:T(8,128)(2,1)S(1)} %get-tuple-element.14, bf16[2,1,192,256]{3,2,1,0:T(8,128)(2,1)S(1)} %get-tuple-element.15, ...), kind=kLoop, calls=%fused_computation | loop fusion | flops 589824 | bytes 1966080 | tf_op jit(solution)/shard_map/concatenate | solution.py:358
  18.0 0.0 copy-start
  18.0 9.4 %all-to-all-start = ((bf16[32,80,128]{2,1,0:T(8,128)(2,1)}), bf16[32,80,128]{2,1,0:T(8,128)(2,1)}, u32[]{:S(2)}, u32[]{:S(2)}) async-start(bf16[32,80,128]{2,1,0:T(8,128)(2,1)} %decode_partials.1), calls=%async_computation | async-start | bytes 1310720 | tf_op jit(solution)/shard_map/all_to_all | solution.py:369
  27.4 0.4 collective-permute-start.7
  27.8 1.7 %collective-permute-start.8 = (bf16[2,2,192,256]{3,2,1,0:T(8,128)(2,1)}, bf16[2,2,192,256]{3,2,1,0:T(8,128)(2,1)S(1)}, u32[]{:S(2)}, u32[]{:S(2)}) collective-permute-start(bf16[2,2,192,256]{3,2,1,0:T(8,128)(2,1)} %get-tuple-element.12), channel_id=1, source_target_pairs={{0,4},{4,0},{8,12},{12,8},{16,20},{20,16},{24,28},{28,24},{1,5},{5... | collective-permute-start | bytes 1179656 | tf_op jit(solution)/shard_map/ppermute | solution.py:363
  29.5 3.0 %collective-permute-start.6 = (bf16[2,2,192,256]{3,2,1,0:T(8,128)(2,1)}, bf16[2,2,192,256]{3,2,1,0:T(8,128)(2,1)S(1)}, u32[]{:S(2)}, u32[]{:S(2)}) collective-permute-start(bf16[2,2,192,256]{3,2,1,0:T(8,128)(2,1)} %get-tuple-element.11), channel_id=1, source_target_pairs={{0,20},{4,16},{8,28},{12,24},{16,4},{20,0},{24,12},{28,8},{1,21},{... | collective-permute-start | bytes 1179656 | tf_op jit(solution)/shard_map/ppermute | solution.py:363
  32.5 2.7 %collective-permute-start.5 = (bf16[2,2,192,256]{3,2,1,0:T(8,128)(2,1)}, bf16[2,2,192,256]{3,2,1,0:T(8,128)(2,1)S(1)}, u32[]{:S(2)}, u32[]{:S(2)}) collective-permute-start(bf16[2,2,192,256]{3,2,1,0:T(8,128)(2,1)} %get-tuple-element.10), channel_id=1, source_target_pairs={{0,12},{4,8},{8,4},{12,0},{16,28},{20,24},{24,20},{28,16},{1,13},{... | collective-permute-start | bytes 1179656 | tf_op jit(solution)/shard_map/ppermute | solution.py:363
  35.2 0.0 copy-done.3
  35.2 0.9 collective-permute-start.2
  36.1 3.8 %all-to-all-done.in_ref = bf16[32,80,128]{2,1,0:T(8,128)(2,1)} async-done(((bf16[32,80,128]{2,1,0:T(8,128)(2,1)}), bf16[32,80,128]{2,1,0:T(8,128)(2,1)}, u32[]{:S(2)}, u32[]{:S(2)}) %all-to-all-start) | async-done | bytes 655392 | tf_op jit(solution)/shard_map/all_to_all | solution.py:369
  39.9 2.5 %join_shares.1 = (bf16[32,64,128]{2,1,0:T(8,128)(2,1)}, f32[8,128]{1,0:T(8,128)}) custom-call(bf16[32,80,128]{2,1,0:T(8,128)(2,1)} %all-to-all-done.in_ref), custom_call_target="tpu_custom_call" | custom-call | flops 1000000 | bytes 1200000 | tf_op jit(solution)/shard_map/join_shares/pallas_call | solution.py:186
  42.5 7.4 %all-to-all-start.1 = ((bf16[32,64,128]{2,1,0:T(8,128)(2,1)}), bf16[32,64,128]{2,1,0:T(8,128)(2,1)}, u32[]{:S(2)}, u32[]{:S(2)}) async-start(bf16[32,64,128]{2,1,0:T(8,128)(2,1)} %get-tuple-element.13), calls=%async_computation.1 | async-start | bytes 1048576 | tf_op jit(solution)/shard_map/all_to_all | solution.py:371
  49.8 0.0 collective-permute-done.7.refs_3_
  49.8 3.0 %collective-permute-start.3 = (bf16[2,2,192,256]{3,2,1,0:T(8,128)(2,1)}, bf16[2,2,192,256]{3,2,1,0:T(8,128)(2,1)}, u32[]{:S(2)}, u32[]{:S(2)}) collective-permute-start(bf16[2,2,192,256]{3,2,1,0:T(8,128)(2,1)} %get-tuple-element.11), channel_id=1, source_target_pairs={{0,24},{4,28},{8,16},{12,20},{16,8},{20,12},{24,0},{28,4},{1,25},{... | collective-permute-start | bytes 1179656 | tf_op jit(solution)/shard_map/ppermute | solution.py:363
  52.9 13.7 %collective-permute-done.8.refs_4_ = bf16[2,2,192,256]{3,2,1,0:T(8,128)(2,1)S(1)} collective-permute-done((bf16[2,2,192,256]{3,2,1,0:T(8,128)(2,1)}, bf16[2,2,192,256]{3,2,1,0:T(8,128)(2,1)S(1)}, u32[]{:S(2)}, u32[]{:S(2)}) %collective-permute-start.8) | collective-permute-done | bytes 393248 | tf_op jit(solution)/shard_map/ppermute | solution.py:363
  66.6 0.0 collective-permute-start.4
  66.6 0.1 pad_add_fusion.1.base_ref
  66.7 0.1 tile.10
  66.9 0.1 stack.69.base_ref
  66.9 0.1 concatenate.19.base_ref
  67.0 0.0 copy-done
  67.0 0.0 copy-start.2
  67.0 0.7 copy-done.2
  67.7 8.9 %prefill_0.1.refs_2_ = f32[4,144,768]{2,1,0:T(8,128)S(1)} custom-call(s32[7]{0:T(128)S(1)} %concatenate.19.base_ref, s32[8,768]{1,0:T(8,128)S(1)} %pad.4.info_ref, f32[8,128]{1,0:T(8,128)S(1)} %copy-done.2, bf16[192,2048]{1,0:T(8,128)(2,1)S(1)} %copy-done, bf16[2,1,192,256]{3,2,1,0:T(8,128)(2,1)S(1)} %bitcast.37, ...), custom_call_target="tpu_custom_call" | custom-call | flops 2113929216 | bytes 5376256 | tf_op jit(solution)/shard_map/prefill_0/pallas_call | solution.py:313
  76.6 0.0 collective-permute-done.5.refs_0_
  76.6 0.0 collective-permute-done.6.refs_1_
  76.6 6.9 %prefill_1.1.refs_3_ = f32[4,144,768]{2,1,0:T(8,128)S(1)} custom-call(s32[4]{0:T(128)S(1)} %pad_add_fusion.1.base_ref, s32[8,768]{1,0:T(8,128)S(1)} %pad.4.info_ref, f32[8,128]{1,0:T(8,128)S(1)} %copy-done.2, bf16[192,2048]{1,0:T(8,128)(2,1)S(1)} %copy-done, bf16[2,2,192,256]{3,2,1,0:T(8,128)(2,1)S(1)} %collective-permute-done.5.refs_0_, ...), custom_call_target="tpu_custom_call" | custom-call | flops 1207959552 | bytes 4786432 | tf_op jit(solution)/shard_map/prefill_1/pallas_call | solution.py:313
  83.5 2.3 %collective-permute-done.2.refs_0_ = bf16[2,2,192,256]{3,2,1,0:T(8,128)(2,1)S(1)} collective-permute-done((bf16[2,2,192,256]{3,2,1,0:T(8,128)(2,1)}, bf16[2,2,192,256]{3,2,1,0:T(8,128)(2,1)S(1)}, u32[]{:S(2)}, u32[]{:S(2)}) %collective-permute-start.2) | collective-permute-done | bytes 393248 | tf_op jit(solution)/shard_map/ppermute | solution.py:363
  85.9 0.0 collective-permute-done.3.refs_1_
  85.9 0.0 collective-permute-done.4.refs_2_
  85.9 10.1 %prefill_2.1 = bf16[192,2048]{1,0:T(8,128)(2,1)} custom-call(s32[6]{0:T(128)S(1)} %stack.69.base_ref, s32[8,768]{1,0:T(8,128)S(1)} %pad.4.info_ref, f32[8,128]{1,0:T(8,128)S(1)} %copy-done.2, bf16[192,2048]{1,0:T(8,128)(2,1)S(1)} %copy-done, bf16[2,2,192,256]{3,2,1,0:T(8,128)(2,1)S(1)} %collective-permute-done.2.refs_0_, ...), custom_call_target="tpu_custom_call" | custom-call | flops 1811939328 | bytes 5179648 | tf_op jit(solution)/shard_map/prefill_2/pallas_call | solution.py:313
  96.0 0.0 all-to-all-done.1
  96.0 1.1 %copy.10 = bf16[4,32,2,8,128]{4,3,2,1,0:T(8,128)(2,1)S(1)} copy(bf16[4,32,2,8,128]{4,3,0,2,1:T(8,128)(2,1)} %bitcast.23) | data formatting | bytes 1048576 | tf_op jit(solution)/shard_map/transpose | solution.py:372
  97.1 1.0 %reshape.23 = bf16[4,32,2048]{2,1,0:T(8,128)(2,1)} reshape(bf16[4,32,2,8,128]{4,3,2,1,0:T(8,128)(2,1)S(1)} %copy.10) | data formatting | bytes 1048576 | tf_op jit(solution)/shard_map/reshape | solution.py:373
  (4 shorter events, 0.0 us)
Async XLA Ops:
  0.6 16.2 %collective-permute-start.1 = (bf16[2,1,192,256]{3,2,1,0:T(8,128)(2,1)}, bf16[2,1,192,256]{3,2,1,0:T(8,128)(2,1)S(1)}, u32[]{:S(2)}, u32[]{:S(2)}) collective-permute-start(bf16[2,1,192,256]{3,2,1,0:T(8,128)(2,1)} %bitcast.35), channel_id=1, source_target_pairs={{0,64},{32,96},{1,65},{33,97},{2,66},{34,98},{3,67},{35,99},{4,68}... | collective-permute-start | bytes 589832 | tf_op jit(solution)/shard_map/ppermute | solution.py:349
  5.7 11.2 %collective-permute-start = (bf16[2,1,192,256]{3,2,1,0:T(8,128)(2,1)}, bf16[2,1,192,256]{3,2,1,0:T(8,128)(2,1)S(1)}, u32[]{:S(2)}, u32[]{:S(2)}) collective-permute-start(bf16[2,1,192,256]{3,2,1,0:T(8,128)(2,1)} %bitcast.36), channel_id=1, source_target_pairs={{0,32},{32,64},{64,96},{1,33},{33,65},{65,97},{2,34},{34,66},{66,9... | collective-permute-start | bytes 589832 | tf_op jit(solution)/shard_map/ppermute | solution.py:348
  10.5 6.4 %copy-start.1 = (bf16[2,192,256]{2,1,0:T(8,128)(2,1)S(1)}, bf16[2,192,256]{2,1,0:T(8,128)(2,1)}, u32[]{:S(2)}) copy-start(bf16[2,192,256]{2,1,0:T(8,128)(2,1)} %param.8) | copy-start | bytes 589828
  16.9 18.3 %copy-start.3 = (s32[192]{0:T(256)S(1)}, s32[192]{0:T(256)}, u32[]{:S(2)}) copy-start(s32[192]{0:T(256)} %param.9) | copy-start | bytes 2308
  18.0 49.0 %copy-start = (bf16[192,2048]{1,0:T(8,128)(2,1)S(1)}, bf16[192,2048]{1,0:T(8,128)(2,1)}, u32[]{:S(2)}) copy-start(bf16[192,2048]{1,0:T(8,128)(2,1)} %q_ref.5) | copy-start | bytes 2359300
  18.0 21.9 %all-to-all-start = ((bf16[32,80,128]{2,1,0:T(8,128)(2,1)}), bf16[32,80,128]{2,1,0:T(8,128)(2,1)}, u32[]{:S(2)}, u32[]{:S(2)}) async-start(bf16[32,80,128]{2,1,0:T(8,128)(2,1)} %decode_partials.1), calls=%async_computation | async-start | bytes 1310720 | tf_op jit(solution)/shard_map/all_to_all | solution.py:369
  27.4 22.4 %collective-permute-start.7 = (bf16[2,2,192,256]{3,2,1,0:T(8,128)(2,1)}, bf16[2,2,192,256]{3,2,1,0:T(8,128)(2,1)S(1)}, u32[]{:S(2)}, u32[]{:S(2)}) collective-permute-start(bf16[2,2,192,256]{3,2,1,0:T(8,128)(2,1)} %get-tuple-element.11), channel_id=1, source_target_pairs={{0,16},{4,20},{8,24},{12,28},{16,0},{20,4},{24,8},{28,12},{1,17},{... | collective-permute-start | bytes 1179656 | tf_op jit(solution)/shard_map/ppermute | solution.py:363
  27.8 38.8 %collective-permute-start.8 = (bf16[2,2,192,256]{3,2,1,0:T(8,128)(2,1)}, bf16[2,2,192,256]{3,2,1,0:T(8,128)(2,1)S(1)}, u32[]{:S(2)}, u32[]{:S(2)}) collective-permute-start(bf16[2,2,192,256]{3,2,1,0:T(8,128)(2,1)} %get-tuple-element.12), channel_id=1, source_target_pairs={{0,4},{4,0},{8,12},{12,8},{16,20},{20,16},{24,28},{28,24},{1,5},{5... | collective-permute-start | bytes 1179656 | tf_op jit(solution)/shard_map/ppermute | solution.py:363
  29.5 47.1 %collective-permute-start.6 = (bf16[2,2,192,256]{3,2,1,0:T(8,128)(2,1)}, bf16[2,2,192,256]{3,2,1,0:T(8,128)(2,1)S(1)}, u32[]{:S(2)}, u32[]{:S(2)}) collective-permute-start(bf16[2,2,192,256]{3,2,1,0:T(8,128)(2,1)} %get-tuple-element.11), channel_id=1, source_target_pairs={{0,20},{4,16},{8,28},{12,24},{16,4},{20,0},{24,12},{28,8},{1,21},{... | collective-permute-start | bytes 1179656 | tf_op jit(solution)/shard_map/ppermute | solution.py:363
  32.5 44.1 %collective-permute-start.5 = (bf16[2,2,192,256]{3,2,1,0:T(8,128)(2,1)}, bf16[2,2,192,256]{3,2,1,0:T(8,128)(2,1)S(1)}, u32[]{:S(2)}, u32[]{:S(2)}) collective-permute-start(bf16[2,2,192,256]{3,2,1,0:T(8,128)(2,1)} %get-tuple-element.10), channel_id=1, source_target_pairs={{0,12},{4,8},{8,4},{12,0},{16,28},{20,24},{24,20},{28,16},{1,13},{... | collective-permute-start | bytes 1179656 | tf_op jit(solution)/shard_map/ppermute | solution.py:363
  35.2 50.7 %collective-permute-start.2 = (bf16[2,2,192,256]{3,2,1,0:T(8,128)(2,1)}, bf16[2,2,192,256]{3,2,1,0:T(8,128)(2,1)S(1)}, u32[]{:S(2)}, u32[]{:S(2)}) collective-permute-start(bf16[2,2,192,256]{3,2,1,0:T(8,128)(2,1)} %get-tuple-element.10), channel_id=1, source_target_pairs={{0,8},{4,12},{8,0},{12,4},{16,24},{20,28},{24,16},{28,20},{1,9},{5... | collective-permute-start | bytes 1179656 | tf_op jit(solution)/shard_map/ppermute | solution.py:363
  42.5 53.5 %all-to-all-start.1 = ((bf16[32,64,128]{2,1,0:T(8,128)(2,1)}), bf16[32,64,128]{2,1,0:T(8,128)(2,1)}, u32[]{:S(2)}, u32[]{:S(2)}) async-start(bf16[32,64,128]{2,1,0:T(8,128)(2,1)} %get-tuple-element.13), calls=%async_computation.1 | async-start | bytes 1048576 | tf_op jit(solution)/shard_map/all_to_all | solution.py:371
  49.8 36.0 %collective-permute-start.3 = (bf16[2,2,192,256]{3,2,1,0:T(8,128)(2,1)}, bf16[2,2,192,256]{3,2,1,0:T(8,128)(2,1)}, u32[]{:S(2)}, u32[]{:S(2)}) collective-permute-start(bf16[2,2,192,256]{3,2,1,0:T(8,128)(2,1)} %get-tuple-element.11), channel_id=1, source_target_pairs={{0,24},{4,28},{8,16},{12,20},{16,8},{20,12},{24,0},{28,4},{1,25},{... | collective-permute-start | bytes 1179656 | tf_op jit(solution)/shard_map/ppermute | solution.py:363
  66.6 19.3 %collective-permute-start.4 = (bf16[2,2,192,256]{3,2,1,0:T(8,128)(2,1)}, bf16[2,2,192,256]{3,2,1,0:T(8,128)(2,1)}, u32[]{:S(2)}, u32[]{:S(2)}) collective-permute-start(bf16[2,2,192,256]{3,2,1,0:T(8,128)(2,1)} %get-tuple-element.11), channel_id=1, source_target_pairs={{0,28},{4,24},{8,20},{12,16},{16,12},{20,8},{24,4},{28,0},{1,29},{... | collective-permute-start | bytes 1179656 | tf_op jit(solution)/shard_map/ppermute | solution.py:363
  67.0 0.7 copy-start.2

commit v3 on v2

v3 whole, which is shorter than its diff:
```python
import functools

import jax
import jax.numpy as jnp
from jax import lax
from jax.experimental import pallas as pl
from jax.experimental.pallas import tpu as pltpu
from jax.sharding import Mesh
from jax.sharding import PartitionSpec as P

HEAD_DIM = 128
GROUP = 8
STEPS = 4
SEQS = 32
SLOTS = 128
ROWS = 192
KV_HEADS = 2
HEADS = KV_HEADS * GROUP
PER_KV = STEPS * GROUP
PER_SEQ = STEPS * HEADS
PACKED = PER_SEQ + 16
FUSED = 8
LANES = FUSED * ROWS
BLOCK = 2 * ROWS + 16
STATE = HEAD_DIM + 16
HIDDEN = -1e30
FLOOR = -1e20
NOWHERE = -1000000
TOO_LARGE = 2.0**100
TO_LOG2 = HEAD_DIM**-0.5 * 1.4426950408889634
CTX = ("y", "xh", "z")
PLANE = ("xh", "z")

NT = (((1,), (1,)), ((), ()))
TN = (((0,), (0,)), ((), ()))
NN = (((1,), (0,)), ((), ()))


def dot(a, b, dims):
    return lax.dot_general(a, b, dims, preferred_element_type=jnp.float32)


def halves(value):
    high = value.astype(jnp.bfloat16).astype(jnp.float32)
    return high, (value - high).astype(jnp.bfloat16).astype(jnp.float32)


def decode_kernel(len_ref, me_ref, q_ref, kv_ref, step_ref, out_ref, *, per_step):
    base = pl.program_id(0) * per_step
    me = me_ref[0]
    lane = lax.broadcasted_iota(jnp.int32, (PER_SEQ, SLOTS), 1)
    tile_row = lax.broadcasted_iota(jnp.int32, (16, HEAD_DIM), 0)
    tile_lane = lax.broadcasted_iota(jnp.int32, (16, HEAD_DIM), 1)
    pick = ((tile_row == tile_lane) & (tile_row < 4)).astype(jnp.bfloat16)

    def pack_stats(m_hi, m_lo, total):
        l_hi, l_lo = halves(total)
        at = lax.broadcasted_iota(jnp.int32, (total.shape[0], HEAD_DIM), 1)
        st = jnp.where(at == 0, m_hi, jnp.where(at == 1, m_lo, jnp.where(at == 2, l_hi, l_lo)))
        return dot(pick, st.astype(jnp.bfloat16), NT)

    def scores(i):
        return jnp.concatenate(
            [
                dot(
                    q_ref[i, h * PER_KV : (h + 1) * PER_KV, :],
                    kv_ref[0, i, :, h * HEAD_DIM : (h + 1) * HEAD_DIM],
                    NT,
                )
                for h in range(KV_HEADS)
            ],
            axis=0,
        )

    s = jnp.concatenate(
        [jnp.where(lane < len_ref[base + i] - me * SLOTS, scores(i) * TO_LOG2, HIDDEN) for i in range(per_step)],
        axis=0,
    )
    m_hi, m_lo = halves(jnp.maximum(jnp.max(s, axis=1, keepdims=True), FLOOR))
    p = jnp.exp2(s - (m_hi + m_lo))
    tile = pack_stats(m_hi, m_lo, jnp.sum(p, axis=1, keepdims=True))
    p = p.astype(jnp.bfloat16)
    for i in range(per_step):
        for h in range(KV_HEADS):
            r = i * PER_SEQ + h * PER_KV
            o = dot(p[r : r + PER_KV], kv_ref[1, i, :, h * HEAD_DIM : (h + 1) * HEAD_DIM], NN)
            out_ref[i, h * PER_KV : (h + 1) * PER_KV, :] = o.astype(jnp.bfloat16)
    for i in range(0, per_step, 2):
        pair = tile[:, i * PER_SEQ : (i + 2) * PER_SEQ]
        out_ref[i, PER_SEQ:, :] = pair.astype(jnp.bfloat16)
        swapped = jnp.concatenate([pair[:, PER_SEQ:], pair[:, :PER_SEQ]], axis=1)
        out_ref[i + 1, PER_SEQ:, :] = swapped.astype(jnp.bfloat16)

    @pl.when((me >= base) & (me < base + per_step))
    def _():
        i = me - base
        row = lax.broadcasted_iota(jnp.int32, (16, KV_HEADS * HEAD_DIM), 0) == lax.rem(me, 16)

        def fresh(kind):
            rows = [
                jnp.sum(jnp.where(row, step_ref[t, kind].astype(jnp.float32), 0.0), axis=0, keepdims=True)
                for t in range(STEPS)
            ]
            rows.append(jnp.zeros((16 - STEPS, KV_HEADS * HEAD_DIM), jnp.float32))
            return jnp.concatenate(rows, axis=0).astype(jnp.bfloat16)

        keys, values = fresh(0), fresh(1)
        t = lax.rem(lax.broadcasted_iota(jnp.int32, (PER_SEQ, 16), 0), PER_KV) // GROUP
        sees = lax.broadcasted_iota(jnp.int32, (PER_SEQ, 16), 1) <= t
        s = jnp.where(lane < len_ref[me] - me * SLOTS, scores(i) * TO_LOG2, HIDDEN)
        f = jnp.concatenate(
            [
                dot(q_ref[i, h * PER_KV : (h + 1) * PER_KV, :], keys[:, h * HEAD_DIM : (h + 1) * HEAD_DIM], NT)
                for h in range(KV_HEADS)
            ],
            axis=0,
        )
        f = jnp.where(sees, f * TO_LOG2, HIDDEN)
        m_hi, m_lo = halves(
            jnp.maximum(jnp.max(s, axis=1, keepdims=True), jnp.max(f, axis=1, keepdims=True))
        )
        p = jnp.exp2(s - (m_hi + m_lo))
        pf = jnp.exp2(f - (m_hi + m_lo))
        total = jnp.sum(p, axis=1, keepdims=True) + jnp.sum(pf, axis=1, keepdims=True)
        stats = [jnp.broadcast_to(x, (PER_SEQ, 1)) for x in (m_hi, m_lo, total)]
        stats = [jnp.concatenate([x, jnp.zeros_like(x)], axis=0) for x in stats]
        out_ref[i, PER_SEQ:, :] = pack_stats(*stats).astype(jnp.bfloat16)
        p, pf = p.astype(jnp.bfloat16), pf.astype(jnp.bfloat16)
        for h in range(KV_HEADS):
            on, at = slice(h * PER_KV, (h + 1) * PER_KV), slice(h * HEAD_DIM, (h + 1) * HEAD_DIM)
            o = dot(p[on], kv_ref[1, i, :, at], NN) + dot(pf[on], values[:, at], NN)
            out_ref[i, on, :] = o.astype(jnp.bfloat16)


def decode_partials(lens, me, queries, cache, fresh):
    per_step = 16
    return pl.pallas_call(
        functools.partial(decode_kernel, per_step=per_step),
        grid_spec=pltpu.PrefetchScalarGridSpec(
            num_scalar_prefetch=2,
            grid=(SEQS // per_step,),
            in_specs=[
                pl.BlockSpec((per_step, PER_SEQ, HEAD_DIM), lambda i, *_: (i, 0, 0)),
                pl.BlockSpec((2, per_step, SLOTS, KV_HEADS * HEAD_DIM), lambda i, *_: (0, i, 0, 0)),
                pl.BlockSpec((STEPS, 2, 16, KV_HEADS * HEAD_DIM), lambda i, lens, me: (0, 0, me[0] // 16, 0)),
            ],
            out_specs=pl.BlockSpec((per_step, PACKED, HEAD_DIM), lambda i, *_: (i, 0, 0)),
        ),
        out_shape=jax.ShapeDtypeStruct((SEQS, PACKED, HEAD_DIM), jnp.bfloat16),
        compiler_params=pltpu.CompilerParams(vmem_limit_bytes=62 * 1024 * 1024),
        cost_estimate=pl.CostEstimate(flops=70_000_000, bytes_accessed=5_500_000, transcendentals=262144),
        name="decode_partials",
    )(lens, me, queries, cache, fresh)


def join_kernel(in_ref, out_ref, coef):
    peaks, totals = [], []
    for i in range(SEQS):
        st = in_ref[i, PER_SEQ:, :].astype(jnp.float32)
        peaks.append(st[0:1] + st[1:2])
        totals.append(st[2:3] + st[3:4])
    top = functools.reduce(jnp.maximum, peaks)
    scales = [jnp.exp2(m - top) for m in peaks]
    total = functools.reduce(jnp.add, [a * b for a, b in zip(scales, totals)])
    coef[...] = jnp.zeros_like(coef)
    for i in range(SEQS):
        coef[i : i + 1, :] = scales[i] / total
    columns = jnp.transpose(coef[...])
    acc = jnp.zeros((PER_SEQ, HEAD_DIM), jnp.float32)
    for i in range(SEQS):
        acc = acc + in_ref[i, :PER_SEQ, :].astype(jnp.float32) * columns[:PER_SEQ, i : i + 1]
    acc = acc.astype(jnp.bfloat16)
    for i in range(SEQS):
        out_ref[i] = acc


def join_shares(shares):
    return pl.pallas_call(
        join_kernel,
        out_shape=jax.ShapeDtypeStruct((SEQS, PER_SEQ, HEAD_DIM), jnp.bfloat16),
        in_specs=[pl.BlockSpec(memory_space=pltpu.VMEM)],
        out_specs=pl.BlockSpec(memory_space=pltpu.VMEM),
        scratch_shapes=[pltpu.VMEM((HEAD_DIM, HEAD_DIM), jnp.float32)],
        cost_estimate=pl.CostEstimate(flops=1_000_000, bytes_accessed=1_200_000, transcendentals=4096),
        name="join_shares",
    )(shares)


def block_kernel(doc_ref, kv_ref, out_ref):
    lane = lax.rem(lax.broadcasted_iota(jnp.int32, (16, KV_HEADS * HEAD_DIM), 1), HEAD_DIM)
    row = jnp.zeros((16, KV_HEADS * HEAD_DIM), jnp.float32)
    for d in range(1, 4):
        below = jnp.sum((doc_ref[...] < d).astype(jnp.float32), axis=1, keepdims=True)
        row = jnp.where(lane == d - 1, below, row)
    out_ref[0, 0 : 2 * ROWS, :] = kv_ref[...]
    out_ref[0, 2 * ROWS :, :] = row.astype(jnp.bfloat16)


def make_block(doc, key_values):
    vmem = pl.BlockSpec(memory_space=pltpu.VMEM)
    return pl.pallas_call(
        block_kernel,
        out_shape=jax.ShapeDtypeStruct((1, BLOCK, KV_HEADS * HEAD_DIM), jnp.bfloat16),
        in_specs=[vmem, vmem],
        out_specs=vmem,
        cost_estimate=pl.CostEstimate(flops=1000, bytes_accessed=400_000, transcendentals=0),
        name="make_block",
    )(doc, key_values)


def pair_valid(y, place, k):
    later = (place & (1 << (k.bit_length() - 1))) != 0
    return [y >= 1, later | (y >= 2)]


def prefill_kernel(at_ref, doc_ref, q_ref, *refs, moves, groups, first, last):
    blocks, rest = refs[: len(groups_of(moves, first))], refs[len(groups_of(moves, first)) :]
    state_in = None
    if not first:
        state_in, rest = rest[0], rest[1:]
    out_ref, rest = rest[0], rest[1:]
    if last:
        state, rest = rest[0], rest[1:]
    else:
        state = out_ref.at[0]
    keys_ref, values_ref, queries_ref, low_ref, flag_ref = rest
    step = pl.program_id(0)
    y, place = at_ref[0], at_ref[1]
    counts = groups_of(moves, first)
    places = [(r, b) for r, n in enumerate(counts) for b in range(n)]
    n = len(places)
    valid = [y >= d for d in range(3)] if first else []
    for k in moves:
        valid += pair_valid(y, place, k)

    @pl.when(step == 0)
    def _():
        doc = doc_ref[...]
        lows = []
        for at, (r, b) in enumerate(places):
            t = blocks[r][b, 2 * ROWS :, :].astype(jnp.float32)[0:1, :].astype(jnp.int32)
            low = jnp.where(doc == 1, t[:, 0:1], jnp.where(doc == 2, t[:, 1:2], jnp.where(doc == 3, t[:, 2:3], 0)))
            low = jnp.where(valid[at], low, ROWS)
            low_ref[at, 0:1, :] = jnp.concatenate([low] * FUSED, axis=1)
            lows.append(low)
        for g, (lo, hi) in enumerate(groups):
            some = jnp.min(functools.reduce(jnp.minimum, lows[lo:hi])) < ROWS
            whole = jnp.max(functools.reduce(jnp.maximum, lows[lo:hi])) == 0
            flag_ref[g] = jnp.where(some, jnp.where(whole, 1, 2), 0)

    @pl.when(lax.rem(step, max(HEADS // FUSED // KV_HEADS, 1)) == 0)
    def _():
        for at, (r, b) in enumerate(places):
            on = slice(at * ROWS, (at + 1) * ROWS)
            keys_ref[on, :] = blocks[r][b, 0:ROWS, :]
            values_ref[on, :] = blocks[r][b, ROWS : 2 * ROWS, :]

    for j in range(FUSED):
        queries_ref[j * ROWS : (j + 1) * ROWS, :] = q_ref[:, j * HEAD_DIM : (j + 1) * HEAD_DIM]

    def scores(lo, hi, masked):
        s = dot(keys_ref[lo * ROWS : hi * ROWS, :], queries_ref[...], NT)
        if not masked:
            return s
        row = lax.broadcasted_iota(jnp.int32, (ROWS, LANES), 0)
        parts = []
        for at in range(lo, hi):
            sees = row >= low_ref[at, 0:1, :]
            if first and at == 0:
                sees = sees & (row <= lax.rem(lax.broadcasted_iota(jnp.int32, (1, LANES), 1), ROWS))
            parts.append(jnp.where(sees, s[(at - lo) * ROWS : (at - lo + 1) * ROWS], HIDDEN))
        return jnp.concatenate(parts, axis=0)

    def weighted(lo, hi, p):
        return dot(values_ref[lo * ROWS : hi * ROWS, :], p.astype(jnp.bfloat16), TN)

    def put(peak, total, summed):
        state[0:HEAD_DIM, :] = summed
        state[HEAD_DIM : HEAD_DIM + 8, :] = jnp.broadcast_to(peak, (8, LANES))
        state[HEAD_DIM + 8 :, :] = jnp.broadcast_to(total, (8, LANES))

    if first:
        s = scores(0, 1, True)
        peak = jnp.max(s, axis=0, keepdims=True)
        p = jnp.exp2((s - peak) * TO_LOG2)
        put(peak, jnp.sum(p, axis=0, keepdims=True), weighted(0, 1, p))
    else:
        state[...] = state_in[0]

    def add(lo, hi, masked):
        about = state[HEAD_DIM : HEAD_DIM + 1, :] * TO_LOG2
        p = jnp.exp2(scores(lo, hi, masked) * TO_LOG2 - about)
        state[HEAD_DIM + 8 :, :] = state[HEAD_DIM + 8 :, :] + jnp.sum(p, axis=0, keepdims=True)
        state[0:HEAD_DIM, :] = state[0:HEAD_DIM, :] + weighted(lo, hi, p)

    for g, (lo, hi) in enumerate(groups):

        @pl.when(flag_ref[g] == 1)
        def _():
            add(lo, hi, False)

        @pl.when(flag_ref[g] == 2)
        def _():
            add(lo, hi, True)

    @pl.when(jnp.logical_not(jnp.max(state[HEAD_DIM + 8 : HEAD_DIM + 9, :]) < TOO_LARGE))
    def _():
        s = scores(0, n, True)
        peak = jnp.max(s, axis=0, keepdims=True)
        if not first:
            old = state_in[0, HEAD_DIM : HEAD_DIM + 1, :]
            peak = jnp.maximum(old, peak)
        p = jnp.exp2((s - peak) * TO_LOG2)
        total, summed = jnp.sum(p, axis=0, keepdims=True), weighted(0, n, p)
        if not first:
            factor = jnp.exp2((old - peak) * TO_LOG2)
            total = total + state_in[0, HEAD_DIM + 8 : HEAD_DIM + 9, :] * factor
            summed = summed + state_in[0, 0:HEAD_DIM, :] * factor
        put(peak, total, summed)

    if last:
        out = state[0:HEAD_DIM, :] / state[HEAD_DIM + 8 : HEAD_DIM + 9, :]
        out = jnp.transpose(out).astype(jnp.bfloat16)
        for j in range(FUSED):
            out_ref[:, j * HEAD_DIM : (j + 1) * HEAD_DIM] = out[j * ROWS : (j + 1) * ROWS]


def groups_of(moves, first):
    return ([1, 1, 1] if first else []) + [2] * len(moves)


def prefill_part(at, doc, queries, blocks, moves, groups, state, last, name):
    first = state is None
    counts = groups_of(moves, first)
    n = sum(counts)
    steps = HEADS // FUSED
    per_kv = steps // KV_HEADS
    q_spec = pl.BlockSpec((ROWS, FUSED * HEAD_DIM), lambda i, *_: (0, i))
    state_spec = pl.BlockSpec((1, STATE, LANES), lambda i, *_: (i, 0, 0))
    in_specs = [
        pl.BlockSpec((1, ROWS), lambda i, *_: (0, 0)),
        q_spec,
    ]
    in_specs += [pl.BlockSpec((c, BLOCK, HEAD_DIM), lambda i, *_: (0, 0, i // per_kv)) for c in counts]
    operands = [at, doc, queries, *blocks]
    scratch = []
    if not first:
        in_specs.append(state_spec)
        operands.append(state)
    if last:
        out_shape = jax.ShapeDtypeStruct((ROWS, HEADS * HEAD_DIM), jnp.bfloat16)
        out_spec = q_spec
        scratch.append(pltpu.VMEM((STATE, LANES), jnp.float32))
    else:
        out_shape = jax.ShapeDtypeStruct((steps, STATE, LANES), jnp.float32)
        out_spec = state_spec
    scratch += [
        pltpu.VMEM((n * ROWS, HEAD_DIM), jnp.bfloat16),
        pltpu.VMEM((n * ROWS, HEAD_DIM), jnp.bfloat16),
        pltpu.VMEM((LANES, HEAD_DIM), jnp.bfloat16),
        pltpu.VMEM((n, 8, LANES), jnp.int32),
        pltpu.SMEM((len(groups),), jnp.int32),
    ]
    return pl.pallas_call(
        functools.partial(prefill_kernel, moves=moves, groups=groups, first=first, last=last),
        grid_spec=pltpu.PrefetchScalarGridSpec(
            num_scalar_prefetch=1,
            grid=(steps,),
            in_specs=in_specs,
            out_specs=out_spec,
            scratch_shapes=scratch,
        ),
        out_shape=out_shape,
        compiler_params=pltpu.CompilerParams(vmem_limit_bytes=62 * 1024 * 1024),
        cost_estimate=pl.CostEstimate(flops=4 * n * ROWS * ROWS * HEADS * HEAD_DIM, bytes_accessed=4_000_000, transcendentals=0),
        name=name,
    )(*operands)


MOVES = (4, 1, 3, 5, 2, 6, 7)
CALLS = ((0, 3), (3, 7))
GROUPS = (((1, 5), (5, 9)), ((0, 4), (4, 8)))


def local(prefill_queries, prefill_key_values, fill_doc, decode_queries, step_key_values, stored_key_values, cached_len):
    y = lax.axis_index("y").astype(jnp.int32)
    place = lax.axis_index(PLANE).astype(jnp.int32)
    me = y * 8 + place

    own = make_block(fill_doc[None], prefill_key_values.reshape(2 * ROWS, KV_HEADS * HEAD_DIM))
    back1 = lax.ppermute(own, "y", [(i, i + 1) for i in range(3)])
    back2 = lax.ppermute(own, "y", [(i, i + 2) for i in range(2)])

    queries = decode_queries.reshape(STEPS, SEQS, KV_HEADS, GROUP, HEAD_DIM)
    queries = queries.transpose(1, 2, 0, 3, 4).reshape(SEQS, PER_SEQ, HEAD_DIM)
    shares = decode_partials(cached_len, me[None], queries, stored_key_values, step_key_values)

    packs = {}
    for bit in (1, 2, 4):
        other = jnp.where((place & bit) == 0, own, back2)
        packs[bit] = jnp.concatenate([back1, other], axis=0)
    packs, shares = lax.optimization_barrier((packs, shares))
    got = []
    for k in MOVES:
        if len(got) == CALLS[0][1]:
            packs, got = lax.optimization_barrier((packs, got))
        bit = 1 << (k.bit_length() - 1)
        got.append(lax.ppermute(packs[bit], PLANE, [(i, i ^ k) for i in range(8)]))

    at, doc = jnp.stack([y, place]), fill_doc[None]

    def part(call, state):
        a, b = CALLS[call]
        blocks = got[a:b] if state is not None else [own, back1, back2] + got[a:b]
        last = call == len(CALLS) - 1
        return prefill_part(
            at, doc, prefill_queries, blocks, MOVES[a:b], GROUPS[call], state, last, "prefill_%d" % call
        )

    shares = lax.all_to_all(shares, CTX, 0, 0)
    state = part(0, None)
    shares, state = lax.optimization_barrier((shares, state))
    spread = lax.all_to_all(join_shares(shares), CTX, 0, 0)
    fill_out = part(1, state)
    step_out = spread.reshape(SEQS, KV_HEADS, STEPS, GROUP, HEAD_DIM).transpose(2, 0, 1, 3, 4)
    return fill_out, step_out.reshape(STEPS, SEQS, HEADS * HEAD_DIM)


def solution(mesh):
    fine = Mesh(mesh.devices.reshape(4, 2, 4, 2, 2), ("y", "xh", "z", "xl", "c"))
    tp = ("xl", "c")
    placed = (
        P(CTX, tp),
        P(None, CTX, tp),
        P(CTX),
        P(None, None, tp),
        P(None, None, None, tp),
        P(None, None, CTX, tp),
        P(),
    )
    return jax.shard_map(
        local,
        mesh=fine,
        in_specs=placed,
        out_specs=(P(CTX, tp), P(None, None, tp)),
        check_vma=False,
    )
```

time: 98.7 us -> 105 us (1.064)
  waiting for transfers between devices: 19.9 us -> 1.38 us
  Pallas kernels: 34.8 us -> 48.2 us
  starting transfers between devices: 36.2 us -> 49.4 us
  local copies, waits for them, and re-layouts: 5.21 us -> 4.05 us
    ppermute x7, waiting for transfers between devices: 16.1 us -> 1.37 us  [local(): got.append(lax.ppermute(packs[bit], PLANE, [(i, i ^ k) for i in range(8)]))]
    pallas_call x4, Pallas kernels: 28.4 us -> 42 us  [the longest x2 37.8 us: prefill_part(): pl.pallas_call(functools.partial(prefill_kernel, moves=moves, groups=grou...]
    ppermute x7, starting transfers between devices: 11.7 us -> 21.9 us  [local(): got.append(lax.ppermute(packs[bit], PLANE, [(i, i ^ k) for i in range(8)]))]
    all_to_all x1, starting transfers between devices: 7.36 us -> 12.8 us  [local(): spread = lax.all_to_all(join_shares(shares), CTX, 0, 0)]
    all_to_all x1, waiting for transfers between devices: 3.79 us -> 0.01 us  [local(): shares = lax.all_to_all(shares, CTX, 0, 0)]
    all_to_all x1, starting transfers between devices: 9.41 us -> 6.86 us  [local(): shares = lax.all_to_all(shares, CTX, 0, 0)]
  transfers between devices with their start and end apart: 11 -> 11, of which waited for: 3 -> 1; matrix products, arithmetic and copies ran while one was open for 3% -> 3% of each run, Pallas kernels for 35% -> 44%
where the time goes in v3:
time: 105 us
  starting transfers between devices  49.4 us (47%)
  Pallas kernels  48.2 us (46%)
  local copies, waits for them, and re-layouts  4.05 us (4%)
  waiting for transfers between devices  1.38 us (1%)
    pallas_call x2, Pallas kernels, prefill_part(): pl.pallas_call(functools.partial(prefill_kernel, moves=moves, groups=grou...  37.8 us
    ppermute x7, starting transfers between devices, local(): got.append(lax.ppermute(packs[bit], PLANE, [(i, i ^ k) for i in range(8)]))  21.9 us
    all_to_all x1, starting transfers between devices, local(): spread = lax.all_to_all(join_shares(shares), CTX, 0, 0)  12.8 us
    all_to_all x1, starting transfers between devices, local(): shares = lax.all_to_all(shares, CTX, 0, 0)  6.86 us
    pallas_call x1, Pallas kernels, decode_partials(): pl.pallas_call(functools.partial(decode_kernel, per_step=per_step), grid_...  6.16 us
    ppermute x1, starting transfers between devices, local(): back2 = lax.ppermute(own, 'y', [(i, i + 2) for i in range(2)])  5.23 us
    ppermute x1, starting transfers between devices, local(): back1 = lax.ppermute(own, 'y', [(i, i + 1) for i in range(3)])  2.59 us
    pallas_call x1, Pallas kernels, join_shares(): pl.pallas_call(join_kernel, out_shape=jax.ShapeDtypeStruct((SEQS, PER_SEQ...  2.54 us
  transfers between devices with their start and end apart: 11, of which 1 were waited for; matrix products, arithmetic and copies ran while one was open for 3% of the time, Pallas kernels for 44%

profile of v3, /device:TPU:4, one launch (start us, length us, event | category | flops | bytes accessed | tf_op | source)
XLA Modules:
  0.0 104.6 jit_solution(9501486187503615539)
XLA Ops:
  0.6 1.7 %make_block.1.refs_0_ = bf16[1,400,256]{2,1,0:T(8,128)(2,1)} custom-call(s32[1,192]{1,0:T(1,128)} %bitcast.22, bf16[384,256]{1,0:T(8,128)(2,1)} %bitcast.21), custom_call_target="tpu_custom_call" | custom-call | flops 1000 | bytes 400000 | tf_op jit(solution)/shard_map/make_block/pallas_call | solution.py:201
  2.3 0.0 copy-start.1
  2.3 5.2 %collective-permute-start.1 = (bf16[1,400,256]{2,1,0:T(8,128)(2,1)}, bf16[1,400,256]{2,1,0:T(8,128)(2,1)S(1)}, u32[]{:S(2)}, u32[]{:S(2)}) collective-permute-start(bf16[1,400,256]{2,1,0:T(8,128)(2,1)} %make_block.1.refs_0_), channel_id=1, source_target_pairs={{0,64},{32,96},{1,65},{33,97},{2,66},{34,98},{3,67},{35,99},{4,68}... | collective-permute-start | bytes 614408 | tf_op jit(solution)/shard_map/ppermute | solution.py:392
  7.6 2.6 %collective-permute-start = (bf16[1,400,256]{2,1,0:T(8,128)(2,1)}, bf16[1,400,256]{2,1,0:T(8,128)(2,1)S(1)}, u32[]{:S(2)}, u32[]{:S(2)}) collective-permute-start(bf16[1,400,256]{2,1,0:T(8,128)(2,1)} %make_block.1.refs_0_), channel_id=1, source_target_pairs={{0,32},{32,64},{64,96},{1,33},{33,65},{65,97},{2,34},{34,66},{66,9... | collective-permute-start | bytes 614408 | tf_op jit(solution)/shard_map/ppermute | solution.py:391
  10.2 1.1 %copy.11 = bf16[16,8,16,128]{3,2,1,0:T(8,128)(2,1)S(1)} copy(bf16[16,8,16,128]{3,1,2,0:T(8,128)(2,1)} %bitcast.20) | data formatting | bytes 1048576
  11.4 0.9 copy.9
  12.3 6.2 %decode_partials.1 = bf16[32,80,128]{2,1,0:T(8,128)(2,1)} custom-call(s32[32]{0:T(128)} %len_ref.1, s32[1]{0:T(128)} %bitcast.4.me_ref, bf16[32,64,128]{2,1,0:T(8,128)(2,1)} %bitcast.17, bf16[2,32,128,256]{3,2,1,0:T(8,128)(2,1)} %kv_ref.1, bf16[4,2,32,256]{3,2,1,0:T(8,128)(2,1)} %step_ref.1), custom_call_target="tpu_custom_call" | custom-call | flops 70000000 | bytes 5500000 | tf_op jit(solution)/shard_map/decode_partials/pallas_call | solution.py:137
  18.5 0.0 collective-permute-done.1.refs_2_
  18.5 0.0 copy-done.1
  18.5 0.0 copy-start.2
  18.5 0.1 broadcast_select_fusion
  18.5 0.0 collective-permute-done.refs_1_
  18.6 0.0 copy-start.3
  18.6 0.1 pad_maximum_fusion
  18.7 0.6 collective-permute-start.2
  19.2 1.9 %collective-permute-start.3 = (bf16[2,400,256]{2,1,0:T(8,128)(2,1)S(1)}, bf16[2,400,256]{2,1,0:T(8,128)(2,1)S(1)}, u32[]{:S(2)}, u32[]{:S(2)}) collective-permute-start(bf16[2,400,256]{2,1,0:T(8,128)(2,1)S(1)} %get-tuple-element.13), channel_id=1, source_target_pairs={{0,4},{4,0},{8,12},{12,8},{16,20},{20,16},{24,28},{28,24},{1,5},{5... | collective-permute-start | bytes 1228808 | tf_op jit(solution)/shard_map/ppermute | solution.py:408
  21.2 2.5 %collective-permute-start.4 = (bf16[2,400,256]{2,1,0:T(8,128)(2,1)S(1)}, bf16[2,400,256]{2,1,0:T(8,128)(2,1)}, u32[]{:S(2)}, u32[]{:S(2)}) collective-permute-start(bf16[2,400,256]{2,1,0:T(8,128)(2,1)S(1)} %get-tuple-element.17), channel_id=1, source_target_pairs={{0,12},{4,8},{8,4},{12,0},{16,28},{20,24},{24,20},{28,16},{1,13},{... | collective-permute-start | bytes 1228808 | tf_op jit(solution)/shard_map/ppermute | solution.py:408
  23.7 6.9 %all-to-all-start = ((bf16[32,80,128]{2,1,0:T(8,128)(2,1)}), bf16[32,80,128]{2,1,0:T(8,128)(2,1)S(1)}, u32[]{:S(2)}, u32[]{:S(2)}) async-start(bf16[32,80,128]{2,1,0:T(8,128)(2,1)} %decode_partials.1), calls=%async_computation | async-start | bytes 1310720 | tf_op jit(solution)/shard_map/all_to_all | solution.py:420
  30.6 0.6 pad_add_fusion.at_ref
  31.2 0.0 collective-permute-done.2.refs_3_
  31.2 0.0 copy-start.4
  31.2 0.0 collective-permute-done.3.refs_4_
  31.2 0.0 copy-start.5
  31.2 1.3 %collective-permute-done.4.refs_5_ = bf16[2,400,256]{2,1,0:T(8,128)(2,1)} collective-permute-done((bf16[2,400,256]{2,1,0:T(8,128)(2,1)S(1)}, bf16[2,400,256]{2,1,0:T(8,128)(2,1)}, u32[]{:S(2)}, u32[]{:S(2)}) %collective-permute-start.4) | collective-permute-done | bytes 409632 | tf_op jit(solution)/shard_map/ppermute | solution.py:408
  32.6 8.4 %collective-permute-start.5 = (bf16[2,400,256]{2,1,0:T(8,128)(2,1)S(1)}, bf16[2,400,256]{2,1,0:T(8,128)(2,1)}, u32[]{:S(2)}, u32[]{:S(2)}) collective-permute-start(bf16[2,400,256]{2,1,0:T(8,128)(2,1)S(1)} %get-tuple-element.16), channel_id=1, source_target_pairs={{0,20},{4,16},{8,28},{12,24},{16,4},{20,0},{24,12},{28,8},{1,21},{... | collective-permute-start | bytes 1228808 | tf_op jit(solution)/shard_map/ppermute | solution.py:408
  41.0 2.6 %collective-permute-start.7 = (bf16[2,400,256]{2,1,0:T(8,128)(2,1)S(1)}, bf16[2,400,256]{2,1,0:T(8,128)(2,1)}, u32[]{:S(2)}, u32[]{:S(2)}) collective-permute-start(bf16[2,400,256]{2,1,0:T(8,128)(2,1)S(1)} %get-tuple-element.16), channel_id=1, source_target_pairs={{0,24},{4,28},{8,16},{12,20},{16,8},{20,12},{24,0},{28,4},{1,25},{... | collective-permute-start | bytes 1228808 | tf_op jit(solution)/shard_map/ppermute | solution.py:408
  43.5 3.0 %collective-permute-start.8 = (bf16[2,400,256]{2,1,0:T(8,128)(2,1)S(1)}, bf16[2,400,256]{2,1,0:T(8,128)(2,1)}, u32[]{:S(2)}, u32[]{:S(2)}) collective-permute-start(bf16[2,400,256]{2,1,0:T(8,128)(2,1)S(1)} %get-tuple-element.16), channel_id=1, source_target_pairs={{0,28},{4,24},{8,20},{12,16},{16,12},{20,8},{24,4},{28,0},{1,29},{... | collective-permute-start | bytes 1228808 | tf_op jit(solution)/shard_map/ppermute | solution.py:408
  46.6 0.0 copy-done.4
  46.6 0.0 copy-done.5
  46.6 2.9 %collective-permute-start.6 = (bf16[2,400,256]{2,1,0:T(8,128)(2,1)S(1)}, bf16[2,400,256]{2,1,0:T(8,128)(2,1)}, u32[]{:S(2)}, u32[]{:S(2)}) collective-permute-start(bf16[2,400,256]{2,1,0:T(8,128)(2,1)S(1)} %get-tuple-element.17), channel_id=1, source_target_pairs={{0,8},{4,12},{8,0},{12,4},{16,24},{20,28},{24,16},{28,20},{1,9},{5... | collective-permute-start | bytes 1228808 | tf_op jit(solution)/shard_map/ppermute | solution.py:408
  49.4 0.0 copy-done.2
  49.4 0.0 copy-done.3
  49.4 17.9 %prefill_0.1.refs_4_ = f32[2,144,1536]{2,1,0:T(8,128)} custom-call(s32[2]{0:T(128)} %pad_add_fusion.at_ref, s32[1,192]{1,0:T(1,128)} %bitcast.23, bf16[192,2048]{1,0:T(8,128)(2,1)} %q_ref.3, bf16[1,400,256]{2,1,0:T(8,128)(2,1)} %make_block.1.refs_0_, bf16[1,400,256]{2,1,0:T(8,128)(2,1)} %copy-done.3, bf16[1,400,256]{2,1,0:T(8,128)(2,1)} %copy-done.2, ...), custom_call_target="tpu_custom_call" | custom-call | flops 2717908992 | bytes 4000000 | tf_op jit(solution)/shard_map/prefill_0/pallas_call | solution.py:364
  67.3 0.0 all-to-all-done.in_ref
  67.3 0.0 copy-start
  67.3 0.8 copy-done
  68.1 2.5 %join_shares.1 = bf16[32,64,128]{2,1,0:T(8,128)(2,1)} custom-call(bf16[32,80,128]{2,1,0:T(8,128)(2,1)} %copy-done), custom_call_target="tpu_custom_call" | custom-call | flops 1000000 | bytes 1200000 | tf_op jit(solution)/shard_map/join_shares/pallas_call | solution.py:178
  70.7 12.8 %all-to-all-start.1 = ((bf16[32,64,128]{2,1,0:T(8,128)(2,1)}), bf16[32,64,128]{2,1,0:T(8,128)(2,1)S(1)}, u32[]{:S(2)}, u32[]{:S(2)}) async-start(bf16[32,64,128]{2,1,0:T(8,128)(2,1)} %join_shares.1), calls=%async_computation.1 | async-start | bytes 1048576 | tf_op jit(solution)/shard_map/all_to_all | solution.py:423
  83.5 0.0 collective-permute-done.5.refs_0_
  83.5 0.0 collective-permute-done.6.refs_1_
  83.5 0.0 collective-permute-done.7.refs_2_
  83.5 0.0 collective-permute-done.8.refs_3_
  83.5 19.9 %prefill_1.1 = bf16[192,2048]{1,0:T(8,128)(2,1)} custom-call(s32[2]{0:T(128)} %pad_add_fusion.at_ref, s32[1,192]{1,0:T(1,128)} %bitcast.24, bf16[192,2048]{1,0:T(8,128)(2,1)} %q_ref.3, bf16[2,400,256]{2,1,0:T(8,128)(2,1)} %collective-permute-done.5.refs_0_, bf16[2,400,256]{2,1,0:T(8,128)(2,1)} %collective-permute-done.6.refs_1_, ...), custom_call_target="tpu_custom_call" | custom-call | flops 2415919104 | bytes 4000000 | tf_op jit(solution)/shard_map/prefill_1/pallas_call | solution.py:364
  103.4 0.0 all-to-all-done.1
  103.5 0.1 copy.10
  103.5 1.0 reshape.23
Async XLA Ops:
  2.3 16.1 %copy-start.1 = (bf16[1,400,256]{2,1,0:T(8,128)(2,1)S(1)}, bf16[1,400,256]{2,1,0:T(8,128)(2,1)}, u32[]{:S(2)}) copy-start(bf16[1,400,256]{2,1,0:T(8,128)(2,1)} %make_block.1.refs_0_) | copy-start | bytes 614404
  2.3 16.1 %collective-permute-start.1 = (bf16[1,400,256]{2,1,0:T(8,128)(2,1)}, bf16[1,400,256]{2,1,0:T(8,128)(2,1)S(1)}, u32[]{:S(2)}, u32[]{:S(2)}) collective-permute-start(bf16[1,400,256]{2,1,0:T(8,128)(2,1)} %make_block.1.refs_0_), channel_id=1, source_target_pairs={{0,64},{32,96},{1,65},{33,97},{2,66},{34,98},{3,67},{35,99},{4,68}... | collective-permute-start | bytes 614408 | tf_op jit(solution)/shard_map/ppermute | solution.py:392
  7.6 11.0 %collective-permute-start = (bf16[1,400,256]{2,1,0:T(8,128)(2,1)}, bf16[1,400,256]{2,1,0:T(8,128)(2,1)S(1)}, u32[]{:S(2)}, u32[]{:S(2)}) collective-permute-start(bf16[1,400,256]{2,1,0:T(8,128)(2,1)} %make_block.1.refs_0_), channel_id=1, source_target_pairs={{0,32},{32,64},{64,96},{1,33},{33,65},{65,97},{2,34},{34,66},{66,9... | collective-permute-start | bytes 614408 | tf_op jit(solution)/shard_map/ppermute | solution.py:391
  18.5 31.0 %copy-start.2 = (bf16[1,400,256]{2,1,0:T(8,128)(2,1)}, bf16[1,400,256]{2,1,0:T(8,128)(2,1)S(1)}, u32[]{:S(2)}) copy-start(bf16[1,400,256]{2,1,0:T(8,128)(2,1)S(1)} %collective-permute-done.1.refs_2_) | copy-start | bytes 614404
  18.6 30.9 %copy-start.3 = (bf16[1,400,256]{2,1,0:T(8,128)(2,1)}, bf16[1,400,256]{2,1,0:T(8,128)(2,1)S(1)}, u32[]{:S(2)}) copy-start(bf16[1,400,256]{2,1,0:T(8,128)(2,1)S(1)} %collective-permute-done.refs_1_) | copy-start | bytes 614404
  18.7 12.5 %collective-permute-start.2 = (bf16[2,400,256]{2,1,0:T(8,128)(2,1)S(1)}, bf16[2,400,256]{2,1,0:T(8,128)(2,1)S(1)}, u32[]{:S(2)}, u32[]{:S(2)}) collective-permute-start(bf16[2,400,256]{2,1,0:T(8,128)(2,1)S(1)} %get-tuple-element.16), channel_id=1, source_target_pairs={{0,16},{4,20},{8,24},{12,28},{16,0},{20,4},{24,8},{28,12},{1,17},{... | collective-permute-start | bytes 1228808 | tf_op jit(solution)/shard_map/ppermute | solution.py:408
  19.2 12.0 %collective-permute-start.3 = (bf16[2,400,256]{2,1,0:T(8,128)(2,1)S(1)}, bf16[2,400,256]{2,1,0:T(8,128)(2,1)S(1)}, u32[]{:S(2)}, u32[]{:S(2)}) collective-permute-start(bf16[2,400,256]{2,1,0:T(8,128)(2,1)S(1)} %get-tuple-element.13), channel_id=1, source_target_pairs={{0,4},{4,0},{8,12},{12,8},{16,20},{20,16},{24,28},{28,24},{1,5},{5... | collective-permute-start | bytes 1228808 | tf_op jit(solution)/shard_map/ppermute | solution.py:408
  21.2 11.4 %collective-permute-start.4 = (bf16[2,400,256]{2,1,0:T(8,128)(2,1)S(1)}, bf16[2,400,256]{2,1,0:T(8,128)(2,1)}, u32[]{:S(2)}, u32[]{:S(2)}) collective-permute-start(bf16[2,400,256]{2,1,0:T(8,128)(2,1)S(1)} %get-tuple-element.17), channel_id=1, source_target_pairs={{0,12},{4,8},{8,4},{12,0},{16,28},{20,24},{24,20},{28,16},{1,13},{... | collective-permute-start | bytes 1228808 | tf_op jit(solution)/shard_map/ppermute | solution.py:408
  23.7 43.6 %all-to-all-start = ((bf16[32,80,128]{2,1,0:T(8,128)(2,1)}), bf16[32,80,128]{2,1,0:T(8,128)(2,1)S(1)}, u32[]{:S(2)}, u32[]{:S(2)}) async-start(bf16[32,80,128]{2,1,0:T(8,128)(2,1)} %decode_partials.1), calls=%async_computation | async-start | bytes 1310720 | tf_op jit(solution)/shard_map/all_to_all | solution.py:420
  31.2 15.4 %copy-start.4 = (bf16[2,400,256]{2,1,0:T(8,128)(2,1)}, bf16[2,400,256]{2,1,0:T(8,128)(2,1)S(1)}, u32[]{:S(2)}) copy-start(bf16[2,400,256]{2,1,0:T(8,128)(2,1)S(1)} %collective-permute-done.2.refs_3_) | copy-start | bytes 1228804
  31.2 15.4 %copy-start.5 = (bf16[2,400,256]{2,1,0:T(8,128)(2,1)}, bf16[2,400,256]{2,1,0:T(8,128)(2,1)S(1)}, u32[]{:S(2)}) copy-start(bf16[2,400,256]{2,1,0:T(8,128)(2,1)S(1)} %collective-permute-done.3.refs_4_) | copy-start | bytes 1228804
  32.6 50.9 %collective-permute-start.5 = (bf16[2,400,256]{2,1,0:T(8,128)(2,1)S(1)}, bf16[2,400,256]{2,1,0:T(8,128)(2,1)}, u32[]{:S(2)}, u32[]{:S(2)}) collective-permute-start(bf16[2,400,256]{2,1,0:T(8,128)(2,1)S(1)} %get-tuple-element.16), channel_id=1, source_target_pairs={{0,20},{4,16},{8,28},{12,24},{16,4},{20,0},{24,12},{28,8},{1,21},{... | collective-permute-start | bytes 1228808 | tf_op jit(solution)/shard_map/ppermute | solution.py:408
  41.0 42.6 %collective-permute-start.7 = (bf16[2,400,256]{2,1,0:T(8,128)(2,1)S(1)}, bf16[2,400,256]{2,1,0:T(8,128)(2,1)}, u32[]{:S(2)}, u32[]{:S(2)}) collective-permute-start(bf16[2,400,256]{2,1,0:T(8,128)(2,1)S(1)} %get-tuple-element.16), channel_id=1, source_target_pairs={{0,24},{4,28},{8,16},{12,20},{16,8},{20,12},{24,0},{28,4},{1,25},{... | collective-permute-start | bytes 1228808 | tf_op jit(solution)/shard_map/ppermute | solution.py:408
  43.5 40.0 %collective-permute-start.8 = (bf16[2,400,256]{2,1,0:T(8,128)(2,1)S(1)}, bf16[2,400,256]{2,1,0:T(8,128)(2,1)}, u32[]{:S(2)}, u32[]{:S(2)}) collective-permute-start(bf16[2,400,256]{2,1,0:T(8,128)(2,1)S(1)} %get-tuple-element.16), channel_id=1, source_target_pairs={{0,28},{4,24},{8,20},{12,16},{16,12},{20,8},{24,4},{28,0},{1,29},{... | collective-permute-start | bytes 1228808 | tf_op jit(solution)/shard_map/ppermute | solution.py:408
  46.6 36.9 %collective-permute-start.6 = (bf16[2,400,256]{2,1,0:T(8,128)(2,1)S(1)}, bf16[2,400,256]{2,1,0:T(8,128)(2,1)}, u32[]{:S(2)}, u32[]{:S(2)}) collective-permute-start(bf16[2,400,256]{2,1,0:T(8,128)(2,1)S(1)} %get-tuple-element.17), channel_id=1, source_target_pairs={{0,8},{4,12},{8,0},{12,4},{16,24},{20,28},{24,16},{28,20},{1,9},{5... | collective-permute-start | bytes 1228808 | tf_op jit(solution)/shard_map/ppermute | solution.py:408
  67.3 0.8 copy-start
  70.7 32.8 %all-to-all-start.1 = ((bf16[32,64,128]{2,1,0:T(8,128)(2,1)}), bf16[32,64,128]{2,1,0:T(8,128)(2,1)S(1)}, u32[]{:S(2)}, u32[]{:S(2)}) async-start(bf16[32,64,128]{2,1,0:T(8,128)(2,1)} %join_shares.1), calls=%async_computation.1 | async-start | bytes 1048576 | tf_op jit(solution)/shard_map/all_to_all | solution.py:423

commit v4 on v3

--- a/solution.py
+++ b/solution.py
@@ -208,13 +208,25 @@
     )(doc, key_values)
 
 
-def pair_valid(y, place, k):
-    later = (place & (1 << (k.bit_length() - 1))) != 0
-    return [y >= 1, later | (y >= 2)]
-
-
-def prefill_kernel(at_ref, doc_ref, q_ref, *refs, moves, groups, first, last):
-    blocks, rest = refs[: len(groups_of(moves, first))], refs[len(groups_of(moves, first)) :]
+def block_valid(y, xh, z, kind):
+    across = (xh == 1) | (y >= 2)
+    if kind == "own":
+        return [y >= 0]
+    if kind == "row":
+        return [y >= 1] * 4
+    if kind == "back":
+        return [y >= 2]
+    if kind == "across":
+        return [across]
+    bit = 1 << (kind.bit_length() - 1)
+    return [((z & bit) != 0) | (y >= 2), across]
+
+
+COUNT = {"own": 1, "row": 4, "back": 1, "across": 1, 1: 2, 2: 2, 3: 2}
+
+
+def prefill_kernel(at_ref, doc_ref, q_ref, *refs, sources, groups, first, last):
+    blocks, rest = refs[: len(sources)], refs[len(sources) :]
     state_in = None
     if not first:
         state_in, rest = rest[0], rest[1:]
@@ -225,13 +237,13 @@
         state = out_ref.at[0]
     keys_ref, values_ref, queries_ref, low_ref, flag_ref = rest
     step = pl.program_id(0)
-    y, place = at_ref[0], at_ref[1]
-    counts = groups_of(moves, first)
+    y, xh, z = at_ref[0], at_ref[1], at_ref[2]
+    counts = [COUNT[source] for source in sources]
     places = [(r, b) for r, n in enumerate(counts) for b in range(n)]
     n = len(places)
-    valid = [y >= d for d in range(3)] if first else []
-    for k in moves:
-        valid += pair_valid(y, place, k)
+    valid = []
+    for source in sources:
+        valid += block_valid(y, xh, z, source)
 
     @pl.when(step == 0)
     def _():
@@ -325,13 +337,9 @@
             out_ref[:, j * HEAD_DIM : (j + 1) * HEAD_DIM] = out[j * ROWS : (j + 1) * ROWS]
 
 
-def groups_of(moves, first):
-    return ([1, 1, 1] if first else []) + [2] * len(moves)
-
-
-def prefill_part(at, doc, queries, blocks, moves, groups, state, last, name):
+def prefill_part(at, doc, queries, blocks, sources, groups, state, last, name):
     first = state is None
-    counts = groups_of(moves, first)
+    counts = [COUNT[source] for source in sources]
     n = sum(counts)
     steps = HEADS // FUSED
     per_kv = steps // KV_HEADS
@@ -362,7 +370,7 @@
         pltpu.SMEM((len(groups),), jnp.int32),
     ]
     return pl.pallas_call(
-        functools.partial(prefill_kernel, moves=moves, groups=groups, first=first, last=last),
+        functools.partial(prefill_kernel, sources=sources, groups=groups, first=first, last=last),
         grid_spec=pltpu.PrefetchScalarGridSpec(
             num_scalar_prefetch=1,
             grid=(steps,),
@@ -377,51 +385,56 @@
     )(*operands)
 
 
-MOVES = (4, 1, 3, 5, 2, 6, 7)
-CALLS = ((0, 3), (3, 7))
-GROUPS = (((1, 5), (5, 9)), ((0, 4), (4, 8)))
+SIDE = (2, 1, 3)
 
 
 def local(prefill_queries, prefill_key_values, fill_doc, decode_queries, step_key_values, stored_key_values, cached_len):
-    y = lax.axis_index("y").astype(jnp.int32)
-    place = lax.axis_index(PLANE).astype(jnp.int32)
-    me = y * 8 + place
+    y, xh, z = [lax.axis_index(axis).astype(jnp.int32) for axis in CTX]
+    me = (y * 2 + xh) * 4 + z
 
     own = make_block(fill_doc[None], prefill_key_values.reshape(2 * ROWS, KV_HEADS * HEAD_DIM))
     back1 = lax.ppermute(own, "y", [(i, i + 1) for i in range(3)])
     back2 = lax.ppermute(own, "y", [(i, i + 2) for i in range(2)])
+    row = lax.all_to_all(jnp.broadcast_to(back1, (4,) + back1.shape[1:]), "z", 0, 0)
+    across = lax.ppermute(jnp.where(xh == 0, own, back2), "xh", [(0, 1), (1, 0)])
 
     queries = decode_queries.reshape(STEPS, SEQS, KV_HEADS, GROUP, HEAD_DIM)
     queries = queries.transpose(1, 2, 0, 3, 4).reshape(SEQS, PER_SEQ, HEAD_DIM)
     shares = decode_partials(cached_len, me[None], queries, stored_key_values, step_key_values)
 
-    packs = {}
-    for bit in (1, 2, 4):
-        other = jnp.where((place & bit) == 0, own, back2)
-        packs[bit] = jnp.concatenate([back1, other], axis=0)
+    far_row = lax.ppermute(row, "xh", [(0, 1), (1, 0)])
+    packs = {bit: jnp.concatenate([jnp.where((z & bit) == 0, own, back2), across], axis=0) for bit in (1, 2)}
     packs, shares = lax.optimization_barrier((packs, shares))
-    got = []
-    for k in MOVES:
-        if len(got) == CALLS[0][1]:
-            packs, got = lax.optimization_barrier((packs, got))
-        bit = 1 << (k.bit_length() - 1)
-        got.append(lax.ppermute(packs[bit], PLANE, [(i, i ^ k) for i in range(8)]))
-
-    at, doc = jnp.stack([y, place]), fill_doc[None]
-
-    def part(call, state):
-        a, b = CALLS[call]
-        blocks = got[a:b] if state is not None else [own, back1, back2] + got[a:b]
-        last = call == len(CALLS) - 1
-        return prefill_part(
-            at, doc, prefill_queries, blocks, MOVES[a:b], GROUPS[call], state, last, "prefill_%d" % call
-        )
+    side = {k: lax.ppermute(packs[min(k, 2)], "z", [(i, i ^ k) for i in range(4)]) for k in SIDE}
+
+    at, doc = jnp.stack([y, xh, z]), fill_doc[None]
 
     shares = lax.all_to_all(shares, CTX, 0, 0)
-    state = part(0, None)
+    state = prefill_part(
+        at,
+        doc,
+        prefill_queries,
+        [own, row, back2, across],
+        ("own", "row", "back", "across"),
+        ((1, 5), (5, 7)),
+        None,
+        False,
+        "prefill_first",
+    )
     shares, state = lax.optimization_barrier((shares, state))
     spread = lax.all_to_all(join_shares(shares), CTX, 0, 0)
-    fill_out = part(1, state)
+    fill_out = prefill_part(
+        at,
+        doc,
+        prefill_queries,
+        [far_row] + [side[k] for k in SIDE],
+        ("row",) + SIDE,
+        ((0, 4), (4, 7), (7, 10)),
+        state,
+        True,
+        "prefill_last",
+    )
+    spread, fill_out = lax.optimization_barrier((spread, fill_out))
     step_out = spread.reshape(SEQS, KV_HEADS, STEPS, GROUP, HEAD_DIM).transpose(2, 0, 1, 3, 4)
     return fill_out, step_out.reshape(STEPS, SEQS, HEADS * HEAD_DIM)
 

time: 105 us -> 100 us (0.952)
  the two profiles are of different devices: /device:TPU:4 before, /device:TPU:14 now
where the time goes in v4:
time: 100 us; the launch traced here: 98.3 us
  Pallas kernels  51.3 us (51%)
  starting transfers between devices  35.2 us (35%)
  waiting for transfers between devices  4.57 us (5%)
  local copies, waits for them, and re-layouts  3.95 us (4%)
  other arithmetic  2.52 us (3%)
    pallas_call x2, Pallas kernels, prefill_part(): pl.pallas_call(functools.partial(prefill_kernel, sources=sources, groups=...  40.8 us
    all_to_all x1, starting transfers between devices, local(): shares = lax.all_to_all(shares, CTX, 0, 0)  9.33 us
    all_to_all x1, starting transfers between devices, local(): spread = lax.all_to_all(join_shares(shares), CTX, 0, 0)  8.83 us
    pallas_call x1, Pallas kernels, decode_partials(): pl.pallas_call(functools.partial(decode_kernel, per_step=per_step), grid_...  6.17 us
    all_to_all x1, starting transfers between devices, local(): lax.all_to_all(jnp.broadcast_to(back1, (4,) + back1.shape[1:]), 'z', 0, 0)  5.31 us
    ppermute x3, starting transfers between devices, local(): lax.ppermute(packs[min(k, 2)], 'z', [(i, i ^ k) for i in range(4)])  4.14 us
    ppermute x1, starting transfers between devices, local(): back1 = lax.ppermute(own, 'y', [(i, i + 1) for i in range(3)])  3.47 us
    ppermute x1, waiting for transfers between devices, local(): back1 = lax.ppermute(own, 'y', [(i, i + 1) for i in range(3)])  3.4 us
  transfers between devices with their start and end apart: 10, of which 2 were waited for; matrix products, arithmetic and copies ran while one was open for 5% of the time, Pallas kernels for 50%

profile of v4, /device:TPU:14, one launch (start us, length us, event | category | flops | bytes accessed | tf_op | source)
XLA Modules:
  0.0 98.3 jit_solution(7471172581388350675)
XLA Ops:
  0.6 0.0 copy-start.2
  0.6 1.8 %make_block.1.refs_0_ = bf16[1,400,256]{2,1,0:T(8,128)(2,1)} custom-call(s32[1,192]{1,0:T(1,128)} %bitcast.25, bf16[384,256]{1,0:T(8,128)(2,1)} %bitcast.24), custom_call_target="tpu_custom_call" | custom-call | flops 1000 | bytes 400000 | tf_op jit(solution)/shard_map/make_block/pallas_call | solution.py:201
  2.4 3.5 %collective-permute-start.2 = (bf16[1,400,256]{2,1,0:T(8,128)(2,1)}, bf16[1,400,256]{2,1,0:T(8,128)(2,1)S(1)}, u32[]{:S(2)}, u32[]{:S(2)}) collective-permute-start(bf16[1,400,256]{2,1,0:T(8,128)(2,1)} %make_block.1.refs_0_), channel_id=1, source_target_pairs={{0,32},{32,64},{64,96},{1,33},{33,65},{65,97},{2,34},{34,66},{66,9... | collective-permute-start | bytes 614408 | tf_op jit(solution)/shard_map/ppermute | solution.py:396
  5.9 2.0 %collective-permute-start = (bf16[1,400,256]{2,1,0:T(8,128)(2,1)}, bf16[1,400,256]{2,1,0:T(8,128)(2,1)S(1)}, u32[]{:S(2)}, u32[]{:S(2)}) collective-permute-start(bf16[1,400,256]{2,1,0:T(8,128)(2,1)} %make_block.1.refs_0_), channel_id=1, source_target_pairs={{0,64},{32,96},{1,65},{33,97},{2,66},{34,98},{3,67},{35,99},{4,68}... | collective-permute-start | bytes 614408 | tf_op jit(solution)/shard_map/ppermute | solution.py:397
  7.9 3.4 %collective-permute-done.2 = bf16[1,400,256]{2,1,0:T(8,128)(2,1)S(1)} collective-permute-done((bf16[1,400,256]{2,1,0:T(8,128)(2,1)}, bf16[1,400,256]{2,1,0:T(8,128)(2,1)S(1)}, u32[]{:S(2)}, u32[]{:S(2)}) %collective-permute-start.2) | collective-permute-done | bytes 204832 | tf_op jit(solution)/shard_map/ppermute | solution.py:396
  11.3 0.9 broadcast_in_dim.17
  12.2 5.3 %all-to-all-start.1 = ((bf16[4,400,256]{2,1,0:T(8,128)(2,1)}), bf16[4,400,256]{2,1,0:T(8,128)(2,1)S(1)}, u32[]{:S(2)}, u32[]{:S(2)}) async-start(bf16[4,400,256]{2,1,0:T(8,128)(2,1)} %broadcast_in_dim.17), calls=%async_computation.1 | async-start | bytes 1638400 | tf_op jit(solution)/shard_map/all_to_all | solution.py:398
  17.6 0.0 collective-permute-done.refs_2_
  17.6 0.0 copy-start.3
  17.6 1.1 %broadcast_select_fusion = (bf16[1,400,256]{2,1,0:T(8,128)(2,1)S(1)}, bf16[1,400,256]{2,1,0:T(8,128)(2,1)S(1)}, bf16[1,400,256]{2,1,0:T(8,128)(2,1)S(1)}) fusion(bf16[1,400,256]{2,1,0:T(8,128)(2,1)} %make_block.1.refs_0_, bf16[1,400,256]{2,1,0:T(8,128)(2,1)S(1)} %collective-permute-done.refs_2_, pred[]{:T(512)S(6)} %eq.11, pred[]{:T(512)S(6)} %eq.10, pred[]{:T(512)S(6)} %eq.9), kind=kLoop, calls=%fused_computation.2 | loop fusion | flops 307200 | bytes 1024003 | tf_op jit(solution)/shard_map/jit(_where)/select_n | solution.py:406
  18.6 1.5 %collective-permute-start.1 = (bf16[1,400,256]{2,1,0:T(8,128)(2,1)S(1)}, bf16[1,400,256]{2,1,0:T(8,128)(2,1)S(1)}, u32[]{:S(2)}, u32[]{:S(2)}) collective-permute-start(bf16[1,400,256]{2,1,0:T(8,128)(2,1)S(1)} %get-tuple-element.17), channel_id=1, source_target_pairs={{0,16},{16,0},{1,17},{17,1},{2,18},{18,2},{3,19},{19,3},{4,20},{20... | collective-permute-start | bytes 614408 | tf_op jit(solution)/shard_map/ppermute | solution.py:399
  20.1 0.0 copy-done.2
  20.1 0.1 copy.11
  20.2 0.9 copy.9
  21.2 0.0 copy-done.3
  21.2 6.2 %decode_partials.1 = bf16[32,80,128]{2,1,0:T(8,128)(2,1)} custom-call(s32[32]{0:T(128)} %len_ref.1, s32[1]{0:T(128)} %bitcast.2.me_ref, bf16[32,64,128]{2,1,0:T(8,128)(2,1)} %bitcast.19, bf16[2,32,128,256]{3,2,1,0:T(8,128)(2,1)} %kv_ref.1, bf16[4,2,32,256]{3,2,1,0:T(8,128)(2,1)} %step_ref.1), custom_call_target="tpu_custom_call" | custom-call | flops 70000000 | bytes 5500000 | tf_op jit(solution)/shard_map/decode_partials/pallas_call | solution.py:137
  27.3 0.0 collective-permute-done.1.refs_3_
  27.3 0.0 copy-start.4
  27.3 0.8 pad_maximum_fusion
  28.2 1.1 %all-to-all-done.1.refs_1_ = bf16[4,400,256]{2,1,0:T(8,128)(2,1)S(1)} async-done(((bf16[4,400,256]{2,1,0:T(8,128)(2,1)}), bf16[4,400,256]{2,1,0:T(8,128)(2,1)S(1)}, u32[]{:S(2)}, u32[]{:S(2)}) %all-to-all-start.1) | async-done | bytes 819232 | tf_op jit(solution)/shard_map/all_to_all | solution.py:398
  29.3 0.0 copy-start.1
  29.3 0.0 copy-done.4
  29.3 9.3 %all-to-all-start = ((bf16[32,80,128]{2,1,0:T(8,128)(2,1)}), bf16[32,80,128]{2,1,0:T(8,128)(2,1)S(1)}, u32[]{:S(2)}, u32[]{:S(2)}) async-start(bf16[32,80,128]{2,1,0:T(8,128)(2,1)} %decode_partials.1), calls=%async_computation | async-start | bytes 1310720 | tf_op jit(solution)/shard_map/all_to_all | solution.py:412
  38.7 0.6 collective-permute-start.3
  39.3 0.6 pad_add_fusion.at_ref
  39.9 3.0 %collective-permute-start.4 = (bf16[2,400,256]{2,1,0:T(8,128)(2,1)S(1)}, bf16[2,400,256]{2,1,0:T(8,128)(2,1)}, u32[]{:S(2)}, u32[]{:S(2)}) collective-permute-start(bf16[2,400,256]{2,1,0:T(8,128)(2,1)S(1)} %get-tuple-element.11), channel_id=1, source_target_pairs={{0,8},{4,12},{8,0},{12,4},{1,9},{5,13},{9,1},{13,5},{2,10},{6,14},... | collective-permute-start | bytes 1228808 | tf_op jit(solution)/shard_map/ppermute | solution.py:408
  42.9 1.2 %collective-permute-start.6 = (bf16[2,400,256]{2,1,0:T(8,128)(2,1)S(1)}, bf16[2,400,256]{2,1,0:T(8,128)(2,1)}, u32[]{:S(2)}, u32[]{:S(2)}) collective-permute-start(bf16[2,400,256]{2,1,0:T(8,128)(2,1)S(1)} %get-tuple-element.11), channel_id=1, source_target_pairs={{0,12},{4,8},{8,4},{12,0},{1,13},{5,9},{9,5},{13,1},{2,14},{6,10},... | collective-permute-start | bytes 1228808 | tf_op jit(solution)/shard_map/ppermute | solution.py:408
  44.1 0.0 collective-permute-start.5
  44.1 0.0 copy-done.1
  44.1 17.1 %prefill_first.1.refs_4_ = f32[2,144,1536]{2,1,0:T(8,128)} custom-call(s32[3]{0:T(128)} %pad_add_fusion.at_ref, s32[1,192]{1,0:T(1,128)} %bitcast.26, bf16[192,2048]{1,0:T(8,128)(2,1)} %q_ref.3, bf16[1,400,256]{2,1,0:T(8,128)(2,1)} %make_block.1.refs_0_, bf16[4,400,256]{2,1,0:T(8,128)(2,1)} %copy-done.1, bf16[1,400,256]{2,1,0:T(8,128)(2,1)} %copy-done.3, ...), custom_call_target="tpu_custom_call" | custom-call | flops 2113929216 | bytes 4000000 | tf_op jit(solution)/shard_map/prefill_first/pallas_call | solution.py:372
  61.2 0.0 all-to-all-done.in_ref
  61.2 0.0 copy-start
  61.2 0.8 copy-done
  62.0 2.5 %join_shares.1 = bf16[32,64,128]{2,1,0:T(8,128)(2,1)} custom-call(bf16[32,80,128]{2,1,0:T(8,128)(2,1)} %copy-done), custom_call_target="tpu_custom_call" | custom-call | flops 1000000 | bytes 1200000 | tf_op jit(solution)/shard_map/join_shares/pallas_call | solution.py:178
  64.6 8.8 %all-to-all-start.2 = ((bf16[32,64,128]{2,1,0:T(8,128)(2,1)}), bf16[32,64,128]{2,1,0:T(8,128)(2,1)S(1)}, u32[]{:S(2)}, u32[]{:S(2)}) async-start(bf16[32,64,128]{2,1,0:T(8,128)(2,1)} %join_shares.1), calls=%async_computation.2 | async-start | bytes 1048576 | tf_op jit(solution)/shard_map/all_to_all | solution.py:425
  73.4 0.0 collective-permute-done.4.refs_1_
  73.4 0.0 collective-permute-done.5.refs_2_
  73.4 0.0 collective-permute-done.6.refs_3_
  73.5 0.0 collective-permute-done.3.refs_0_
  73.5 23.7 %prefill_last.1 = bf16[192,2048]{1,0:T(8,128)(2,1)} custom-call(s32[3]{0:T(128)} %pad_add_fusion.at_ref, s32[1,192]{1,0:T(1,128)} %bitcast.27, bf16[192,2048]{1,0:T(8,128)(2,1)} %q_ref.3, bf16[4,400,256]{2,1,0:T(8,128)(2,1)} %collective-permute-done.3.refs_0_, bf16[2,400,256]{2,1,0:T(8,128)(2,1)} %collective-permute-done.4.refs_1_, ...), custom_call_target="tpu_custom_call" | custom-call | flops 3019898880 | bytes 4000000 | tf_op jit(solution)/shard_map/prefill_last/pallas_call | solution.py:372
  97.1 0.0 all-to-all-done.2
  97.2 0.1 copy.10
  97.3 1.0 %reshape.23 = bf16[4,32,2048]{2,1,0:T(8,128)(2,1)} reshape(bf16[4,32,2,8,128]{4,3,2,1,0:T(8,128)(2,1)S(1)} %copy.10) | data formatting | bytes 1048576 | tf_op jit(solution)/shard_map/reshape | solution.py:439
Async XLA Ops:
  0.6 19.5 %copy-start.2 = (bf16[4,32,2048]{2,1,0:T(8,128)(2,1)S(1)}, bf16[4,32,2048]{2,1,0:T(8,128)(2,1)}, u32[]{:S(2)}) copy-start(bf16[4,32,2048]{2,1,0:T(8,128)(2,1)} %param.10) | copy-start | bytes 1572868
  2.4 8.9 %collective-permute-start.2 = (bf16[1,400,256]{2,1,0:T(8,128)(2,1)}, bf16[1,400,256]{2,1,0:T(8,128)(2,1)S(1)}, u32[]{:S(2)}, u32[]{:S(2)}) collective-permute-start(bf16[1,400,256]{2,1,0:T(8,128)(2,1)} %make_block.1.refs_0_), channel_id=1, source_target_pairs={{0,32},{32,64},{64,96},{1,33},{33,65},{65,97},{2,34},{34,66},{66,9... | collective-permute-start | bytes 614408 | tf_op jit(solution)/shard_map/ppermute | solution.py:396
  5.9 11.7 %collective-permute-start = (bf16[1,400,256]{2,1,0:T(8,128)(2,1)}, bf16[1,400,256]{2,1,0:T(8,128)(2,1)S(1)}, u32[]{:S(2)}, u32[]{:S(2)}) collective-permute-start(bf16[1,400,256]{2,1,0:T(8,128)(2,1)} %make_block.1.refs_0_), channel_id=1, source_target_pairs={{0,64},{32,96},{1,65},{33,97},{2,66},{34,98},{3,67},{35,99},{4,68}... | collective-permute-start | bytes 614408 | tf_op jit(solution)/shard_map/ppermute | solution.py:397
  12.2 17.1 %all-to-all-start.1 = ((bf16[4,400,256]{2,1,0:T(8,128)(2,1)}), bf16[4,400,256]{2,1,0:T(8,128)(2,1)S(1)}, u32[]{:S(2)}, u32[]{:S(2)}) async-start(bf16[4,400,256]{2,1,0:T(8,128)(2,1)} %broadcast_in_dim.17), calls=%async_computation.1 | async-start | bytes 1638400 | tf_op jit(solution)/shard_map/all_to_all | solution.py:398
  17.6 3.6 %copy-start.3 = (bf16[1,400,256]{2,1,0:T(8,128)(2,1)}, bf16[1,400,256]{2,1,0:T(8,128)(2,1)S(1)}, u32[]{:S(2)}) copy-start(bf16[1,400,256]{2,1,0:T(8,128)(2,1)S(1)} %collective-permute-done.refs_2_) | copy-start | bytes 614404
  18.6 8.7 %collective-permute-start.1 = (bf16[1,400,256]{2,1,0:T(8,128)(2,1)S(1)}, bf16[1,400,256]{2,1,0:T(8,128)(2,1)S(1)}, u32[]{:S(2)}, u32[]{:S(2)}) collective-permute-start(bf16[1,400,256]{2,1,0:T(8,128)(2,1)S(1)} %get-tuple-element.17), channel_id=1, source_target_pairs={{0,16},{16,0},{1,17},{17,1},{2,18},{18,2},{3,19},{19,3},{4,20},{20... | collective-permute-start | bytes 614408 | tf_op jit(solution)/shard_map/ppermute | solution.py:399
  27.3 2.0 %copy-start.4 = (bf16[1,400,256]{2,1,0:T(8,128)(2,1)}, bf16[1,400,256]{2,1,0:T(8,128)(2,1)S(1)}, u32[]{:S(2)}) copy-start(bf16[1,400,256]{2,1,0:T(8,128)(2,1)S(1)} %collective-permute-done.1.refs_3_) | copy-start | bytes 614404
  29.3 14.8 %copy-start.1 = (bf16[4,400,256]{2,1,0:T(8,128)(2,1)}, bf16[4,400,256]{2,1,0:T(8,128)(2,1)S(1)}, u32[]{:S(2)}) copy-start(bf16[4,400,256]{2,1,0:T(8,128)(2,1)S(1)} %all-to-all-done.1.refs_1_) | copy-start | bytes 2457604
  29.3 31.9 %all-to-all-start = ((bf16[32,80,128]{2,1,0:T(8,128)(2,1)}), bf16[32,80,128]{2,1,0:T(8,128)(2,1)S(1)}, u32[]{:S(2)}, u32[]{:S(2)}) async-start(bf16[32,80,128]{2,1,0:T(8,128)(2,1)} %decode_partials.1), calls=%async_computation | async-start | bytes 1310720 | tf_op jit(solution)/shard_map/all_to_all | solution.py:412
  38.7 34.8 %collective-permute-start.3 = (bf16[4,400,256]{2,1,0:T(8,128)(2,1)S(1)}, bf16[4,400,256]{2,1,0:T(8,128)(2,1)}, u32[]{:S(2)}, u32[]{:S(2)}) collective-permute-start(bf16[4,400,256]{2,1,0:T(8,128)(2,1)S(1)} %all-to-all-done.1.refs_1_), channel_id=1, source_target_pairs={{0,16},{16,0},{1,17},{17,1},{2,18},{18,2},{3,19},{19,3},{4,20},{20... | collective-permute-start | bytes 2457608 | tf_op jit(solution)/shard_map/ppermute | solution.py:405
  39.9 33.5 %collective-permute-start.4 = (bf16[2,400,256]{2,1,0:T(8,128)(2,1)S(1)}, bf16[2,400,256]{2,1,0:T(8,128)(2,1)}, u32[]{:S(2)}, u32[]{:S(2)}) collective-permute-start(bf16[2,400,256]{2,1,0:T(8,128)(2,1)S(1)} %get-tuple-element.11), channel_id=1, source_target_pairs={{0,8},{4,12},{8,0},{12,4},{1,9},{5,13},{9,1},{13,5},{2,10},{6,14},... | collective-permute-start | bytes 1228808 | tf_op jit(solution)/shard_map/ppermute | solution.py:408
  42.9 30.5 %collective-permute-start.6 = (bf16[2,400,256]{2,1,0:T(8,128)(2,1)S(1)}, bf16[2,400,256]{2,1,0:T(8,128)(2,1)}, u32[]{:S(2)}, u32[]{:S(2)}) collective-permute-start(bf16[2,400,256]{2,1,0:T(8,128)(2,1)S(1)} %get-tuple-element.11), channel_id=1, source_target_pairs={{0,12},{4,8},{8,4},{12,0},{1,13},{5,9},{9,5},{13,1},{2,14},{6,10},... | collective-permute-start | bytes 1228808 | tf_op jit(solution)/shard_map/ppermute | solution.py:408
  44.1 29.4 %collective-permute-start.5 = (bf16[2,400,256]{2,1,0:T(8,128)(2,1)}, bf16[2,400,256]{2,1,0:T(8,128)(2,1)}, u32[]{:S(2)}, u32[]{:S(2)}) collective-permute-start(bf16[2,400,256]{2,1,0:T(8,128)(2,1)} %get-tuple-element.12), channel_id=1, source_target_pairs={{0,4},{4,0},{8,12},{12,8},{1,5},{5,1},{9,13},{13,9},{2,6},{6,2},{1... | collective-permute-start | bytes 1228808 | tf_op jit(solution)/shard_map/ppermute | solution.py:408
  61.2 0.8 copy-start
  64.6 32.6 %all-to-all-start.2 = ((bf16[32,64,128]{2,1,0:T(8,128)(2,1)}), bf16[32,64,128]{2,1,0:T(8,128)(2,1)S(1)}, u32[]{:S(2)}, u32[]{:S(2)}) async-start(bf16[32,64,128]{2,1,0:T(8,128)(2,1)} %join_shares.1), calls=%async_computation.2 | async-start | bytes 1048576 | tf_op jit(solution)/shard_map/all_to_all | solution.py:425

commit v5 on v4

--- a/solution.py
+++ b/solution.py
@@ -52,6 +52,21 @@
     tile_row = lax.broadcasted_iota(jnp.int32, (16, HEAD_DIM), 0)
     tile_lane = lax.broadcasted_iota(jnp.int32, (16, HEAD_DIM), 1)
     pick = ((tile_row == tile_lane) & (tile_row < 4)).astype(jnp.bfloat16)
+    row = lax.broadcasted_iota(jnp.int32, (PER_SEQ, HEAD_DIM), 0)
+    second = lax.rem(row, HEADS) >= GROUP
+
+    def queries_of(i):
+        q = jnp.concatenate([q_ref[t, i] for t in range(STEPS)], axis=0)
+        none = jnp.zeros_like(q)
+        return jnp.concatenate([jnp.where(second, none, q), jnp.where(second, q, none)], axis=1)
+
+    def scores(i):
+        return jnp.where(
+            lane < len_ref[base + i] - me * SLOTS, dot(queries_of(i), kv_ref[0, i], NT) * TO_LOG2, HIDDEN
+        )
+
+    def own_head(o):
+        return jnp.where(second, o[:, HEAD_DIM:], o[:, :HEAD_DIM])
 
     def pack_stats(m_hi, m_lo, total):
         l_hi, l_lo = halves(total)
@@ -59,32 +74,14 @@
         st = jnp.where(at == 0, m_hi, jnp.where(at == 1, m_lo, jnp.where(at == 2, l_hi, l_lo)))
         return dot(pick, st.astype(jnp.bfloat16), NT)
 
-    def scores(i):
-        return jnp.concatenate(
-            [
-                dot(
-                    q_ref[i, h * PER_KV : (h + 1) * PER_KV, :],
-                    kv_ref[0, i, :, h * HEAD_DIM : (h + 1) * HEAD_DIM],
-                    NT,
-                )
-                for h in range(KV_HEADS)
-            ],
-            axis=0,
-        )
-
-    s = jnp.concatenate(
-        [jnp.where(lane < len_ref[base + i] - me * SLOTS, scores(i) * TO_LOG2, HIDDEN) for i in range(per_step)],
-        axis=0,
-    )
+    s = jnp.concatenate([scores(i) for i in range(per_step)], axis=0)
     m_hi, m_lo = halves(jnp.maximum(jnp.max(s, axis=1, keepdims=True), FLOOR))
     p = jnp.exp2(s - (m_hi + m_lo))
     tile = pack_stats(m_hi, m_lo, jnp.sum(p, axis=1, keepdims=True))
     p = p.astype(jnp.bfloat16)
     for i in range(per_step):
-        for h in range(KV_HEADS):
-            r = i * PER_SEQ + h * PER_KV
-            o = dot(p[r : r + PER_KV], kv_ref[1, i, :, h * HEAD_DIM : (h + 1) * HEAD_DIM], NN)
-            out_ref[i, h * PER_KV : (h + 1) * PER_KV, :] = o.astype(jnp.bfloat16)
+        o = dot(p[i * PER_SEQ : (i + 1) * PER_SEQ], kv_ref[1, i], NN)
+        out_ref[i, :PER_SEQ, :] = own_head(o).astype(jnp.bfloat16)
     for i in range(0, per_step, 2):
         pair = tile[:, i * PER_SEQ : (i + 2) * PER_SEQ]
         out_ref[i, PER_SEQ:, :] = pair.astype(jnp.bfloat16)
@@ -94,42 +91,26 @@
     @pl.when((me >= base) & (me < base + per_step))
     def _():
         i = me - base
-        row = lax.broadcasted_iota(jnp.int32, (16, KV_HEADS * HEAD_DIM), 0) == lax.rem(me, 16)
+        chosen = lax.broadcasted_iota(jnp.int32, (16, KV_HEADS * HEAD_DIM), 0) == lax.rem(me, 16)
 
         def fresh(kind):
             rows = [
-                jnp.sum(jnp.where(row, step_ref[t, kind].astype(jnp.float32), 0.0), axis=0, keepdims=True)
+                jnp.sum(jnp.where(chosen, step_ref[t, kind].astype(jnp.float32), 0.0), axis=0, keepdims=True)
                 for t in range(STEPS)
             ]
-            rows.append(jnp.zeros((16 - STEPS, KV_HEADS * HEAD_DIM), jnp.float32))
+            rows.append(jnp.zeros((HEAD_DIM - STEPS, KV_HEADS * HEAD_DIM), jnp.float32))
             return jnp.concatenate(rows, axis=0).astype(jnp.bfloat16)
 
-        keys, values = fresh(0), fresh(1)
-        t = lax.rem(lax.broadcasted_iota(jnp.int32, (PER_SEQ, 16), 0), PER_KV) // GROUP
-        sees = lax.broadcasted_iota(jnp.int32, (PER_SEQ, 16), 1) <= t
-        s = jnp.where(lane < len_ref[me] - me * SLOTS, scores(i) * TO_LOG2, HIDDEN)
-        f = jnp.concatenate(
-            [
-                dot(q_ref[i, h * PER_KV : (h + 1) * PER_KV, :], keys[:, h * HEAD_DIM : (h + 1) * HEAD_DIM], NT)
-                for h in range(KV_HEADS)
-            ],
-            axis=0,
-        )
-        f = jnp.where(sees, f * TO_LOG2, HIDDEN)
-        m_hi, m_lo = halves(
-            jnp.maximum(jnp.max(s, axis=1, keepdims=True), jnp.max(f, axis=1, keepdims=True))
-        )
+        s = scores(i)
+        f = jnp.where(lane <= row // HEADS, dot(queries_of(i), fresh(0), NT) * TO_LOG2, HIDDEN)
+        m_hi, m_lo = halves(jnp.maximum(jnp.max(s, axis=1, keepdims=True), jnp.max(f, axis=1, keepdims=True)))
         p = jnp.exp2(s - (m_hi + m_lo))
         pf = jnp.exp2(f - (m_hi + m_lo))
         total = jnp.sum(p, axis=1, keepdims=True) + jnp.sum(pf, axis=1, keepdims=True)
-        stats = [jnp.broadcast_to(x, (PER_SEQ, 1)) for x in (m_hi, m_lo, total)]
-        stats = [jnp.concatenate([x, jnp.zeros_like(x)], axis=0) for x in stats]
+        stats = [jnp.concatenate([x, jnp.zeros_like(x)], axis=0) for x in (m_hi, m_lo, total)]
         out_ref[i, PER_SEQ:, :] = pack_stats(*stats).astype(jnp.bfloat16)
-        p, pf = p.astype(jnp.bfloat16), pf.astype(jnp.bfloat16)
-        for h in range(KV_HEADS):
-            on, at = slice(h * PER_KV, (h + 1) * PER_KV), slice(h * HEAD_DIM, (h + 1) * HEAD_DIM)
-            o = dot(p[on], kv_ref[1, i, :, at], NN) + dot(pf[on], values[:, at], NN)
-            out_ref[i, on, :] = o.astype(jnp.bfloat16)
+        o = dot(p.astype(jnp.bfloat16), kv_ref[1, i], NN) + dot(pf.astype(jnp.bfloat16), fresh(1), NN)
+        out_ref[i, :PER_SEQ, :] = own_head(o).astype(jnp.bfloat16)
 
 
 def decode_partials(lens, me, queries, cache, fresh):
@@ -140,7 +121,7 @@
             num_scalar_prefetch=2,
             grid=(SEQS // per_step,),
             in_specs=[
-                pl.BlockSpec((per_step, PER_SEQ, HEAD_DIM), lambda i, *_: (i, 0, 0)),
+                pl.BlockSpec((STEPS, per_step, HEADS, HEAD_DIM), lambda i, *_: (0, i, 0, 0)),
                 pl.BlockSpec((2, per_step, SLOTS, KV_HEADS * HEAD_DIM), lambda i, *_: (0, i, 0, 0)),
                 pl.BlockSpec((STEPS, 2, 16, KV_HEADS * HEAD_DIM), lambda i, lens, me: (0, 0, me[0] // 16, 0)),
             ],
@@ -225,7 +206,7 @@
 COUNT = {"own": 1, "row": 4, "back": 1, "across": 1, 1: 2, 2: 2, 3: 2}
 
 
-def prefill_kernel(at_ref, doc_ref, q_ref, *refs, sources, groups, first, last):
+def prefill_kernel(me_ref, doc_ref, q_ref, *refs, sources, order, groups, first, last):
     blocks, rest = refs[: len(sources)], refs[len(sources) :]
     state_in = None
     if not first:
@@ -237,13 +218,14 @@
         state = out_ref.at[0]
     keys_ref, values_ref, queries_ref, low_ref, flag_ref = rest
     step = pl.program_id(0)
-    y, xh, z = at_ref[0], at_ref[1], at_ref[2]
+    y, xh, z = me_ref[0] // 8, lax.rem(me_ref[0] // 4, 2), lax.rem(me_ref[0], 4)
     counts = [COUNT[source] for source in sources]
-    places = [(r, b) for r, n in enumerate(counts) for b in range(n)]
-    n = len(places)
+    places = [(r, b) for r, c in enumerate(counts) for b in range(c)]
     valid = []
     for source in sources:
         valid += block_valid(y, xh, z, source)
+    places, valid = [places[i] for i in order], [valid[i] for i in order]
+    n = len(places)
 
     @pl.when(step == 0)
     def _():
@@ -257,8 +239,9 @@
             lows.append(low)
         for g, (lo, hi) in enumerate(groups):
             some = jnp.min(functools.reduce(jnp.minimum, lows[lo:hi])) < ROWS
-            whole = jnp.max(functools.reduce(jnp.maximum, lows[lo:hi])) == 0
-            flag_ref[g] = jnp.where(some, jnp.where(whole, 1, 2), 0)
+            inside = [jnp.where((low > 0) & (low < ROWS), 1, 0) for low in lows[lo:hi]]
+            inside = jnp.max(functools.reduce(jnp.maximum, inside)) > 0
+            flag_ref[g] = jnp.where(some, jnp.where(inside, 2, 1), 0)
 
     @pl.when(lax.rem(step, max(HEADS // FUSED // KV_HEADS, 1)) == 0)
     def _():
@@ -301,7 +284,16 @@
 
     def add(lo, hi, masked):
         about = state[HEAD_DIM : HEAD_DIM + 1, :] * TO_LOG2
-        p = jnp.exp2(scores(lo, hi, masked) * TO_LOG2 - about)
+        s = scores(lo, hi, masked) * TO_LOG2
+        if masked:
+            s = s - about
+        else:
+            parts = []
+            for at in range(lo, hi):
+                part = s[(at - lo) * ROWS : (at - lo + 1) * ROWS]
+                parts.append(part - jnp.where(low_ref[at, 0:1, :] < ROWS, about, -HIDDEN))
+            s = jnp.concatenate(parts, axis=0)
+        p = jnp.exp2(s)
         state[HEAD_DIM + 8 :, :] = state[HEAD_DIM + 8 :, :] + jnp.sum(p, axis=0, keepdims=True)
         state[0:HEAD_DIM, :] = state[0:HEAD_DIM, :] + weighted(lo, hi, p)
 
@@ -337,7 +329,7 @@
             out_ref[:, j * HEAD_DIM : (j + 1) * HEAD_DIM] = out[j * ROWS : (j + 1) * ROWS]
 
 
-def prefill_part(at, doc, queries, blocks, sources, groups, state, last, name):
+def prefill_part(me, doc, queries, blocks, sources, order, groups, state, last, name):
     first = state is None
     counts = [COUNT[source] for source in sources]
     n = sum(counts)
@@ -350,7 +342,7 @@
         q_spec,
     ]
     in_specs += [pl.BlockSpec((c, BLOCK, HEAD_DIM), lambda i, *_: (0, 0, i // per_kv)) for c in counts]
-    operands = [at, doc, queries, *blocks]
+    operands = [me, doc, queries, *blocks]
     scratch = []
     if not first:
         in_specs.append(state_spec)
@@ -370,7 +362,7 @@
         pltpu.SMEM((len(groups),), jnp.int32),
     ]
     return pl.pallas_call(
-        functools.partial(prefill_kernel, sources=sources, groups=groups, first=first, last=last),
+        functools.partial(prefill_kernel, sources=sources, order=order, groups=groups, first=first, last=last),
         grid_spec=pltpu.PrefetchScalarGridSpec(
             num_scalar_prefetch=1,
             grid=(steps,),
@@ -398,8 +390,7 @@
     row = lax.all_to_all(jnp.broadcast_to(back1, (4,) + back1.shape[1:]), "z", 0, 0)
     across = lax.ppermute(jnp.where(xh == 0, own, back2), "xh", [(0, 1), (1, 0)])
 
-    queries = decode_queries.reshape(STEPS, SEQS, KV_HEADS, GROUP, HEAD_DIM)
-    queries = queries.transpose(1, 2, 0, 3, 4).reshape(SEQS, PER_SEQ, HEAD_DIM)
+    queries = decode_queries.reshape(STEPS, SEQS, HEADS, HEAD_DIM)
     shares = decode_partials(cached_len, me[None], queries, stored_key_values, step_key_values)
 
     far_row = lax.ppermute(row, "xh", [(0, 1), (1, 0)])
@@ -407,15 +398,16 @@
     packs, shares = lax.optimization_barrier((packs, shares))
     side = {k: lax.ppermute(packs[min(k, 2)], "z", [(i, i ^ k) for i in range(4)]) for k in SIDE}
 
-    at, doc = jnp.stack([y, xh, z]), fill_doc[None]
+    doc = fill_doc[None]
 
     shares = lax.all_to_all(shares, CTX, 0, 0)
     state = prefill_part(
-        at,
+        me[None],
         doc,
         prefill_queries,
         [own, row, back2, across],
         ("own", "row", "back", "across"),
+        tuple(range(7)),
         ((1, 5), (5, 7)),
         None,
         False,
@@ -424,18 +416,19 @@
     shares, state = lax.optimization_barrier((shares, state))
     spread = lax.all_to_all(join_shares(shares), CTX, 0, 0)
     fill_out = prefill_part(
-        at,
+        me[None],
         doc,
         prefill_queries,
         [far_row] + [side[k] for k in SIDE],
         ("row",) + SIDE,
+        (0, 1, 2, 3, 5, 7, 9, 4, 6, 8),
         ((0, 4), (4, 7), (7, 10)),
         state,
         True,
         "prefill_last",
     )
     spread, fill_out = lax.optimization_barrier((spread, fill_out))
-    step_out = spread.reshape(SEQS, KV_HEADS, STEPS, GROUP, HEAD_DIM).transpose(2, 0, 1, 3, 4)
+    step_out = spread.reshape(SEQS, STEPS, HEADS, HEAD_DIM).transpose(1, 0, 2, 3)
     return fill_out, step_out.reshape(STEPS, SEQS, HEADS * HEAD_DIM)
 
 

time: 100 us -> 94.6 us (0.946)
  the two profiles are of different devices: /device:TPU:14 before, /device:TPU:46 now
where the time goes in v5:
time: 94.6 us; the launch traced here: 95.2 us
  Pallas kernels  47.1 us (50%)
  starting transfers between devices  37.8 us (40%)
  local copies, waits for them, and re-layouts  3.89 us (4%)
  waiting for transfers between devices  3.77 us (4%)
  other arithmetic  1.88 us (2%)
    pallas_call x2, Pallas kernels, prefill_part(): pl.pallas_call(functools.partial(prefill_kernel, sources=sources, order=o...  37.2 us
    all_to_all x1, starting transfers between devices, local(): spread = lax.all_to_all(join_shares(shares), CTX, 0, 0)  10.5 us
    all_to_all x1, starting transfers between devices, local(): shares = lax.all_to_all(shares, CTX, 0, 0)  9.55 us
    pallas_call x1, Pallas kernels, decode_partials(): pl.pallas_call(functools.partial(decode_kernel, per_step=per_step), grid_...  5.67 us
    all_to_all x1, starting transfers between devices, local(): lax.all_to_all(jnp.broadcast_to(back1, (4,) + back1.shape[1:]), 'z', 0, 0)  5.41 us
    ppermute x3, starting transfers between devices, local(): lax.ppermute(packs[min(k, 2)], 'z', [(i, i ^ k) for i in range(4)])  4.7 us
    ppermute x1, starting transfers between devices, local(): back1 = lax.ppermute(own, 'y', [(i, i + 1) for i in range(3)])  3.47 us
    ppermute x1, waiting for transfers between devices, local(): back1 = lax.ppermute(own, 'y', [(i, i + 1) for i in range(3)])  3.4 us
  transfers between devices with their start and end apart: 10, of which 2 were waited for; matrix products, arithmetic and copies ran while one was open for 4% of the time, Pallas kernels for 48%

profile of v5, /device:TPU:46, one launch (start us, length us, event | category | flops | bytes accessed | tf_op | source)
XLA Modules:
  0.0 95.2 jit_solution(951071375873379708)
XLA Ops:
  0.6 0.0 copy-start.2
  0.6 1.8 %make_block.1.refs_0_ = bf16[1,400,256]{2,1,0:T(8,128)(2,1)} custom-call(s32[1,192]{1,0:T(1,128)} %bitcast.20, bf16[384,256]{1,0:T(8,128)(2,1)} %bitcast.19), custom_call_target="tpu_custom_call" | custom-call | flops 1000 | bytes 400000 | tf_op jit(solution)/shard_map/make_block/pallas_call | solution.py:182
  2.4 3.5 %collective-permute-start.2 = (bf16[1,400,256]{2,1,0:T(8,128)(2,1)}, bf16[1,400,256]{2,1,0:T(8,128)(2,1)S(1)}, u32[]{:S(2)}, u32[]{:S(2)}) collective-permute-start(bf16[1,400,256]{2,1,0:T(8,128)(2,1)} %make_block.1.refs_0_), channel_id=1, source_target_pairs={{0,32},{32,64},{64,96},{1,33},{33,65},{65,97},{2,34},{34,66},{66,9... | collective-permute-start | bytes 614408 | tf_op jit(solution)/shard_map/ppermute | solution.py:388
  5.9 2.0 %collective-permute-start = (bf16[1,400,256]{2,1,0:T(8,128)(2,1)}, bf16[1,400,256]{2,1,0:T(8,128)(2,1)S(1)}, u32[]{:S(2)}, u32[]{:S(2)}) collective-permute-start(bf16[1,400,256]{2,1,0:T(8,128)(2,1)} %make_block.1.refs_0_), channel_id=1, source_target_pairs={{0,64},{32,96},{1,65},{33,97},{2,66},{34,98},{3,67},{35,99},{4,68}... | collective-permute-start | bytes 614408 | tf_op jit(solution)/shard_map/ppermute | solution.py:389
  7.9 3.4 %collective-permute-done.2 = bf16[1,400,256]{2,1,0:T(8,128)(2,1)S(1)} collective-permute-done((bf16[1,400,256]{2,1,0:T(8,128)(2,1)}, bf16[1,400,256]{2,1,0:T(8,128)(2,1)S(1)}, u32[]{:S(2)}, u32[]{:S(2)}) %collective-permute-start.2) | collective-permute-done | bytes 204832 | tf_op jit(solution)/shard_map/ppermute | solution.py:388
  11.3 0.9 broadcast_in_dim.19
  12.2 5.4 %all-to-all-start.1 = ((bf16[4,400,256]{2,1,0:T(8,128)(2,1)}), bf16[4,400,256]{2,1,0:T(8,128)(2,1)S(1)}, u32[]{:S(2)}, u32[]{:S(2)}) async-start(bf16[4,400,256]{2,1,0:T(8,128)(2,1)} %broadcast_in_dim.19), calls=%async_computation.1 | async-start | bytes 1638400 | tf_op jit(solution)/shard_map/all_to_all | solution.py:390
  17.7 0.0 collective-permute-done.refs_2_
  17.7 0.0 copy-start.3
  17.7 1.1 %broadcast_select_fusion = (bf16[1,400,256]{2,1,0:T(8,128)(2,1)S(1)}, bf16[1,400,256]{2,1,0:T(8,128)(2,1)S(1)}, bf16[1,400,256]{2,1,0:T(8,128)(2,1)S(1)}) fusion(bf16[1,400,256]{2,1,0:T(8,128)(2,1)} %make_block.1.refs_0_, bf16[1,400,256]{2,1,0:T(8,128)(2,1)S(1)} %collective-permute-done.refs_2_, pred[]{:T(512)S(6)} %eq.11, pred[]{:T(512)S(6)} %eq.10, pred[]{:T(512)S(6)} %eq.9), kind=kLoop, calls=%fused_computation.2 | loop fusion | flops 307200 | bytes 1024003 | tf_op jit(solution)/shard_map/jit(_where)/select_n | solution.py:397
  18.7 1.5 %collective-permute-start.1 = (bf16[1,400,256]{2,1,0:T(8,128)(2,1)S(1)}, bf16[1,400,256]{2,1,0:T(8,128)(2,1)S(1)}, u32[]{:S(2)}, u32[]{:S(2)}) collective-permute-start(bf16[1,400,256]{2,1,0:T(8,128)(2,1)S(1)} %get-tuple-element.17), channel_id=1, source_target_pairs={{0,16},{16,0},{1,17},{17,1},{2,18},{18,2},{3,19},{19,3},{4,20},{20... | collective-permute-start | bytes 614408 | tf_op jit(solution)/shard_map/ppermute | solution.py:391
  20.2 0.0 copy-done.2
  20.2 0.9 copy.11
  21.1 0.0 copy-done.3
  21.1 5.7 %decode_partials.1 = bf16[32,80,128]{2,1,0:T(8,128)(2,1)} custom-call(s32[32]{0:T(128)} %len_ref.1, s32[1]{0:T(128)} %bitcast.2.me_ref, bf16[4,32,16,128]{3,2,1,0:T(8,128)(2,1)} %bitcast.15, bf16[2,32,128,256]{3,2,1,0:T(8,128)(2,1)} %kv_ref.1, bf16[4,2,32,256]{3,2,1,0:T(8,128)(2,1)} %step_ref.1), custom_call_target="tpu_custom_call" | custom-call | flops 70000000 | bytes 5500000 | tf_op jit(solution)/shard_map/decode_partials/pallas_call | solution.py:118
  26.8 0.0 collective-permute-done.1.refs_3_
  26.8 0.0 copy-start.4
  26.8 0.8 pad_maximum_fusion
  27.6 0.3 all-to-all-done.1.refs_1_
  28.0 0.0 copy-start.1
  28.0 0.0 copy-done.4
  28.0 9.6 %all-to-all-start = ((bf16[32,80,128]{2,1,0:T(8,128)(2,1)}), bf16[32,80,128]{2,1,0:T(8,128)(2,1)S(1)}, u32[]{:S(2)}, u32[]{:S(2)}) async-start(bf16[32,80,128]{2,1,0:T(8,128)(2,1)} %decode_partials.1), calls=%async_computation | async-start | bytes 1310720 | tf_op jit(solution)/shard_map/all_to_all | solution.py:403
  37.5 0.6 collective-permute-start.3
  38.2 2.1 %collective-permute-start.4 = (bf16[2,400,256]{2,1,0:T(8,128)(2,1)S(1)}, bf16[2,400,256]{2,1,0:T(8,128)(2,1)}, u32[]{:S(2)}, u32[]{:S(2)}) collective-permute-start(bf16[2,400,256]{2,1,0:T(8,128)(2,1)S(1)} %get-tuple-element.11), channel_id=1, source_target_pairs={{0,8},{4,12},{8,0},{12,4},{1,9},{5,13},{9,1},{13,5},{2,10},{6,14},... | collective-permute-start | bytes 1228808 | tf_op jit(solution)/shard_map/ppermute | solution.py:399
  40.2 0.0 collective-permute-start.6
  40.2 2.6 %collective-permute-start.5 = (bf16[2,400,256]{2,1,0:T(8,128)(2,1)}, bf16[2,400,256]{2,1,0:T(8,128)(2,1)}, u32[]{:S(2)}, u32[]{:S(2)}) collective-permute-start(bf16[2,400,256]{2,1,0:T(8,128)(2,1)} %get-tuple-element.12), channel_id=1, source_target_pairs={{0,4},{4,0},{8,12},{12,8},{1,5},{5,1},{9,13},{13,9},{2,6},{6,2},{1... | collective-permute-start | bytes 1228808 | tf_op jit(solution)/shard_map/ppermute | solution.py:399
  42.9 0.0 copy-done.1
  42.9 15.9 %prefill_first.1.refs_4_ = f32[2,144,1536]{2,1,0:T(8,128)} custom-call(s32[1]{0:T(128)} %bitcast.2.me_ref, s32[1,192]{1,0:T(1,128)} %bitcast.21, bf16[192,2048]{1,0:T(8,128)(2,1)} %q_ref.3, bf16[1,400,256]{2,1,0:T(8,128)(2,1)} %make_block.1.refs_0_, bf16[4,400,256]{2,1,0:T(8,128)(2,1)} %copy-done.1, bf16[1,400,256]{2,1,0:T(8,128)(2,1)} %copy-done.3, ...), custom_call_target="tpu_custom_call" | custom-call | flops 2113929216 | bytes 4000000 | tf_op jit(solution)/shard_map/prefill_first/pallas_call | solution.py:364
  58.8 0.0 all-to-all-done.in_ref
  58.8 0.0 copy-start
  58.8 0.8 copy-done
  59.6 2.5 %join_shares.1 = bf16[32,64,128]{2,1,0:T(8,128)(2,1)} custom-call(bf16[32,80,128]{2,1,0:T(8,128)(2,1)} %copy-done), custom_call_target="tpu_custom_call" | custom-call | flops 1000000 | bytes 1200000 | tf_op jit(solution)/shard_map/join_shares/pallas_call | solution.py:159
  62.2 10.5 %all-to-all-start.2 = ((bf16[32,64,128]{2,1,0:T(8,128)(2,1)}), bf16[32,64,128]{2,1,0:T(8,128)(2,1)S(1)}, u32[]{:S(2)}, u32[]{:S(2)}) async-start(bf16[32,64,128]{2,1,0:T(8,128)(2,1)} %join_shares.1), calls=%async_computation.2 | async-start | bytes 1048576 | tf_op jit(solution)/shard_map/all_to_all | solution.py:417
  72.7 0.0 collective-permute-done.4.refs_1_
  72.7 0.0 collective-permute-done.5.refs_2_
  72.7 0.0 collective-permute-done.6.refs_3_
  72.7 0.0 collective-permute-done.3.refs_0_
  72.8 21.3 %prefill_last.1 = bf16[192,2048]{1,0:T(8,128)(2,1)} custom-call(s32[1]{0:T(128)} %bitcast.2.me_ref, s32[1,192]{1,0:T(1,128)} %bitcast.22, bf16[192,2048]{1,0:T(8,128)(2,1)} %q_ref.3, bf16[4,400,256]{2,1,0:T(8,128)(2,1)} %collective-permute-done.3.refs_0_, bf16[2,400,256]{2,1,0:T(8,128)(2,1)} %collective-permute-done.4.refs_1_, ...), custom_call_target="tpu_custom_call" | custom-call | flops 3019898880 | bytes 4000000 | tf_op jit(solution)/shard_map/prefill_last/pallas_call | solution.py:364
  94.0 0.0 all-to-all-done.2
  94.0 0.1 reshape.20
  94.1 1.1 %copy.10 = bf16[4,32,2048]{2,1,0:T(8,128)(2,1)} copy(bf16[4,32,2048]{2,0,1:T(4,128)(2,1)S(1)} %reshape.20) | data formatting | bytes 1048576 | tf_op jit(solution)/shard_map/reshape | solution.py:432
Async XLA Ops:
  0.6 19.6 %copy-start.2 = (bf16[4,32,2048]{2,1,0:T(8,128)(2,1)S(1)}, bf16[4,32,2048]{2,1,0:T(8,128)(2,1)}, u32[]{:S(2)}) copy-start(bf16[4,32,2048]{2,1,0:T(8,128)(2,1)} %param.10) | copy-start | bytes 1572868
  2.4 8.9 %collective-permute-start.2 = (bf16[1,400,256]{2,1,0:T(8,128)(2,1)}, bf16[1,400,256]{2,1,0:T(8,128)(2,1)S(1)}, u32[]{:S(2)}, u32[]{:S(2)}) collective-permute-start(bf16[1,400,256]{2,1,0:T(8,128)(2,1)} %make_block.1.refs_0_), channel_id=1, source_target_pairs={{0,32},{32,64},{64,96},{1,33},{33,65},{65,97},{2,34},{34,66},{66,9... | collective-permute-start | bytes 614408 | tf_op jit(solution)/shard_map/ppermute | solution.py:388
  5.9 11.8 %collective-permute-start = (bf16[1,400,256]{2,1,0:T(8,128)(2,1)}, bf16[1,400,256]{2,1,0:T(8,128)(2,1)S(1)}, u32[]{:S(2)}, u32[]{:S(2)}) collective-permute-start(bf16[1,400,256]{2,1,0:T(8,128)(2,1)} %make_block.1.refs_0_), channel_id=1, source_target_pairs={{0,64},{32,96},{1,65},{33,97},{2,66},{34,98},{3,67},{35,99},{4,68}... | collective-permute-start | bytes 614408 | tf_op jit(solution)/shard_map/ppermute | solution.py:389
  12.2 15.7 %all-to-all-start.1 = ((bf16[4,400,256]{2,1,0:T(8,128)(2,1)}), bf16[4,400,256]{2,1,0:T(8,128)(2,1)S(1)}, u32[]{:S(2)}, u32[]{:S(2)}) async-start(bf16[4,400,256]{2,1,0:T(8,128)(2,1)} %broadcast_in_dim.19), calls=%async_computation.1 | async-start | bytes 1638400 | tf_op jit(solution)/shard_map/all_to_all | solution.py:390
  17.7 3.4 %copy-start.3 = (bf16[1,400,256]{2,1,0:T(8,128)(2,1)}, bf16[1,400,256]{2,1,0:T(8,128)(2,1)S(1)}, u32[]{:S(2)}) copy-start(bf16[1,400,256]{2,1,0:T(8,128)(2,1)S(1)} %collective-permute-done.refs_2_) | copy-start | bytes 614404
  18.7 8.1 %collective-permute-start.1 = (bf16[1,400,256]{2,1,0:T(8,128)(2,1)S(1)}, bf16[1,400,256]{2,1,0:T(8,128)(2,1)S(1)}, u32[]{:S(2)}, u32[]{:S(2)}) collective-permute-start(bf16[1,400,256]{2,1,0:T(8,128)(2,1)S(1)} %get-tuple-element.17), channel_id=1, source_target_pairs={{0,16},{16,0},{1,17},{17,1},{2,18},{18,2},{3,19},{19,3},{4,20},{20... | collective-permute-start | bytes 614408 | tf_op jit(solution)/shard_map/ppermute | solution.py:391
  26.8 1.2 %copy-start.4 = (bf16[1,400,256]{2,1,0:T(8,128)(2,1)}, bf16[1,400,256]{2,1,0:T(8,128)(2,1)S(1)}, u32[]{:S(2)}) copy-start(bf16[1,400,256]{2,1,0:T(8,128)(2,1)S(1)} %collective-permute-done.1.refs_3_) | copy-start | bytes 614404
  28.0 14.9 %copy-start.1 = (bf16[4,400,256]{2,1,0:T(8,128)(2,1)}, bf16[4,400,256]{2,1,0:T(8,128)(2,1)S(1)}, u32[]{:S(2)}) copy-start(bf16[4,400,256]{2,1,0:T(8,128)(2,1)S(1)} %all-to-all-done.1.refs_1_) | copy-start | bytes 2457604
  28.0 30.8 %all-to-all-start = ((bf16[32,80,128]{2,1,0:T(8,128)(2,1)}), bf16[32,80,128]{2,1,0:T(8,128)(2,1)S(1)}, u32[]{:S(2)}, u32[]{:S(2)}) async-start(bf16[32,80,128]{2,1,0:T(8,128)(2,1)} %decode_partials.1), calls=%async_computation | async-start | bytes 1310720 | tf_op jit(solution)/shard_map/all_to_all | solution.py:403
  37.5 35.2 %collective-permute-start.3 = (bf16[4,400,256]{2,1,0:T(8,128)(2,1)S(1)}, bf16[4,400,256]{2,1,0:T(8,128)(2,1)}, u32[]{:S(2)}, u32[]{:S(2)}) collective-permute-start(bf16[4,400,256]{2,1,0:T(8,128)(2,1)S(1)} %all-to-all-done.1.refs_1_), channel_id=1, source_target_pairs={{0,16},{16,0},{1,17},{17,1},{2,18},{18,2},{3,19},{19,3},{4,20},{20... | collective-permute-start | bytes 2457608 | tf_op jit(solution)/shard_map/ppermute | solution.py:396
  38.2 34.5 %collective-permute-start.4 = (bf16[2,400,256]{2,1,0:T(8,128)(2,1)S(1)}, bf16[2,400,256]{2,1,0:T(8,128)(2,1)}, u32[]{:S(2)}, u32[]{:S(2)}) collective-permute-start(bf16[2,400,256]{2,1,0:T(8,128)(2,1)S(1)} %get-tuple-element.11), channel_id=1, source_target_pairs={{0,8},{4,12},{8,0},{12,4},{1,9},{5,13},{9,1},{13,5},{2,10},{6,14},... | collective-permute-start | bytes 1228808 | tf_op jit(solution)/shard_map/ppermute | solution.py:399
  40.2 32.5 %collective-permute-start.6 = (bf16[2,400,256]{2,1,0:T(8,128)(2,1)S(1)}, bf16[2,400,256]{2,1,0:T(8,128)(2,1)}, u32[]{:S(2)}, u32[]{:S(2)}) collective-permute-start(bf16[2,400,256]{2,1,0:T(8,128)(2,1)S(1)} %get-tuple-element.11), channel_id=1, source_target_pairs={{0,12},{4,8},{8,4},{12,0},{1,13},{5,9},{9,5},{13,1},{2,14},{6,10},... | collective-permute-start | bytes 1228808 | tf_op jit(solution)/shard_map/ppermute | solution.py:399
  40.2 32.5 %collective-permute-start.5 = (bf16[2,400,256]{2,1,0:T(8,128)(2,1)}, bf16[2,400,256]{2,1,0:T(8,128)(2,1)}, u32[]{:S(2)}, u32[]{:S(2)}) collective-permute-start(bf16[2,400,256]{2,1,0:T(8,128)(2,1)} %get-tuple-element.12), channel_id=1, source_target_pairs={{0,4},{4,0},{8,12},{12,8},{1,5},{5,1},{9,13},{13,9},{2,6},{6,2},{1... | collective-permute-start | bytes 1228808 | tf_op jit(solution)/shard_map/ppermute | solution.py:399
  58.8 0.8 copy-start
  62.2 31.8 %all-to-all-start.2 = ((bf16[32,64,128]{2,1,0:T(8,128)(2,1)}), bf16[32,64,128]{2,1,0:T(8,128)(2,1)S(1)}, u32[]{:S(2)}, u32[]{:S(2)}) async-start(bf16[32,64,128]{2,1,0:T(8,128)(2,1)} %join_shares.1), calls=%async_computation.2 | async-start | bytes 1048576 | tf_op jit(solution)/shard_map/all_to_all | solution.py:417

commit v6 on v5

--- a/solution.py
+++ b/solution.py
@@ -27,6 +27,7 @@
 FLOOR = -1e20
 NOWHERE = -1000000
 TOO_LARGE = 2.0**100
+HIDDEN_KEY = 4
 TO_LOG2 = HEAD_DIM**-0.5 * 1.4426950408889634
 CTX = ("y", "xh", "z")
 PLANE = ("xh", "z")
@@ -194,6 +195,8 @@
     if kind == "own":
         return [y >= 0]
     if kind == "row":
+        return [y >= 1]
+    if kind == "far_row":
         return [y >= 1] * 4
     if kind == "back":
         return [y >= 2]
@@ -203,10 +206,10 @@
     return [((z & bit) != 0) | (y >= 2), across]
 
 
-COUNT = {"own": 1, "row": 4, "back": 1, "across": 1, 1: 2, 2: 2, 3: 2}
-
-
-def prefill_kernel(me_ref, doc_ref, q_ref, *refs, sources, order, groups, first, last):
+COUNT = {"own": 1, "row": 1, "far_row": 4, "back": 1, "across": 1, 1: 2, 2: 2, 3: 2}
+
+
+def prefill_kernel(me_ref, q_ref, own_info_ref, *refs, sources, first, last):
     blocks, rest = refs[: len(sources)], refs[len(sources) :]
     state_in = None
     if not first:
@@ -216,55 +219,46 @@
         state, rest = rest[0], rest[1:]
     else:
         state = out_ref.at[0]
-    keys_ref, values_ref, queries_ref, low_ref, flag_ref = rest
+    keys_ref, values_ref, queries_ref = rest
     step = pl.program_id(0)
     y, xh, z = me_ref[0] // 8, lax.rem(me_ref[0] // 4, 2), lax.rem(me_ref[0], 4)
-    counts = [COUNT[source] for source in sources]
-    places = [(r, b) for r, c in enumerate(counts) for b in range(c)]
-    valid = []
-    for source in sources:
-        valid += block_valid(y, xh, z, source)
-    places, valid = [places[i] for i in order], [valid[i] for i in order]
+    places = [(r, b) for r, source in enumerate(sources) for b in range(COUNT[source])]
     n = len(places)
 
     @pl.when(step == 0)
     def _():
-        doc = doc_ref[...]
-        lows = []
+        row = lax.broadcasted_iota(jnp.int32, (ROWS, HEAD_DIM), 0)
+        lane = lax.broadcasted_iota(jnp.int32, (ROWS, HEAD_DIM), 1)
+
+        def documents(info):
+            t = info.astype(jnp.float32)[0:1, :].astype(jnp.int32)
+            return sum((row >= t[:, d : d + 1]).astype(jnp.int32) for d in range(3))
+
+        valid = []
+        for source in sources:
+            valid += block_valid(y, xh, z, source)
         for at, (r, b) in enumerate(places):
-            t = blocks[r][b, 2 * ROWS :, :].astype(jnp.float32)[0:1, :].astype(jnp.int32)
-            low = jnp.where(doc == 1, t[:, 0:1], jnp.where(doc == 2, t[:, 1:2], jnp.where(doc == 3, t[:, 2:3], 0)))
-            low = jnp.where(valid[at], low, ROWS)
-            low_ref[at, 0:1, :] = jnp.concatenate([low] * FUSED, axis=1)
-            lows.append(low)
-        for g, (lo, hi) in enumerate(groups):
-            some = jnp.min(functools.reduce(jnp.minimum, lows[lo:hi])) < ROWS
-            inside = [jnp.where((low > 0) & (low < ROWS), 1, 0) for low in lows[lo:hi]]
-            inside = jnp.max(functools.reduce(jnp.maximum, inside)) > 0
-            flag_ref[g] = jnp.where(some, jnp.where(inside, 2, 1), 0)
-
-    @pl.when(lax.rem(step, max(HEADS // FUSED // KV_HEADS, 1)) == 0)
-    def _():
-        for at, (r, b) in enumerate(places):
-            on = slice(at * ROWS, (at + 1) * ROWS)
-            keys_ref[on, :] = blocks[r][b, 0:ROWS, :]
-            values_ref[on, :] = blocks[r][b, ROWS : 2 * ROWS, :]
-
+            doc = jnp.where(valid[at], documents(blocks[r][b, 2 * ROWS :, :]), HIDDEN_KEY)
+            keys_ref[at * ROWS : (at + 1) * ROWS, HEAD_DIM:] = (lane == doc).astype(jnp.bfloat16)
+        other = (lane <= HIDDEN_KEY) & (lane != documents(own_info_ref[0]))
+        other = jnp.where(other, HIDDEN, 0.0).astype(jnp.bfloat16)
+        for j in range(FUSED):
+            queries_ref[j * ROWS : (j + 1) * ROWS, HEAD_DIM:] = other
+
+    for at, (r, b) in enumerate(places):
+        on = slice(at * ROWS, (at + 1) * ROWS)
+        keys_ref[on, :HEAD_DIM] = blocks[r][b, 0:ROWS, :]
+        values_ref[on, :] = blocks[r][b, ROWS : 2 * ROWS, :]
     for j in range(FUSED):
-        queries_ref[j * ROWS : (j + 1) * ROWS, :] = q_ref[:, j * HEAD_DIM : (j + 1) * HEAD_DIM]
-
-    def scores(lo, hi, masked):
-        s = dot(keys_ref[lo * ROWS : hi * ROWS, :], queries_ref[...], NT)
-        if not masked:
-            return s
-        row = lax.broadcasted_iota(jnp.int32, (ROWS, LANES), 0)
-        parts = []
-        for at in range(lo, hi):
-            sees = row >= low_ref[at, 0:1, :]
-            if first and at == 0:
-                sees = sees & (row <= lax.rem(lax.broadcasted_iota(jnp.int32, (1, LANES), 1), ROWS))
-            parts.append(jnp.where(sees, s[(at - lo) * ROWS : (at - lo + 1) * ROWS], HIDDEN))
-        return jnp.concatenate(parts, axis=0)
+        queries_ref[j * ROWS : (j + 1) * ROWS, :HEAD_DIM] = q_ref[:, j * HEAD_DIM : (j + 1) * HEAD_DIM]
+
+    def scores(lo, hi):
+        return dot(keys_ref[lo * ROWS : hi * ROWS, :], queries_ref[...], NT)
+
+    def own_scores():
+        key = lax.broadcasted_iota(jnp.int32, (ROWS, LANES), 0)
+        query = lax.rem(lax.broadcasted_iota(jnp.int32, (1, LANES), 1), ROWS)
+        return jnp.where(key <= query, scores(0, 1), HIDDEN)
 
     def weighted(lo, hi, p):
         return dot(values_ref[lo * ROWS : hi * ROWS, :], p.astype(jnp.bfloat16), TN)
@@ -275,41 +269,24 @@
         state[HEAD_DIM + 8 :, :] = jnp.broadcast_to(total, (8, LANES))
 
     if first:
-        s = scores(0, 1, True)
+        s = own_scores()
         peak = jnp.max(s, axis=0, keepdims=True)
         p = jnp.exp2((s - peak) * TO_LOG2)
-        put(peak, jnp.sum(p, axis=0, keepdims=True), weighted(0, 1, p))
+        total, summed = jnp.sum(p, axis=0, keepdims=True), weighted(0, 1, p)
     else:
-        state[...] = state_in[0]
-
-    def add(lo, hi, masked):
-        about = state[HEAD_DIM : HEAD_DIM + 1, :] * TO_LOG2
-        s = scores(lo, hi, masked) * TO_LOG2
-        if masked:
-            s = s - about
-        else:
-            parts = []
-            for at in range(lo, hi):
-                part = s[(at - lo) * ROWS : (at - lo + 1) * ROWS]
-                parts.append(part - jnp.where(low_ref[at, 0:1, :] < ROWS, about, -HIDDEN))
-            s = jnp.concatenate(parts, axis=0)
-        p = jnp.exp2(s)
-        state[HEAD_DIM + 8 :, :] = state[HEAD_DIM + 8 :, :] + jnp.sum(p, axis=0, keepdims=True)
-        state[0:HEAD_DIM, :] = state[0:HEAD_DIM, :] + weighted(lo, hi, p)
-
-    for g, (lo, hi) in enumerate(groups):
-
-        @pl.when(flag_ref[g] == 1)
-        def _():
-            add(lo, hi, False)
-
-        @pl.when(flag_ref[g] == 2)
-        def _():
-            add(lo, hi, True)
-
-    @pl.when(jnp.logical_not(jnp.max(state[HEAD_DIM + 8 : HEAD_DIM + 9, :]) < TOO_LARGE))
+        peak = state_in[0, HEAD_DIM : HEAD_DIM + 1, :]
+        total = state_in[0, HEAD_DIM + 8 : HEAD_DIM + 9, :]
+        summed = state_in[0, 0:HEAD_DIM, :]
+    lo = 1 if first else 0
+    p = jnp.exp2(scores(lo, n) * TO_LOG2 - peak * TO_LOG2)
+    total = total + jnp.sum(p, axis=0, keepdims=True)
+    put(peak, total, summed + weighted(lo, n, p))
+
+    @pl.when(jnp.logical_not(jnp.max(total) < TOO_LARGE))
     def _():
-        s = scores(0, n, True)
+        s = scores(0, n)
+        if first:
+            s = jnp.concatenate([own_scores(), s[ROWS:]], axis=0)
         peak = jnp.max(s, axis=0, keepdims=True)
         if not first:
             old = state_in[0, HEAD_DIM : HEAD_DIM + 1, :]
@@ -329,20 +306,18 @@
             out_ref[:, j * HEAD_DIM : (j + 1) * HEAD_DIM] = out[j * ROWS : (j + 1) * ROWS]
 
 
-def prefill_part(me, doc, queries, blocks, sources, order, groups, state, last, name):
+def prefill_part(me, queries, own, blocks, sources, state, last, name):
     first = state is None
-    counts = [COUNT[source] for source in sources]
-    n = sum(counts)
+    n = sum(COUNT[source] for source in sources)
     steps = HEADS // FUSED
     per_kv = steps // KV_HEADS
     q_spec = pl.BlockSpec((ROWS, FUSED * HEAD_DIM), lambda i, *_: (0, i))
     state_spec = pl.BlockSpec((1, STATE, LANES), lambda i, *_: (i, 0, 0))
-    in_specs = [
-        pl.BlockSpec((1, ROWS), lambda i, *_: (0, 0)),
-        q_spec,
+    in_specs = [q_spec, pl.BlockSpec((1, 16, HEAD_DIM), lambda i, *_: (0, 2 * ROWS // 16, 0))]
+    in_specs += [
+        pl.BlockSpec((COUNT[source], BLOCK, HEAD_DIM), lambda i, *_: (0, 0, i // per_kv)) for source in sources
     ]
-    in_specs += [pl.BlockSpec((c, BLOCK, HEAD_DIM), lambda i, *_: (0, 0, i // per_kv)) for c in counts]
-    operands = [me, doc, queries, *blocks]
+    operands = [me, queries, own, *blocks]
     scratch = []
     if not first:
         in_specs.append(state_spec)
@@ -355,14 +330,12 @@
         out_shape = jax.ShapeDtypeStruct((steps, STATE, LANES), jnp.float32)
         out_spec = state_spec
     scratch += [
+        pltpu.VMEM((n * ROWS, 2 * HEAD_DIM), jnp.bfloat16),
         pltpu.VMEM((n * ROWS, HEAD_DIM), jnp.bfloat16),
-        pltpu.VMEM((n * ROWS, HEAD_DIM), jnp.bfloat16),
-        pltpu.VMEM((LANES, HEAD_DIM), jnp.bfloat16),
-        pltpu.VMEM((n, 8, LANES), jnp.int32),
-        pltpu.SMEM((len(groups),), jnp.int32),
+        pltpu.VMEM((LANES, 2 * HEAD_DIM), jnp.bfloat16),
     ]
     return pl.pallas_call(
-        functools.partial(prefill_kernel, sources=sources, order=order, groups=groups, first=first, last=last),
+        functools.partial(prefill_kernel, sources=sources, first=first, last=last),
         grid_spec=pltpu.PrefetchScalarGridSpec(
             num_scalar_prefetch=1,
             grid=(steps,),
@@ -372,7 +345,9 @@
         ),
         out_shape=out_shape,
         compiler_params=pltpu.CompilerParams(vmem_limit_bytes=62 * 1024 * 1024),
-        cost_estimate=pl.CostEstimate(flops=4 * n * ROWS * ROWS * HEADS * HEAD_DIM, bytes_accessed=4_000_000, transcendentals=0),
+        cost_estimate=pl.CostEstimate(
+            flops=4 * n * ROWS * ROWS * HEADS * HEAD_DIM, bytes_accessed=4_000_000, transcendentals=0
+        ),
         name=name,
     )(*operands)
 
@@ -387,46 +362,26 @@
     own = make_block(fill_doc[None], prefill_key_values.reshape(2 * ROWS, KV_HEADS * HEAD_DIM))
     back1 = lax.ppermute(own, "y", [(i, i + 1) for i in range(3)])
     back2 = lax.ppermute(own, "y", [(i, i + 2) for i in range(2)])
-    row = lax.all_to_all(jnp.broadcast_to(back1, (4,) + back1.shape[1:]), "z", 0, 0)
-    across = lax.ppermute(jnp.where(xh == 0, own, back2), "xh", [(0, 1), (1, 0)])
-
     queries = decode_queries.reshape(STEPS, SEQS, HEADS, HEAD_DIM)
     shares = decode_partials(cached_len, me[None], queries, stored_key_values, step_key_values)
 
-    far_row = lax.ppermute(row, "xh", [(0, 1), (1, 0)])
+    back1, back2, shares = lax.optimization_barrier((back1, back2, shares))
+    row = [back1] + [lax.ppermute(back1, "z", [(i, i ^ k) for i in range(4)]) for k in SIDE]
+    across = lax.ppermute(jnp.where(xh == 0, own, back2), "xh", [(0, 1), (1, 0)])
+    far_row = lax.ppermute(jnp.concatenate(row, axis=0), "xh", [(0, 1), (1, 0)])
     packs = {bit: jnp.concatenate([jnp.where((z & bit) == 0, own, back2), across], axis=0) for bit in (1, 2)}
     packs, shares = lax.optimization_barrier((packs, shares))
     side = {k: lax.ppermute(packs[min(k, 2)], "z", [(i, i ^ k) for i in range(4)]) for k in SIDE}
 
-    doc = fill_doc[None]
-
     shares = lax.all_to_all(shares, CTX, 0, 0)
-    state = prefill_part(
-        me[None],
-        doc,
-        prefill_queries,
-        [own, row, back2, across],
-        ("own", "row", "back", "across"),
-        tuple(range(7)),
-        ((1, 5), (5, 7)),
-        None,
-        False,
-        "prefill_first",
-    )
+    sources = ("own",) + ("row",) * 4 + ("back", "across")
+    blocks = [own, *row, back2, across]
+    state = prefill_part(me[None], prefill_queries, own, blocks, sources, None, False, "prefill_first")
     shares, state = lax.optimization_barrier((shares, state))
     spread = lax.all_to_all(join_shares(shares), CTX, 0, 0)
-    fill_out = prefill_part(
-        me[None],
-        doc,
-        prefill_queries,
-        [far_row] + [side[k] for k in SIDE],
-        ("row",) + SIDE,
-        (0, 1, 2, 3, 5, 7, 9, 4, 6, 8),
-        ((0, 4), (4, 7), (7, 10)),
-        state,
-        True,
-        "prefill_last",
-    )
+    sources = ("far_row",) + SIDE
+    blocks = [far_row] + [side[k] for k in SIDE]
+    fill_out = prefill_part(me[None], prefill_queries, own, blocks, sources, state, True, "prefill_last")
     spread, fill_out = lax.optimization_barrier((spread, fill_out))
     step_out = spread.reshape(SEQS, STEPS, HEADS, HEAD_DIM).transpose(1, 0, 2, 3)
     return fill_out, step_out.reshape(STEPS, SEQS, HEADS * HEAD_DIM)

time: 94.6 us -> 91 us (0.962)
  the two profiles are of different devices: /device:TPU:46 before, /device:TPU:4 now
where the time goes in v6:
time: 91 us; the launch traced here: 90.5 us
  Pallas kernels  43.6 us (48%)
  starting transfers between devices  37.5 us (41%)
  local copies, waits for them, and re-layouts  4.02 us (4%)
  waiting for transfers between devices  2.39 us (3%)
  other arithmetic  2.11 us (2%)
    pallas_call x2, Pallas kernels, prefill_part(): pl.pallas_call(functools.partial(prefill_kernel, sources=sources, first=f...  33.6 us
    all_to_all x1, starting transfers between devices, local(): spread = lax.all_to_all(join_shares(shares), CTX, 0, 0)  10.3 us
    all_to_all x1, starting transfers between devices, local(): shares = lax.all_to_all(shares, CTX, 0, 0)  8.44 us
    pallas_call x1, Pallas kernels, decode_partials(): pl.pallas_call(functools.partial(decode_kernel, per_step=per_step), grid_...  5.67 us
    ppermute x3, starting transfers between devices, local(): lax.ppermute(back1, 'z', [(i, i ^ k) for i in range(4)])  4.9 us
    ppermute x1, starting transfers between devices, local(): back2 = lax.ppermute(own, 'y', [(i, i + 2) for i in range(2)])  4.81 us
    ppermute x3, starting transfers between devices, local(): lax.ppermute(packs[min(k, 2)], 'z', [(i, i ^ k) for i in range(4)])  4.55 us
    ppermute x1, starting transfers between devices, local(): back1 = lax.ppermute(own, 'y', [(i, i + 1) for i in range(3)])  3.61 us
  transfers between devices with their start and end apart: 12, of which 1 were waited for; matrix products, arithmetic and copies ran while one was open for 4% of the time, Pallas kernels for 46%

profile of v6, /device:TPU:4, one launch (start us, length us, event | category | flops | bytes accessed | tf_op | source)
XLA Modules:
  0.0 90.5 jit_solution(8853465772529582480)
XLA Ops:
  0.6 1.7 %make_block.1.own_info_ref.refs_0_ = bf16[1,400,256]{2,1,0:T(8,128)(2,1)} custom-call(s32[1,192]{1,0:T(1,128)} %bitcast.18, bf16[384,256]{1,0:T(8,128)(2,1)} %bitcast.17), custom_call_target="tpu_custom_call" | custom-call | flops 1000 | bytes 400000 | tf_op jit(solution)/shard_map/make_block/pallas_call | solution.py:183
  2.4 0.0 copy-start.1
  2.4 3.6 %collective-permute-start = (bf16[1,400,256]{2,1,0:T(8,128)(2,1)}, bf16[1,400,256]{2,1,0:T(8,128)(2,1)S(1)}, u32[]{:S(2)}, u32[]{:S(2)}) collective-permute-start(bf16[1,400,256]{2,1,0:T(8,128)(2,1)} %make_block.1.own_info_ref.refs_0_), channel_id=1, source_target_pairs={{0,32},{32,64},{64,96},{1,33},{33,65},{65,97},{2,34},{34,66},{66,9... | collective-permute-start | bytes 614408 | tf_op jit(solution)/shard_map/ppermute | solution.py:363
  6.0 4.8 %collective-permute-start.1 = (bf16[1,400,256]{2,1,0:T(8,128)(2,1)}, bf16[1,400,256]{2,1,0:T(8,128)(2,1)S(1)}, u32[]{:S(2)}, u32[]{:S(2)}) collective-permute-start(bf16[1,400,256]{2,1,0:T(8,128)(2,1)} %make_block.1.own_info_ref.refs_0_), channel_id=1, source_target_pairs={{0,64},{32,96},{1,65},{33,97},{2,66},{34,98},{3,67},{35,99},{4,68}... | collective-permute-start | bytes 614408 | tf_op jit(solution)/shard_map/ppermute | solution.py:364
  10.8 2.0 %copy.11 = bf16[16,8,16,128]{3,2,1,0:T(8,128)(2,1)} copy(bf16[16,8,16,128]{3,1,2,0:T(8,128)(2,1)} %bitcast.16) | data formatting | bytes 1048576
  12.8 5.7 %decode_partials.1 = bf16[32,80,128]{2,1,0:T(8,128)(2,1)} custom-call(s32[32]{0:T(128)} %len_ref.1, s32[1]{0:T(128)} %bitcast.2.me_ref, bf16[4,32,16,128]{3,2,1,0:T(8,128)(2,1)} %bitcast.14, bf16[2,32,128,256]{3,2,1,0:T(8,128)(2,1)} %kv_ref.1, bf16[4,2,32,256]{3,2,1,0:T(8,128)(2,1)} %step_ref.1), custom_call_target="tpu_custom_call" | custom-call | flops 70000000 | bytes 5500000 | tf_op jit(solution)/shard_map/decode_partials/pallas_call | solution.py:119
  18.4 0.0 collective-permute-done.refs_1_
  18.4 0.0 copy-start.2
  18.4 0.0 collective-permute-done.1.refs_5_
  18.4 0.0 copy-done.1
  18.4 0.0 copy-start.6
  18.5 0.1 broadcast_select_fusion
  18.5 0.6 collective-permute-start.2
  19.1 3.9 %collective-permute-start.3 = (bf16[1,400,256]{2,1,0:T(8,128)(2,1)S(1)}, bf16[1,400,256]{2,1,0:T(8,128)(2,1)S(1)}, u32[]{:S(2)}, u32[]{:S(2)}) collective-permute-start(bf16[1,400,256]{2,1,0:T(8,128)(2,1)S(1)} %collective-permute-done.refs_1_), channel_id=1, source_target_pairs={{0,8},{4,12},{8,0},{12,4},{1,9},{5,13},{9,1},{13,5},{2,10},{6,14},... | collective-permute-start | bytes 614408 | tf_op jit(solution)/shard_map/ppermute | solution.py:369
  23.0 1.0 %collective-permute-start.4 = (bf16[1,400,256]{2,1,0:T(8,128)(2,1)S(1)}, bf16[1,400,256]{2,1,0:T(8,128)(2,1)S(1)}, u32[]{:S(2)}, u32[]{:S(2)}) collective-permute-start(bf16[1,400,256]{2,1,0:T(8,128)(2,1)S(1)} %collective-permute-done.refs_1_), channel_id=1, source_target_pairs={{0,4},{4,0},{8,12},{12,8},{1,5},{5,1},{9,13},{13,9},{2,6},{6,2},{1... | collective-permute-start | bytes 614408 | tf_op jit(solution)/shard_map/ppermute | solution.py:369
  24.0 0.0 collective-permute-start.5
  24.0 2.4 %collective-permute-done.2.refs_6_ = bf16[1,400,256]{2,1,0:T(8,128)(2,1)S(1)} collective-permute-done((bf16[1,400,256]{2,1,0:T(8,128)(2,1)S(1)}, bf16[1,400,256]{2,1,0:T(8,128)(2,1)S(1)}, u32[]{:S(2)}, u32[]{:S(2)}) %collective-permute-start.2) | collective-permute-done | bytes 204832 | tf_op jit(solution)/shard_map/ppermute | solution.py:370
  26.4 0.0 copy-start.7
  26.4 0.0 copy-done.6
  26.4 0.8 pad_maximum_fusion.1
  27.2 8.4 %all-to-all-start = ((bf16[32,80,128]{2,1,0:T(8,128)(2,1)}), bf16[32,80,128]{2,1,0:T(8,128)(2,1)S(1)}, u32[]{:S(2)}, u32[]{:S(2)}) async-start(bf16[32,80,128]{2,1,0:T(8,128)(2,1)} %decode_partials.1), calls=%async_computation | async-start | bytes 1310720 | tf_op jit(solution)/shard_map/all_to_all | solution.py:376
  35.6 0.0 collective-permute-done.3.refs_2_
  35.7 0.0 copy-start.3
  35.7 0.0 collective-permute-done.4.refs_3_
  35.7 0.0 copy-done.2
  35.7 0.0 copy-start.4
  35.7 0.0 collective-permute-done.5.refs_4_
  35.7 0.0 copy-start.5
  35.7 1.2 %pad_maximum_fusion = bf16[4,400,256]{2,1,0:T(8,128)(2,1)S(1)} fusion(bf16[1,400,256]{2,1,0:T(8,128)(2,1)S(1)} %collective-permute-done.5.refs_4_, bf16[1,400,256]{2,1,0:T(8,128)(2,1)S(1)} %collective-permute-done.4.refs_3_, bf16[1,400,256]{2,1,0:T(8,128)(2,1)S(1)} %collective-permute-done.3.refs_2_, bf16[1,400,256]{2,1,0:T(8,128)(2,1)} %copy-done.2), kind=kLoop, calls=%fused_computation | loop fusion | flops 1228800 | bytes 1638400 | tf_op jit(solution)/shard_map/concatenate | solution.py:371
  36.9 0.3 collective-permute-start.6
  37.3 3.3 %collective-permute-start.7 = (bf16[2,400,256]{2,1,0:T(8,128)(2,1)S(1)}, bf16[2,400,256]{2,1,0:T(8,128)(2,1)}, u32[]{:S(2)}, u32[]{:S(2)}) collective-permute-start(bf16[2,400,256]{2,1,0:T(8,128)(2,1)S(1)} %get-tuple-element.17), channel_id=1, source_target_pairs={{0,8},{4,12},{8,0},{12,4},{1,9},{5,13},{9,1},{13,5},{2,10},{6,14},... | collective-permute-start | bytes 1228808 | tf_op jit(solution)/shard_map/ppermute | solution.py:374
  40.5 1.2 %collective-permute-start.9 = (bf16[2,400,256]{2,1,0:T(8,128)(2,1)S(1)}, bf16[2,400,256]{2,1,0:T(8,128)(2,1)}, u32[]{:S(2)}, u32[]{:S(2)}) collective-permute-start(bf16[2,400,256]{2,1,0:T(8,128)(2,1)S(1)} %get-tuple-element.17), channel_id=1, source_target_pairs={{0,12},{4,8},{8,4},{12,0},{1,13},{5,9},{9,5},{13,1},{2,14},{6,10},... | collective-permute-start | bytes 1228808 | tf_op jit(solution)/shard_map/ppermute | solution.py:374
  41.7 0.0 copy-done.7
  41.7 0.0 copy-done.3
  41.7 0.0 copy-done.4
  41.7 0.0 copy-done.5
  41.7 0.1 collective-permute-start.8
  41.8 15.2 %prefill_first.1.refs_4_ = f32[2,144,1536]{2,1,0:T(8,128)} custom-call(s32[1]{0:T(128)} %bitcast.2.me_ref, bf16[192,2048]{1,0:T(8,128)(2,1)} %q_ref.3, bf16[1,400,256]{2,1,0:T(8,128)(2,1)} %make_block.1.own_info_ref.refs_0_, bf16[1,400,256]{2,1,0:T(8,128)(2,1)} %make_block.1.own_info_ref.refs_0_, bf16[1,400,256]{2,1,0:T(8,128)(2,1)} %copy-done.2, ...), custom_call_target="tpu_custom_call" | custom-call | flops 2113929216 | bytes 4000000 | tf_op jit(solution)/shard_map/prefill_first/pallas_call | solution.py:337
  57.0 0.0 all-to-all-done.in_ref
  57.0 0.0 copy-start
  57.0 0.8 copy-done
  57.8 2.5 %join_shares.1 = bf16[32,64,128]{2,1,0:T(8,128)(2,1)} custom-call(bf16[32,80,128]{2,1,0:T(8,128)(2,1)} %copy-done), custom_call_target="tpu_custom_call" | custom-call | flops 1000000 | bytes 1200000 | tf_op jit(solution)/shard_map/join_shares/pallas_call | solution.py:160
  60.4 10.3 %all-to-all-start.1 = ((bf16[32,64,128]{2,1,0:T(8,128)(2,1)}), bf16[32,64,128]{2,1,0:T(8,128)(2,1)S(1)}, u32[]{:S(2)}, u32[]{:S(2)}) async-start(bf16[32,64,128]{2,1,0:T(8,128)(2,1)} %join_shares.1), calls=%async_computation.1 | async-start | bytes 1048576 | tf_op jit(solution)/shard_map/all_to_all | solution.py:381
  70.7 0.0 collective-permute-done.7.refs_1_
  70.7 0.0 collective-permute-done.8.refs_2_
  70.7 0.0 collective-permute-done.9.refs_3_
  70.8 0.0 collective-permute-done.6.refs_0_
  70.8 18.5 %prefill_last.1 = bf16[192,2048]{1,0:T(8,128)(2,1)} custom-call(s32[1]{0:T(128)} %bitcast.2.me_ref, bf16[192,2048]{1,0:T(8,128)(2,1)} %q_ref.3, bf16[1,400,256]{2,1,0:T(8,128)(2,1)} %make_block.1.own_info_ref.refs_0_, bf16[4,400,256]{2,1,0:T(8,128)(2,1)} %collective-permute-done.6.refs_0_, bf16[2,400,256]{2,1,0:T(8,128)(2,1)} %collective-permute-done.7.refs_1_, ...), custom_call_target="tpu_custom_call" | custom-call | flops 3019898880 | bytes 4000000 | tf_op jit(solution)/shard_map/prefill_last/pallas_call | solution.py:337
  89.2 0.0 all-to-all-done.1
  89.2 0.1 reshape.20
  89.4 1.1 %copy.10 = bf16[4,32,2048]{2,1,0:T(8,128)(2,1)} copy(bf16[4,32,2048]{2,0,1:T(4,128)(2,1)S(1)} %reshape.20) | data formatting | bytes 1048576 | tf_op jit(solution)/shard_map/reshape | solution.py:387
Async XLA Ops:
  2.4 16.1 %copy-start.1 = (bf16[1,400,256]{2,1,0:T(8,128)(2,1)S(1)}, bf16[1,400,256]{2,1,0:T(8,128)(2,1)}, u32[]{:S(2)}) copy-start(bf16[1,400,256]{2,1,0:T(8,128)(2,1)} %make_block.1.own_info_ref.refs_0_) | copy-start | bytes 614404
  2.4 16.1 %collective-permute-start = (bf16[1,400,256]{2,1,0:T(8,128)(2,1)}, bf16[1,400,256]{2,1,0:T(8,128)(2,1)S(1)}, u32[]{:S(2)}, u32[]{:S(2)}) collective-permute-start(bf16[1,400,256]{2,1,0:T(8,128)(2,1)} %make_block.1.own_info_ref.refs_0_), channel_id=1, source_target_pairs={{0,32},{32,64},{64,96},{1,33},{33,65},{65,97},{2,34},{34,66},{66,9... | collective-permute-start | bytes 614408 | tf_op jit(solution)/shard_map/ppermute | solution.py:363
  6.0 12.5 %collective-permute-start.1 = (bf16[1,400,256]{2,1,0:T(8,128)(2,1)}, bf16[1,400,256]{2,1,0:T(8,128)(2,1)S(1)}, u32[]{:S(2)}, u32[]{:S(2)}) collective-permute-start(bf16[1,400,256]{2,1,0:T(8,128)(2,1)} %make_block.1.own_info_ref.refs_0_), channel_id=1, source_target_pairs={{0,64},{32,96},{1,65},{33,97},{2,66},{34,98},{3,67},{35,99},{4,68}... | collective-permute-start | bytes 614408 | tf_op jit(solution)/shard_map/ppermute | solution.py:364
  18.4 17.3 %copy-start.2 = (bf16[1,400,256]{2,1,0:T(8,128)(2,1)}, bf16[1,400,256]{2,1,0:T(8,128)(2,1)S(1)}, u32[]{:S(2)}) copy-start(bf16[1,400,256]{2,1,0:T(8,128)(2,1)S(1)} %collective-permute-done.refs_1_) | copy-start | bytes 614404
  18.4 7.9 %copy-start.6 = (bf16[1,400,256]{2,1,0:T(8,128)(2,1)}, bf16[1,400,256]{2,1,0:T(8,128)(2,1)S(1)}, u32[]{:S(2)}) copy-start(bf16[1,400,256]{2,1,0:T(8,128)(2,1)S(1)} %collective-permute-done.1.refs_5_) | copy-start | bytes 614404
  18.5 7.8 %collective-permute-start.2 = (bf16[1,400,256]{2,1,0:T(8,128)(2,1)S(1)}, bf16[1,400,256]{2,1,0:T(8,128)(2,1)S(1)}, u32[]{:S(2)}, u32[]{:S(2)}) collective-permute-start(bf16[1,400,256]{2,1,0:T(8,128)(2,1)S(1)} %get-tuple-element.23), channel_id=1, source_target_pairs={{0,16},{16,0},{1,17},{17,1},{2,18},{18,2},{3,19},{19,3},{4,20},{20... | collective-permute-start | bytes 614408 | tf_op jit(solution)/shard_map/ppermute | solution.py:370
  19.1 16.5 %collective-permute-start.3 = (bf16[1,400,256]{2,1,0:T(8,128)(2,1)S(1)}, bf16[1,400,256]{2,1,0:T(8,128)(2,1)S(1)}, u32[]{:S(2)}, u32[]{:S(2)}) collective-permute-start(bf16[1,400,256]{2,1,0:T(8,128)(2,1)S(1)} %collective-permute-done.refs_1_), channel_id=1, source_target_pairs={{0,8},{4,12},{8,0},{12,4},{1,9},{5,13},{9,1},{13,5},{2,10},{6,14},... | collective-permute-start | bytes 614408 | tf_op jit(solution)/shard_map/ppermute | solution.py:369
  23.0 12.7 %collective-permute-start.4 = (bf16[1,400,256]{2,1,0:T(8,128)(2,1)S(1)}, bf16[1,400,256]{2,1,0:T(8,128)(2,1)S(1)}, u32[]{:S(2)}, u32[]{:S(2)}) collective-permute-start(bf16[1,400,256]{2,1,0:T(8,128)(2,1)S(1)} %collective-permute-done.refs_1_), channel_id=1, source_target_pairs={{0,4},{4,0},{8,12},{12,8},{1,5},{5,1},{9,13},{13,9},{2,6},{6,2},{1... | collective-permute-start | bytes 614408 | tf_op jit(solution)/shard_map/ppermute | solution.py:369
  24.0 11.7 %collective-permute-start.5 = (bf16[1,400,256]{2,1,0:T(8,128)(2,1)S(1)}, bf16[1,400,256]{2,1,0:T(8,128)(2,1)S(1)}, u32[]{:S(2)}, u32[]{:S(2)}) collective-permute-start(bf16[1,400,256]{2,1,0:T(8,128)(2,1)S(1)} %collective-permute-done.refs_1_), channel_id=1, source_target_pairs={{0,12},{4,8},{8,4},{12,0},{1,13},{5,9},{9,5},{13,1},{2,14},{6,10},... | collective-permute-start | bytes 614408 | tf_op jit(solution)/shard_map/ppermute | solution.py:369
  26.4 15.4 %copy-start.7 = (bf16[1,400,256]{2,1,0:T(8,128)(2,1)}, bf16[1,400,256]{2,1,0:T(8,128)(2,1)S(1)}, u32[]{:S(2)}) copy-start(bf16[1,400,256]{2,1,0:T(8,128)(2,1)S(1)} %collective-permute-done.2.refs_6_) | copy-start | bytes 614404
  27.2 29.8 %all-to-all-start = ((bf16[32,80,128]{2,1,0:T(8,128)(2,1)}), bf16[32,80,128]{2,1,0:T(8,128)(2,1)S(1)}, u32[]{:S(2)}, u32[]{:S(2)}) async-start(bf16[32,80,128]{2,1,0:T(8,128)(2,1)} %decode_partials.1), calls=%async_computation | async-start | bytes 1310720 | tf_op jit(solution)/shard_map/all_to_all | solution.py:376
  35.7 6.1 %copy-start.3 = (bf16[1,400,256]{2,1,0:T(8,128)(2,1)}, bf16[1,400,256]{2,1,0:T(8,128)(2,1)S(1)}, u32[]{:S(2)}) copy-start(bf16[1,400,256]{2,1,0:T(8,128)(2,1)S(1)} %collective-permute-done.3.refs_2_) | copy-start | bytes 614404
  35.7 6.0 %copy-start.4 = (bf16[1,400,256]{2,1,0:T(8,128)(2,1)}, bf16[1,400,256]{2,1,0:T(8,128)(2,1)S(1)}, u32[]{:S(2)}) copy-start(bf16[1,400,256]{2,1,0:T(8,128)(2,1)S(1)} %collective-permute-done.4.refs_3_) | copy-start | bytes 614404
  35.7 6.0 %copy-start.5 = (bf16[1,400,256]{2,1,0:T(8,128)(2,1)}, bf16[1,400,256]{2,1,0:T(8,128)(2,1)S(1)}, u32[]{:S(2)}) copy-start(bf16[1,400,256]{2,1,0:T(8,128)(2,1)S(1)} %collective-permute-done.5.refs_4_) | copy-start | bytes 614404
  36.9 33.8 %collective-permute-start.6 = (bf16[4,400,256]{2,1,0:T(8,128)(2,1)S(1)}, bf16[4,400,256]{2,1,0:T(8,128)(2,1)}, u32[]{:S(2)}, u32[]{:S(2)}) collective-permute-start(bf16[4,400,256]{2,1,0:T(8,128)(2,1)S(1)} %pad_maximum_fusion), channel_id=1, source_target_pairs={{0,16},{16,0},{1,17},{17,1},{2,18},{18,2},{3,19},{19,3},{4,20},{20... | collective-permute-start | bytes 2457608 | tf_op jit(solution)/shard_map/ppermute | solution.py:371
  37.3 33.5 %collective-permute-start.7 = (bf16[2,400,256]{2,1,0:T(8,128)(2,1)S(1)}, bf16[2,400,256]{2,1,0:T(8,128)(2,1)}, u32[]{:S(2)}, u32[]{:S(2)}) collective-permute-start(bf16[2,400,256]{2,1,0:T(8,128)(2,1)S(1)} %get-tuple-element.17), channel_id=1, source_target_pairs={{0,8},{4,12},{8,0},{12,4},{1,9},{5,13},{9,1},{13,5},{2,10},{6,14},... | collective-permute-start | bytes 1228808 | tf_op jit(solution)/shard_map/ppermute | solution.py:374
  40.5 30.2 %collective-permute-start.9 = (bf16[2,400,256]{2,1,0:T(8,128)(2,1)S(1)}, bf16[2,400,256]{2,1,0:T(8,128)(2,1)}, u32[]{:S(2)}, u32[]{:S(2)}) collective-permute-start(bf16[2,400,256]{2,1,0:T(8,128)(2,1)S(1)} %get-tuple-element.17), channel_id=1, source_target_pairs={{0,12},{4,8},{8,4},{12,0},{1,13},{5,9},{9,5},{13,1},{2,14},{6,10},... | collective-permute-start | bytes 1228808 | tf_op jit(solution)/shard_map/ppermute | solution.py:374
  41.7 29.0 %collective-permute-start.8 = (bf16[2,400,256]{2,1,0:T(8,128)(2,1)}, bf16[2,400,256]{2,1,0:T(8,128)(2,1)}, u32[]{:S(2)}, u32[]{:S(2)}) collective-permute-start(bf16[2,400,256]{2,1,0:T(8,128)(2,1)} %get-tuple-element.18), channel_id=1, source_target_pairs={{0,4},{4,0},{8,12},{12,8},{1,5},{5,1},{9,13},{13,9},{2,6},{6,2},{1... | collective-permute-start | bytes 1228808 | tf_op jit(solution)/shard_map/ppermute | solution.py:374
  57.0 0.8 copy-start
  60.4 28.9 %all-to-all-start.1 = ((bf16[32,64,128]{2,1,0:T(8,128)(2,1)}), bf16[32,64,128]{2,1,0:T(8,128)(2,1)S(1)}, u32[]{:S(2)}, u32[]{:S(2)}) async-start(bf16[32,64,128]{2,1,0:T(8,128)(2,1)} %join_shares.1), calls=%async_computation.1 | async-start | bytes 1048576 | tf_op jit(solution)/shard_map/all_to_all | solution.py:381

commit v7 on v6

--- a/solution.py
+++ b/solution.py
@@ -46,7 +46,7 @@
     return high, (value - high).astype(jnp.bfloat16).astype(jnp.float32)
 
 
-def decode_kernel(len_ref, me_ref, q_ref, kv_ref, step_ref, out_ref, *, per_step):
+def decode_kernel(len_ref, me_ref, q_ref, kv_ref, step_ref, out_ref, rows_ref, *, per_step):
     base = pl.program_id(0) * per_step
     me = me_ref[0]
     lane = lax.broadcasted_iota(jnp.int32, (PER_SEQ, SLOTS), 1)
@@ -56,8 +56,13 @@
     row = lax.broadcasted_iota(jnp.int32, (PER_SEQ, HEAD_DIM), 0)
     second = lax.rem(row, HEADS) >= GROUP
 
+    for t in range(STEPS):
+        for h in range(HEADS):
+            at = (t * HEADS + h) * per_step
+            rows_ref[at : at + per_step, :] = q_ref[t, :, h * HEAD_DIM : (h + 1) * HEAD_DIM].astype(jnp.float32)
+
     def queries_of(i):
-        q = jnp.concatenate([q_ref[t, i] for t in range(STEPS)], axis=0)
+        q = rows_ref[pl.ds(i, PER_SEQ, stride=per_step), :].astype(jnp.bfloat16)
         none = jnp.zeros_like(q)
         return jnp.concatenate([jnp.where(second, none, q), jnp.where(second, q, none)], axis=1)
 
@@ -122,11 +127,12 @@
             num_scalar_prefetch=2,
             grid=(SEQS // per_step,),
             in_specs=[
-                pl.BlockSpec((STEPS, per_step, HEADS, HEAD_DIM), lambda i, *_: (0, i, 0, 0)),
+                pl.BlockSpec((STEPS, per_step, HEADS * HEAD_DIM), lambda i, *_: (0, i, 0)),
                 pl.BlockSpec((2, per_step, SLOTS, KV_HEADS * HEAD_DIM), lambda i, *_: (0, i, 0, 0)),
                 pl.BlockSpec((STEPS, 2, 16, KV_HEADS * HEAD_DIM), lambda i, lens, me: (0, 0, me[0] // 16, 0)),
             ],
             out_specs=pl.BlockSpec((per_step, PACKED, HEAD_DIM), lambda i, *_: (i, 0, 0)),
+            scratch_shapes=[pltpu.VMEM((PER_SEQ * per_step, HEAD_DIM), jnp.float32)],
         ),
         out_shape=jax.ShapeDtypeStruct((SEQS, PACKED, HEAD_DIM), jnp.bfloat16),
         compiler_params=pltpu.CompilerParams(vmem_limit_bytes=62 * 1024 * 1024),
@@ -135,7 +141,7 @@
     )(lens, me, queries, cache, fresh)
 
 
-def join_kernel(in_ref, out_ref, coef):
+def join_kernel(in_ref, out_ref, coef, joined):
     peaks, totals = [], []
     for i in range(SEQS):
         st = in_ref[i, PER_SEQ:, :].astype(jnp.float32)
@@ -151,18 +157,21 @@
     acc = jnp.zeros((PER_SEQ, HEAD_DIM), jnp.float32)
     for i in range(SEQS):
         acc = acc + in_ref[i, :PER_SEQ, :].astype(jnp.float32) * columns[:PER_SEQ, i : i + 1]
-    acc = acc.astype(jnp.bfloat16)
+    joined[...] = acc
+    heads = [joined[pl.ds(h, STEPS, stride=HEADS), :] for h in range(HEADS)]
+    out = jnp.concatenate(heads, axis=1).astype(jnp.bfloat16)
     for i in range(SEQS):
-        out_ref[i] = acc
+        out_ref[i] = out
 
 
 def join_shares(shares):
     return pl.pallas_call(
         join_kernel,
-        out_shape=jax.ShapeDtypeStruct((SEQS, PER_SEQ, HEAD_DIM), jnp.bfloat16),
+        out_shape=jax.ShapeDtypeStruct((SEQS, STEPS, HEADS * HEAD_DIM), jnp.bfloat16),
         in_specs=[pl.BlockSpec(memory_space=pltpu.VMEM)],
         out_specs=pl.BlockSpec(memory_space=pltpu.VMEM),
-        scratch_shapes=[pltpu.VMEM((HEAD_DIM, HEAD_DIM), jnp.float32)],
+        scratch_shapes=[pltpu.VMEM((HEAD_DIM, HEAD_DIM), jnp.float32), pltpu.VMEM((PER_SEQ, HEAD_DIM), jnp.float32)],
+        compiler_params=pltpu.CompilerParams(vmem_limit_bytes=8 * 1024 * 1024),
         cost_estimate=pl.CostEstimate(flops=1_000_000, bytes_accessed=1_200_000, transcendentals=4096),
         name="join_shares",
     )(shares)
@@ -362,8 +371,7 @@
     own = make_block(fill_doc[None], prefill_key_values.reshape(2 * ROWS, KV_HEADS * HEAD_DIM))
     back1 = lax.ppermute(own, "y", [(i, i + 1) for i in range(3)])
     back2 = lax.ppermute(own, "y", [(i, i + 2) for i in range(2)])
-    queries = decode_queries.reshape(STEPS, SEQS, HEADS, HEAD_DIM)
-    shares = decode_partials(cached_len, me[None], queries, stored_key_values, step_key_values)
+    shares = decode_partials(cached_len, me[None], decode_queries, stored_key_values, step_key_values)
 
     back1, back2, shares = lax.optimization_barrier((back1, back2, shares))
     row = [back1] + [lax.ppermute(back1, "z", [(i, i ^ k) for i in range(4)]) for k in SIDE]
@@ -383,8 +391,7 @@
     blocks = [far_row] + [side[k] for k in SIDE]
     fill_out = prefill_part(me[None], prefill_queries, own, blocks, sources, state, True, "prefill_last")
     spread, fill_out = lax.optimization_barrier((spread, fill_out))
-    step_out = spread.reshape(SEQS, STEPS, HEADS, HEAD_DIM).transpose(1, 0, 2, 3)
-    return fill_out, step_out.reshape(STEPS, SEQS, HEADS * HEAD_DIM)
+    return fill_out, spread.transpose(1, 0, 2)
 
 
 def solution(mesh):

time: 91 us -> 88.3 us (0.970)
  local copies, waits for them, and re-layouts: 4.02 us -> 1.11 us
  starting transfers between devices: 37.5 us -> 38.9 us
  Pallas kernels: 43.6 us -> 42.5 us
    unnamed x17 -> x15, local copies, waits for them, and re-layouts: 2.81 us -> 1.11 us
    all_to_all x1, starting transfers between devices: 8.44 us -> 9.82 us  [local(): shares = lax.all_to_all(shares, CTX, 0, 0)]
    reshape x2 -> x0, local copies, waits for them, and re-layouts: 1.21 us -> none  [local(): return (fill_out, step_out.reshape(STEPS, SEQS, HEADS * HEAD_DIM))]
    pallas_call x1, Pallas kernels: 2.54 us -> 1.47 us  [join_shares(): pl.pallas_call(join_kernel, out_shape=jax.ShapeDtypeStruct((SEQS, STEPS,...]
  transfers between devices with their start and end apart: 12 -> 12, of which waited for: 1 -> 1; matrix products, arithmetic and copies ran while one was open for 4% -> 2% of each run, Pallas kernels for 46% -> 46%
where the time goes in v7:
time: 88.3 us; the launch traced here: 87.9 us
  Pallas kernels  42.5 us (48%)
  starting transfers between devices  38.9 us (44%)
  waiting for transfers between devices  2.39 us (3%)
  other arithmetic  2.13 us (2%)
  local copies, waits for them, and re-layouts  1.11 us (1%)
    pallas_call x2, Pallas kernels, prefill_part(): pl.pallas_call(functools.partial(prefill_kernel, sources=sources, first=f...  33.6 us
    all_to_all x1, starting transfers between devices, local(): spread = lax.all_to_all(join_shares(shares), CTX, 0, 0)  10.3 us
    all_to_all x1, starting transfers between devices, local(): shares = lax.all_to_all(shares, CTX, 0, 0)  9.82 us
    pallas_call x1, Pallas kernels, decode_partials(): pl.pallas_call(functools.partial(decode_kernel, per_step=per_step), grid_...  5.72 us
    ppermute x3, starting transfers between devices, local(): lax.ppermute(back1, 'z', [(i, i ^ k) for i in range(4)])  4.9 us
    ppermute x1, starting transfers between devices, local(): back2 = lax.ppermute(own, 'y', [(i, i + 2) for i in range(2)])  4.81 us
    ppermute x3, starting transfers between devices, local(): lax.ppermute(packs[min(k, 2)], 'z', [(i, i ^ k) for i in range(4)])  4.55 us
    ppermute x1, starting transfers between devices, local(): back1 = lax.ppermute(own, 'y', [(i, i + 1) for i in range(3)])  3.61 us
  transfers between devices with their start and end apart: 12, of which 1 were waited for; matrix products, arithmetic and copies ran while one was open for 2% of the time, Pallas kernels for 46%

profile of v7, /device:TPU:4, one launch (start us, length us, event | category | flops | bytes accessed | tf_op | source)
XLA Modules:
  0.0 87.9 jit_solution(7845029406084610592)
XLA Ops:
  0.6 1.7 %make_block.1.own_info_ref.refs_0_ = bf16[1,400,256]{2,1,0:T(8,128)(2,1)} custom-call(s32[1,192]{1,0:T(1,128)} %bitcast.6, bf16[384,256]{1,0:T(8,128)(2,1)} %bitcast.5), custom_call_target="tpu_custom_call" | custom-call | flops 1000 | bytes 400000 | tf_op jit(solution)/shard_map/make_block/pallas_call | solution.py:192
  2.4 0.0 copy-start
  2.4 3.6 %collective-permute-start = (bf16[1,400,256]{2,1,0:T(8,128)(2,1)}, bf16[1,400,256]{2,1,0:T(8,128)(2,1)S(1)}, u32[]{:S(2)}, u32[]{:S(2)}) collective-permute-start(bf16[1,400,256]{2,1,0:T(8,128)(2,1)} %make_block.1.own_info_ref.refs_0_), channel_id=1, source_target_pairs={{0,32},{32,64},{64,96},{1,33},{33,65},{65,97},{2,34},{34,66},{66,9... | collective-permute-start | bytes 614408 | tf_op jit(solution)/shard_map/ppermute | solution.py:372
  6.0 4.8 %collective-permute-start.1 = (bf16[1,400,256]{2,1,0:T(8,128)(2,1)}, bf16[1,400,256]{2,1,0:T(8,128)(2,1)S(1)}, u32[]{:S(2)}, u32[]{:S(2)}) collective-permute-start(bf16[1,400,256]{2,1,0:T(8,128)(2,1)} %make_block.1.own_info_ref.refs_0_), channel_id=1, source_target_pairs={{0,64},{32,96},{1,65},{33,97},{2,66},{34,98},{3,67},{35,99},{4,68}... | collective-permute-start | bytes 614408 | tf_op jit(solution)/shard_map/ppermute | solution.py:373
  10.8 5.7 %decode_partials.1 = bf16[32,80,128]{2,1,0:T(8,128)(2,1)} custom-call(s32[32]{0:T(128)} %len_ref.1, s32[1]{0:T(128)} %bitcast.2.me_ref, bf16[4,32,2048]{2,1,0:T(8,128)(2,1)} %q_ref.3, bf16[2,32,128,256]{3,2,1,0:T(8,128)(2,1)} %kv_ref.1, bf16[4,2,32,256]{3,2,1,0:T(8,128)(2,1)} %step_ref.1), custom_call_target="tpu_custom_call" | custom-call | flops 70000000 | bytes 5500000 | tf_op jit(solution)/shard_map/decode_partials/pallas_call | solution.py:124
  16.5 0.0 collective-permute-done.refs_1_
  16.5 0.0 copy-start.1
  16.5 0.0 collective-permute-done.1.refs_5_
  16.5 0.0 copy-done
  16.6 0.0 copy-start.5
  16.6 0.1 broadcast_select_fusion
  16.6 0.6 collective-permute-start.2
  17.2 3.9 %collective-permute-start.3 = (bf16[1,400,256]{2,1,0:T(8,128)(2,1)S(1)}, bf16[1,400,256]{2,1,0:T(8,128)(2,1)S(1)}, u32[]{:S(2)}, u32[]{:S(2)}) collective-permute-start(bf16[1,400,256]{2,1,0:T(8,128)(2,1)S(1)} %collective-permute-done.refs_1_), channel_id=1, source_target_pairs={{0,8},{4,12},{8,0},{12,4},{1,9},{5,13},{9,1},{13,5},{2,10},{6,14},... | collective-permute-start | bytes 614408 | tf_op jit(solution)/shard_map/ppermute | solution.py:377
  21.1 1.0 %collective-permute-start.4 = (bf16[1,400,256]{2,1,0:T(8,128)(2,1)S(1)}, bf16[1,400,256]{2,1,0:T(8,128)(2,1)S(1)}, u32[]{:S(2)}, u32[]{:S(2)}) collective-permute-start(bf16[1,400,256]{2,1,0:T(8,128)(2,1)S(1)} %collective-permute-done.refs_1_), channel_id=1, source_target_pairs={{0,4},{4,0},{8,12},{12,8},{1,5},{5,1},{9,13},{13,9},{2,6},{6,2},{1... | collective-permute-start | bytes 614408 | tf_op jit(solution)/shard_map/ppermute | solution.py:377
  22.1 0.0 collective-permute-start.5
  22.1 2.4 %collective-permute-done.2.refs_6_ = bf16[1,400,256]{2,1,0:T(8,128)(2,1)S(1)} collective-permute-done((bf16[1,400,256]{2,1,0:T(8,128)(2,1)S(1)}, bf16[1,400,256]{2,1,0:T(8,128)(2,1)S(1)}, u32[]{:S(2)}, u32[]{:S(2)}) %collective-permute-start.2) | collective-permute-done | bytes 204832 | tf_op jit(solution)/shard_map/ppermute | solution.py:378
  24.5 0.0 copy-start.6
  24.5 0.0 copy-done.5
  24.5 0.9 pad_maximum_fusion.1
  25.3 9.8 %all-to-all-start = ((bf16[32,80,128]{2,1,0:T(8,128)(2,1)}), bf16[32,80,128]{2,1,0:T(8,128)(2,1)S(1)}, u32[]{:S(2)}, u32[]{:S(2)}) async-start(bf16[32,80,128]{2,1,0:T(8,128)(2,1)} %decode_partials.1), calls=%async_computation | async-start | bytes 1310720 | tf_op jit(solution)/shard_map/all_to_all | solution.py:384
  35.2 0.0 collective-permute-done.3.refs_2_
  35.2 0.0 copy-start.2
  35.2 0.0 collective-permute-done.4.refs_3_
  35.2 0.0 copy-done.1
  35.2 0.0 copy-start.3
  35.2 0.0 collective-permute-done.5.refs_4_
  35.2 0.0 copy-start.4
  35.2 1.2 %pad_maximum_fusion = bf16[4,400,256]{2,1,0:T(8,128)(2,1)S(1)} fusion(bf16[1,400,256]{2,1,0:T(8,128)(2,1)S(1)} %collective-permute-done.5.refs_4_, bf16[1,400,256]{2,1,0:T(8,128)(2,1)S(1)} %collective-permute-done.4.refs_3_, bf16[1,400,256]{2,1,0:T(8,128)(2,1)S(1)} %collective-permute-done.3.refs_2_, bf16[1,400,256]{2,1,0:T(8,128)(2,1)} %copy-done.1), kind=kLoop, calls=%fused_computation | loop fusion | flops 1228800 | bytes 1638400 | tf_op jit(solution)/shard_map/concatenate | solution.py:379
  36.4 0.3 collective-permute-start.6
  36.8 3.3 %collective-permute-start.7 = (bf16[2,400,256]{2,1,0:T(8,128)(2,1)S(1)}, bf16[2,400,256]{2,1,0:T(8,128)(2,1)}, u32[]{:S(2)}, u32[]{:S(2)}) collective-permute-start(bf16[2,400,256]{2,1,0:T(8,128)(2,1)S(1)} %get-tuple-element.17), channel_id=1, source_target_pairs={{0,8},{4,12},{8,0},{12,4},{1,9},{5,13},{9,1},{13,5},{2,10},{6,14},... | collective-permute-start | bytes 1228808 | tf_op jit(solution)/shard_map/ppermute | solution.py:382
  40.1 1.2 %collective-permute-start.9 = (bf16[2,400,256]{2,1,0:T(8,128)(2,1)S(1)}, bf16[2,400,256]{2,1,0:T(8,128)(2,1)}, u32[]{:S(2)}, u32[]{:S(2)}) collective-permute-start(bf16[2,400,256]{2,1,0:T(8,128)(2,1)S(1)} %get-tuple-element.17), channel_id=1, source_target_pairs={{0,12},{4,8},{8,4},{12,0},{1,13},{5,9},{9,5},{13,1},{2,14},{6,10},... | collective-permute-start | bytes 1228808 | tf_op jit(solution)/shard_map/ppermute | solution.py:382
  41.2 0.0 copy-done.6
  41.2 0.0 copy-done.2
  41.2 0.0 copy-done.3
  41.2 0.0 copy-done.4
  41.2 0.1 collective-permute-start.8
  41.3 15.2 %prefill_first.1.refs_4_ = f32[2,144,1536]{2,1,0:T(8,128)} custom-call(s32[1]{0:T(128)} %bitcast.2.me_ref, bf16[192,2048]{1,0:T(8,128)(2,1)} %q_ref.5, bf16[1,400,256]{2,1,0:T(8,128)(2,1)} %make_block.1.own_info_ref.refs_0_, bf16[1,400,256]{2,1,0:T(8,128)(2,1)} %make_block.1.own_info_ref.refs_0_, bf16[1,400,256]{2,1,0:T(8,128)(2,1)} %copy-done.1, ...), custom_call_target="tpu_custom_call" | custom-call | flops 2113929216 | bytes 4000000 | tf_op jit(solution)/shard_map/prefill_first/pallas_call | solution.py:346
  56.5 0.0 all-to-all-done.in_ref
  56.5 1.5 %join_shares.1 = bf16[32,4,2048]{2,1,0:T(4,128)(2,1)} custom-call(bf16[32,80,128]{2,1,0:T(8,128)(2,1)S(1)} %all-to-all-done.in_ref), custom_call_target="tpu_custom_call" | custom-call | flops 1000000 | bytes 1200000 | tf_op jit(solution)/shard_map/join_shares/pallas_call | solution.py:168
  58.0 10.3 %all-to-all-start.1 = ((bf16[32,4,2048]{2,1,0:T(4,128)(2,1)}), bf16[32,4,2048]{2,1,0:T(4,128)(2,1)S(1)}, u32[]{:S(2)}, u32[]{:S(2)}) async-start(bf16[32,4,2048]{2,1,0:T(4,128)(2,1)} %join_shares.1), calls=%async_computation.1 | async-start | bytes 1048576 | tf_op jit(solution)/shard_map/all_to_all | solution.py:389
  68.3 0.0 collective-permute-done.7.refs_1_
  68.3 0.0 collective-permute-done.8.refs_2_
  68.3 0.0 collective-permute-done.9.refs_3_
  68.3 0.0 collective-permute-done.6.refs_0_
  68.4 18.5 %prefill_last.1 = bf16[192,2048]{1,0:T(8,128)(2,1)} custom-call(s32[1]{0:T(128)} %bitcast.2.me_ref, bf16[192,2048]{1,0:T(8,128)(2,1)} %q_ref.5, bf16[1,400,256]{2,1,0:T(8,128)(2,1)} %make_block.1.own_info_ref.refs_0_, bf16[4,400,256]{2,1,0:T(8,128)(2,1)} %collective-permute-done.6.refs_0_, bf16[2,400,256]{2,1,0:T(8,128)(2,1)} %collective-permute-done.7.refs_1_, ...), custom_call_target="tpu_custom_call" | custom-call | flops 3019898880 | bytes 4000000 | tf_op jit(solution)/shard_map/prefill_last/pallas_call | solution.py:346
  86.8 0.0 all-to-all-done.1
  86.8 1.1 %copy.9 = bf16[4,32,2048]{2,1,0:T(8,128)(2,1)} copy(bf16[4,32,2048]{2,0,1:T(4,128)(2,1)S(1)} %bitcast.4) | data formatting | bytes 1048576
Async XLA Ops:
  2.4 14.2 %copy-start = (bf16[1,400,256]{2,1,0:T(8,128)(2,1)S(1)}, bf16[1,400,256]{2,1,0:T(8,128)(2,1)}, u32[]{:S(2)}) copy-start(bf16[1,400,256]{2,1,0:T(8,128)(2,1)} %make_block.1.own_info_ref.refs_0_) | copy-start | bytes 614404
  2.4 14.2 %collective-permute-start = (bf16[1,400,256]{2,1,0:T(8,128)(2,1)}, bf16[1,400,256]{2,1,0:T(8,128)(2,1)S(1)}, u32[]{:S(2)}, u32[]{:S(2)}) collective-permute-start(bf16[1,400,256]{2,1,0:T(8,128)(2,1)} %make_block.1.own_info_ref.refs_0_), channel_id=1, source_target_pairs={{0,32},{32,64},{64,96},{1,33},{33,65},{65,97},{2,34},{34,66},{66,9... | collective-permute-start | bytes 614408 | tf_op jit(solution)/shard_map/ppermute | solution.py:372
  6.0 10.6 %collective-permute-start.1 = (bf16[1,400,256]{2,1,0:T(8,128)(2,1)}, bf16[1,400,256]{2,1,0:T(8,128)(2,1)S(1)}, u32[]{:S(2)}, u32[]{:S(2)}) collective-permute-start(bf16[1,400,256]{2,1,0:T(8,128)(2,1)} %make_block.1.own_info_ref.refs_0_), channel_id=1, source_target_pairs={{0,64},{32,96},{1,65},{33,97},{2,66},{34,98},{3,67},{35,99},{4,68}... | collective-permute-start | bytes 614408 | tf_op jit(solution)/shard_map/ppermute | solution.py:373
  16.5 18.7 %copy-start.1 = (bf16[1,400,256]{2,1,0:T(8,128)(2,1)}, bf16[1,400,256]{2,1,0:T(8,128)(2,1)S(1)}, u32[]{:S(2)}) copy-start(bf16[1,400,256]{2,1,0:T(8,128)(2,1)S(1)} %collective-permute-done.refs_1_) | copy-start | bytes 614404
  16.6 7.9 %copy-start.5 = (bf16[1,400,256]{2,1,0:T(8,128)(2,1)}, bf16[1,400,256]{2,1,0:T(8,128)(2,1)S(1)}, u32[]{:S(2)}) copy-start(bf16[1,400,256]{2,1,0:T(8,128)(2,1)S(1)} %collective-permute-done.1.refs_5_) | copy-start | bytes 614404
  16.6 7.8 %collective-permute-start.2 = (bf16[1,400,256]{2,1,0:T(8,128)(2,1)S(1)}, bf16[1,400,256]{2,1,0:T(8,128)(2,1)S(1)}, u32[]{:S(2)}, u32[]{:S(2)}) collective-permute-start(bf16[1,400,256]{2,1,0:T(8,128)(2,1)S(1)} %get-tuple-element.25), channel_id=1, source_target_pairs={{0,16},{16,0},{1,17},{17,1},{2,18},{18,2},{3,19},{19,3},{4,20},{20... | collective-permute-start | bytes 614408 | tf_op jit(solution)/shard_map/ppermute | solution.py:378
  17.2 17.9 %collective-permute-start.3 = (bf16[1,400,256]{2,1,0:T(8,128)(2,1)S(1)}, bf16[1,400,256]{2,1,0:T(8,128)(2,1)S(1)}, u32[]{:S(2)}, u32[]{:S(2)}) collective-permute-start(bf16[1,400,256]{2,1,0:T(8,128)(2,1)S(1)} %collective-permute-done.refs_1_), channel_id=1, source_target_pairs={{0,8},{4,12},{8,0},{12,4},{1,9},{5,13},{9,1},{13,5},{2,10},{6,14},... | collective-permute-start | bytes 614408 | tf_op jit(solution)/shard_map/ppermute | solution.py:377
  21.1 14.1 %collective-permute-start.4 = (bf16[1,400,256]{2,1,0:T(8,128)(2,1)S(1)}, bf16[1,400,256]{2,1,0:T(8,128)(2,1)S(1)}, u32[]{:S(2)}, u32[]{:S(2)}) collective-permute-start(bf16[1,400,256]{2,1,0:T(8,128)(2,1)S(1)} %collective-permute-done.refs_1_), channel_id=1, source_target_pairs={{0,4},{4,0},{8,12},{12,8},{1,5},{5,1},{9,13},{13,9},{2,6},{6,2},{1... | collective-permute-start | bytes 614408 | tf_op jit(solution)/shard_map/ppermute | solution.py:377
  22.1 13.1 %collective-permute-start.5 = (bf16[1,400,256]{2,1,0:T(8,128)(2,1)S(1)}, bf16[1,400,256]{2,1,0:T(8,128)(2,1)S(1)}, u32[]{:S(2)}, u32[]{:S(2)}) collective-permute-start(bf16[1,400,256]{2,1,0:T(8,128)(2,1)S(1)} %collective-permute-done.refs_1_), channel_id=1, source_target_pairs={{0,12},{4,8},{8,4},{12,0},{1,13},{5,9},{9,5},{13,1},{2,14},{6,10},... | collective-permute-start | bytes 614408 | tf_op jit(solution)/shard_map/ppermute | solution.py:377
  24.5 16.8 %copy-start.6 = (bf16[1,400,256]{2,1,0:T(8,128)(2,1)}, bf16[1,400,256]{2,1,0:T(8,128)(2,1)S(1)}, u32[]{:S(2)}) copy-start(bf16[1,400,256]{2,1,0:T(8,128)(2,1)S(1)} %collective-permute-done.2.refs_6_) | copy-start | bytes 614404
  25.3 31.2 %all-to-all-start = ((bf16[32,80,128]{2,1,0:T(8,128)(2,1)}), bf16[32,80,128]{2,1,0:T(8,128)(2,1)S(1)}, u32[]{:S(2)}, u32[]{:S(2)}) async-start(bf16[32,80,128]{2,1,0:T(8,128)(2,1)} %decode_partials.1), calls=%async_computation | async-start | bytes 1310720 | tf_op jit(solution)/shard_map/all_to_all | solution.py:384
  35.2 6.1 %copy-start.2 = (bf16[1,400,256]{2,1,0:T(8,128)(2,1)}, bf16[1,400,256]{2,1,0:T(8,128)(2,1)S(1)}, u32[]{:S(2)}) copy-start(bf16[1,400,256]{2,1,0:T(8,128)(2,1)S(1)} %collective-permute-done.3.refs_2_) | copy-start | bytes 614404
  35.2 6.0 %copy-start.3 = (bf16[1,400,256]{2,1,0:T(8,128)(2,1)}, bf16[1,400,256]{2,1,0:T(8,128)(2,1)S(1)}, u32[]{:S(2)}) copy-start(bf16[1,400,256]{2,1,0:T(8,128)(2,1)S(1)} %collective-permute-done.4.refs_3_) | copy-start | bytes 614404
  35.2 6.0 %copy-start.4 = (bf16[1,400,256]{2,1,0:T(8,128)(2,1)}, bf16[1,400,256]{2,1,0:T(8,128)(2,1)S(1)}, u32[]{:S(2)}) copy-start(bf16[1,400,256]{2,1,0:T(8,128)(2,1)S(1)} %collective-permute-done.5.refs_4_) | copy-start | bytes 614404
  36.4 31.9 %collective-permute-start.6 = (bf16[4,400,256]{2,1,0:T(8,128)(2,1)S(1)}, bf16[4,400,256]{2,1,0:T(8,128)(2,1)}, u32[]{:S(2)}, u32[]{:S(2)}) collective-permute-start(bf16[4,400,256]{2,1,0:T(8,128)(2,1)S(1)} %pad_maximum_fusion), channel_id=1, source_target_pairs={{0,16},{16,0},{1,17},{17,1},{2,18},{18,2},{3,19},{19,3},{4,20},{20... | collective-permute-start | bytes 2457608 | tf_op jit(solution)/shard_map/ppermute | solution.py:379
  36.8 31.6 %collective-permute-start.7 = (bf16[2,400,256]{2,1,0:T(8,128)(2,1)S(1)}, bf16[2,400,256]{2,1,0:T(8,128)(2,1)}, u32[]{:S(2)}, u32[]{:S(2)}) collective-permute-start(bf16[2,400,256]{2,1,0:T(8,128)(2,1)S(1)} %get-tuple-element.17), channel_id=1, source_target_pairs={{0,8},{4,12},{8,0},{12,4},{1,9},{5,13},{9,1},{13,5},{2,10},{6,14},... | collective-permute-start | bytes 1228808 | tf_op jit(solution)/shard_map/ppermute | solution.py:382
  40.1 28.3 %collective-permute-start.9 = (bf16[2,400,256]{2,1,0:T(8,128)(2,1)S(1)}, bf16[2,400,256]{2,1,0:T(8,128)(2,1)}, u32[]{:S(2)}, u32[]{:S(2)}) collective-permute-start(bf16[2,400,256]{2,1,0:T(8,128)(2,1)S(1)} %get-tuple-element.17), channel_id=1, source_target_pairs={{0,12},{4,8},{8,4},{12,0},{1,13},{5,9},{9,5},{13,1},{2,14},{6,10},... | collective-permute-start | bytes 1228808 | tf_op jit(solution)/shard_map/ppermute | solution.py:382
  41.2 27.1 %collective-permute-start.8 = (bf16[2,400,256]{2,1,0:T(8,128)(2,1)}, bf16[2,400,256]{2,1,0:T(8,128)(2,1)}, u32[]{:S(2)}, u32[]{:S(2)}) collective-permute-start(bf16[2,400,256]{2,1,0:T(8,128)(2,1)} %get-tuple-element.18), channel_id=1, source_target_pairs={{0,4},{4,0},{8,12},{12,8},{1,5},{5,1},{9,13},{13,9},{2,6},{6,2},{1... | collective-permute-start | bytes 1228808 | tf_op jit(solution)/shard_map/ppermute | solution.py:382
  58.0 28.9 %all-to-all-start.1 = ((bf16[32,4,2048]{2,1,0:T(4,128)(2,1)}), bf16[32,4,2048]{2,1,0:T(4,128)(2,1)S(1)}, u32[]{:S(2)}, u32[]{:S(2)}) async-start(bf16[32,4,2048]{2,1,0:T(4,128)(2,1)} %join_shares.1), calls=%async_computation.1 | async-start | bytes 1048576 | tf_op jit(solution)/shard_map/all_to_all | solution.py:389

commit v8 on v7

--- a/solution.py
+++ b/solution.py
@@ -353,7 +353,7 @@
             scratch_shapes=scratch,
         ),
         out_shape=out_shape,
-        compiler_params=pltpu.CompilerParams(vmem_limit_bytes=62 * 1024 * 1024),
+        compiler_params=pltpu.CompilerParams(vmem_limit_bytes=52 * 1024 * 1024),
         cost_estimate=pl.CostEstimate(
             flops=4 * n * ROWS * ROWS * HEADS * HEAD_DIM, bytes_accessed=4_000_000, transcendentals=0
         ),

time: 88.3 us -> 87.4 us (0.990)
  Pallas kernels: 42.5 us -> 35.2 us
  starting transfers between devices: 38.9 us -> 45.6 us
    pallas_call x2, Pallas kernels: 33.6 us -> 26.3 us  [prefill_part(): pl.pallas_call(functools.partial(prefill_kernel, sources=sources, first=f...]
    all_to_all x1, starting transfers between devices: 10.3 us -> 17.2 us  [local(): spread = lax.all_to_all(join_shares(shares), CTX, 0, 0)]
  transfers between devices with their start and end apart: 12 -> 12, of which waited for: 1 -> 1; matrix products, arithmetic and copies ran while one was open for 2% -> 2% of each run, Pallas kernels for 46% -> 38%
where the time goes in v8:
time: 87.4 us; the launch traced here: 87 us
  starting transfers between devices  45.6 us (52%)
  Pallas kernels  35.2 us (40%)
  waiting for transfers between devices  2.38 us (3%)
  other arithmetic  2.01 us (2%)
  local copies, waits for them, and re-layouts  1.09 us (1%)
    pallas_call x2, Pallas kernels, prefill_part(): pl.pallas_call(functools.partial(prefill_kernel, sources=sources, first=f...  26.3 us
    all_to_all x1, starting transfers between devices, local(): spread = lax.all_to_all(join_shares(shares), CTX, 0, 0)  17.2 us
    all_to_all x1, starting transfers between devices, local(): shares = lax.all_to_all(shares, CTX, 0, 0)  9.83 us
    pallas_call x1, Pallas kernels, decode_partials(): pl.pallas_call(functools.partial(decode_kernel, per_step=per_step), grid_...  5.72 us
    ppermute x3, starting transfers between devices, local(): lax.ppermute(back1, 'z', [(i, i ^ k) for i in range(4)])  4.9 us
    ppermute x1, starting transfers between devices, local(): back2 = lax.ppermute(own, 'y', [(i, i + 2) for i in range(2)])  4.81 us
    ppermute x3, starting transfers between devices, local(): lax.ppermute(packs[min(k, 2)], 'z', [(i, i ^ k) for i in range(4)])  4.46 us
    ppermute x1, starting transfers between devices, local(): back1 = lax.ppermute(own, 'y', [(i, i + 1) for i in range(3)])  3.61 us
  transfers between devices with their start and end apart: 12, of which 1 were waited for; matrix products, arithmetic and copies ran while one was open for 2% of the time, Pallas kernels for 38%

profile of v8, /device:TPU:4, one launch (start us, length us, event | category | flops | bytes accessed | tf_op | source)
XLA Modules:
  0.0 87.0 jit_solution(5473938222048633611)
XLA Ops:
  0.6 1.7 %make_block.1.own_info_ref.refs_0_ = bf16[1,400,256]{2,1,0:T(8,128)(2,1)} custom-call(s32[1,192]{1,0:T(1,128)} %bitcast.6, bf16[384,256]{1,0:T(8,128)(2,1)} %bitcast.5), custom_call_target="tpu_custom_call" | custom-call | flops 1000 | bytes 400000 | tf_op jit(solution)/shard_map/make_block/pallas_call | solution.py:192
  2.3 0.0 copy-start
  2.3 3.6 %collective-permute-start = (bf16[1,400,256]{2,1,0:T(8,128)(2,1)}, bf16[1,400,256]{2,1,0:T(8,128)(2,1)S(1)}, u32[]{:S(2)}, u32[]{:S(2)}) collective-permute-start(bf16[1,400,256]{2,1,0:T(8,128)(2,1)} %make_block.1.own_info_ref.refs_0_), channel_id=1, source_target_pairs={{0,32},{32,64},{64,96},{1,33},{33,65},{65,97},{2,34},{34,66},{66,9... | collective-permute-start | bytes 614408 | tf_op jit(solution)/shard_map/ppermute | solution.py:372
  6.0 4.8 %collective-permute-start.1 = (bf16[1,400,256]{2,1,0:T(8,128)(2,1)}, bf16[1,400,256]{2,1,0:T(8,128)(2,1)S(1)}, u32[]{:S(2)}, u32[]{:S(2)}) collective-permute-start(bf16[1,400,256]{2,1,0:T(8,128)(2,1)} %make_block.1.own_info_ref.refs_0_), channel_id=1, source_target_pairs={{0,64},{32,96},{1,65},{33,97},{2,66},{34,98},{3,67},{35,99},{4,68}... | collective-permute-start | bytes 614408 | tf_op jit(solution)/shard_map/ppermute | solution.py:373
  10.8 5.7 %decode_partials.1 = bf16[32,80,128]{2,1,0:T(8,128)(2,1)} custom-call(s32[32]{0:T(128)} %len_ref.1, s32[1]{0:T(128)} %bitcast.2.me_ref, bf16[4,32,2048]{2,1,0:T(8,128)(2,1)} %q_ref.3, bf16[2,32,128,256]{3,2,1,0:T(8,128)(2,1)} %kv_ref.1, bf16[4,2,32,256]{3,2,1,0:T(8,128)(2,1)} %step_ref.1), custom_call_target="tpu_custom_call" | custom-call | flops 70000000 | bytes 5500000 | tf_op jit(solution)/shard_map/decode_partials/pallas_call | solution.py:124
  16.5 0.0 collective-permute-done.refs_1_
  16.5 0.0 collective-permute-done.1.refs_5_
  16.5 0.0 copy-done
  16.5 0.1 broadcast_select_fusion
  16.6 0.6 collective-permute-start.2
  17.2 3.9 %collective-permute-start.3 = (bf16[1,400,256]{2,1,0:T(8,128)(2,1)S(1)}, bf16[1,400,256]{2,1,0:T(8,128)(2,1)S(1)}, u32[]{:S(2)}, u32[]{:S(2)}) collective-permute-start(bf16[1,400,256]{2,1,0:T(8,128)(2,1)S(1)} %collective-permute-done.refs_1_), channel_id=1, source_target_pairs={{0,8},{4,12},{8,0},{12,4},{1,9},{5,13},{9,1},{13,5},{2,10},{6,14},... | collective-permute-start | bytes 614408 | tf_op jit(solution)/shard_map/ppermute | solution.py:377
  21.1 1.0 %collective-permute-start.4 = (bf16[1,400,256]{2,1,0:T(8,128)(2,1)S(1)}, bf16[1,400,256]{2,1,0:T(8,128)(2,1)S(1)}, u32[]{:S(2)}, u32[]{:S(2)}) collective-permute-start(bf16[1,400,256]{2,1,0:T(8,128)(2,1)S(1)} %collective-permute-done.refs_1_), channel_id=1, source_target_pairs={{0,4},{4,0},{8,12},{12,8},{1,5},{5,1},{9,13},{13,9},{2,6},{6,2},{1... | collective-permute-start | bytes 614408 | tf_op jit(solution)/shard_map/ppermute | solution.py:377
  22.1 0.0 collective-permute-start.5
  22.1 2.4 %collective-permute-done.2.refs_6_ = bf16[1,400,256]{2,1,0:T(8,128)(2,1)S(1)} collective-permute-done((bf16[1,400,256]{2,1,0:T(8,128)(2,1)S(1)}, bf16[1,400,256]{2,1,0:T(8,128)(2,1)S(1)}, u32[]{:S(2)}, u32[]{:S(2)}) %collective-permute-start.2) | collective-permute-done | bytes 204832 | tf_op jit(solution)/shard_map/ppermute | solution.py:378
  24.4 1.0 %pad_maximum_fusion.1 = (bf16[2,400,256]{2,1,0:T(8,128)(2,1)}, bf16[2,400,256]{2,1,0:T(8,128)(2,1)}) fusion(bf16[1,400,256]{2,1,0:T(8,128)(2,1)S(1)} %collective-permute-done.2.refs_6_, bf16[1,400,256]{2,1,0:T(8,128)(2,1)S(1)} %get-tuple-element.24, bf16[1,400,256]{2,1,0:T(8,128)(2,1)S(1)} %get-tuple-element.26), kind=kLoop, calls=%fused_computation.1 | loop fusion | flops 409600 | bytes 1433600 | tf_op jit(solution)/shard_map/concatenate | solution.py:380
  25.4 9.8 %all-to-all-start = ((bf16[32,80,128]{2,1,0:T(8,128)(2,1)}), bf16[32,80,128]{2,1,0:T(8,128)(2,1)S(1)}, u32[]{:S(2)}, u32[]{:S(2)}) async-start(bf16[32,80,128]{2,1,0:T(8,128)(2,1)} %decode_partials.1), calls=%async_computation | async-start | bytes 1310720 | tf_op jit(solution)/shard_map/all_to_all | solution.py:384
  35.2 0.0 collective-permute-done.3.refs_2_
  35.2 0.0 collective-permute-done.4.refs_3_
  35.3 0.0 collective-permute-done.5.refs_4_
  35.3 1.0 %pad_maximum_fusion = bf16[4,400,256]{2,1,0:T(8,128)(2,1)} fusion(bf16[1,400,256]{2,1,0:T(8,128)(2,1)S(1)} %collective-permute-done.5.refs_4_, bf16[1,400,256]{2,1,0:T(8,128)(2,1)S(1)} %collective-permute-done.4.refs_3_, bf16[1,400,256]{2,1,0:T(8,128)(2,1)S(1)} %collective-permute-done.3.refs_2_, bf16[1,400,256]{2,1,0:T(8,128)(2,1)S(1)} %collective-permute-done.refs_1_), kind=kLoop, calls=%fused_computation | loop fusion | flops 1228800 | bytes 1638400 | tf_op jit(solution)/shard_map/concatenate | solution.py:379
  36.3 0.2 collective-permute-start.6
  36.5 3.3 %collective-permute-start.7 = (bf16[2,400,256]{2,1,0:T(8,128)(2,1)}, bf16[2,400,256]{2,1,0:T(8,128)(2,1)S(1)}, u32[]{:S(2)}, u32[]{:S(2)}) collective-permute-start(bf16[2,400,256]{2,1,0:T(8,128)(2,1)} %get-tuple-element.17), channel_id=1, source_target_pairs={{0,8},{4,12},{8,0},{12,4},{1,9},{5,13},{9,1},{13,5},{2,10},{6,14},... | collective-permute-start | bytes 1228808 | tf_op jit(solution)/shard_map/ppermute | solution.py:382
  39.8 1.2 %collective-permute-start.9 = (bf16[2,400,256]{2,1,0:T(8,128)(2,1)}, bf16[2,400,256]{2,1,0:T(8,128)(2,1)S(1)}, u32[]{:S(2)}, u32[]{:S(2)}) collective-permute-start(bf16[2,400,256]{2,1,0:T(8,128)(2,1)} %get-tuple-element.17), channel_id=1, source_target_pairs={{0,12},{4,8},{8,4},{12,0},{1,13},{5,9},{9,5},{13,1},{2,14},{6,10},... | collective-permute-start | bytes 1228808 | tf_op jit(solution)/shard_map/ppermute | solution.py:382
  41.0 0.0 collective-permute-start.8
  41.0 8.0 %prefill_first.1.refs_4_ = f32[2,144,1536]{2,1,0:T(8,128)} custom-call(s32[1]{0:T(128)} %bitcast.2.me_ref, bf16[192,2048]{1,0:T(8,128)(2,1)} %q_ref.5, bf16[1,400,256]{2,1,0:T(8,128)(2,1)S(1)} %copy-done, bf16[1,400,256]{2,1,0:T(8,128)(2,1)S(1)} %copy-done, bf16[1,400,256]{2,1,0:T(8,128)(2,1)S(1)} %collective-permute-done.refs_1_, ...), custom_call_target="tpu_custom_call" | custom-call | flops 2113929216 | bytes 4000000 | tf_op jit(solution)/shard_map/prefill_first/pallas_call | solution.py:346
  49.0 0.0 all-to-all-done.in_ref
  49.0 1.5 %join_shares.1 = bf16[32,4,2048]{2,1,0:T(4,128)(2,1)} custom-call(bf16[32,80,128]{2,1,0:T(8,128)(2,1)S(1)} %all-to-all-done.in_ref), custom_call_target="tpu_custom_call" | custom-call | flops 1000000 | bytes 1200000 | tf_op jit(solution)/shard_map/join_shares/pallas_call | solution.py:168
  50.5 17.2 %all-to-all-start.1 = ((bf16[32,4,2048]{2,1,0:T(4,128)(2,1)}), bf16[32,4,2048]{2,1,0:T(4,128)(2,1)S(1)}, u32[]{:S(2)}, u32[]{:S(2)}) async-start(bf16[32,4,2048]{2,1,0:T(4,128)(2,1)} %join_shares.1), calls=%async_computation.1 | async-start | bytes 1048576 | tf_op jit(solution)/shard_map/all_to_all | solution.py:389
  67.7 0.0 collective-permute-done.7.refs_1_
  67.7 0.0 collective-permute-done.8.refs_2_
  67.7 0.0 collective-permute-done.9.refs_3_
  67.7 0.0 collective-permute-done.6.refs_0_
  67.7 18.2 %prefill_last.1 = bf16[192,2048]{1,0:T(8,128)(2,1)} custom-call(s32[1]{0:T(128)} %bitcast.2.me_ref, bf16[192,2048]{1,0:T(8,128)(2,1)} %q_ref.5, bf16[1,400,256]{2,1,0:T(8,128)(2,1)S(1)} %copy-done, bf16[4,400,256]{2,1,0:T(8,128)(2,1)} %collective-permute-done.6.refs_0_, bf16[2,400,256]{2,1,0:T(8,128)(2,1)S(1)} %collective-permute-done.7.refs_1_, ...), custom_call_target="tpu_custom_call" | custom-call | flops 3019898880 | bytes 4000000 | tf_op jit(solution)/shard_map/prefill_last/pallas_call | solution.py:346
  85.9 0.0 all-to-all-done.1
  85.9 1.1 %copy.9 = bf16[4,32,2048]{2,1,0:T(8,128)(2,1)} copy(bf16[4,32,2048]{2,0,1:T(4,128)(2,1)S(1)} %bitcast.4) | data formatting | bytes 1048576
Async XLA Ops:
  2.3 14.2 %copy-start = (bf16[1,400,256]{2,1,0:T(8,128)(2,1)S(1)}, bf16[1,400,256]{2,1,0:T(8,128)(2,1)}, u32[]{:S(2)}) copy-start(bf16[1,400,256]{2,1,0:T(8,128)(2,1)} %make_block.1.own_info_ref.refs_0_) | copy-start | bytes 614404
  2.3 14.2 %collective-permute-start = (bf16[1,400,256]{2,1,0:T(8,128)(2,1)}, bf16[1,400,256]{2,1,0:T(8,128)(2,1)S(1)}, u32[]{:S(2)}, u32[]{:S(2)}) collective-permute-start(bf16[1,400,256]{2,1,0:T(8,128)(2,1)} %make_block.1.own_info_ref.refs_0_), channel_id=1, source_target_pairs={{0,32},{32,64},{64,96},{1,33},{33,65},{65,97},{2,34},{34,66},{66,9... | collective-permute-start | bytes 614408 | tf_op jit(solution)/shard_map/ppermute | solution.py:372
  6.0 10.6 %collective-permute-start.1 = (bf16[1,400,256]{2,1,0:T(8,128)(2,1)}, bf16[1,400,256]{2,1,0:T(8,128)(2,1)S(1)}, u32[]{:S(2)}, u32[]{:S(2)}) collective-permute-start(bf16[1,400,256]{2,1,0:T(8,128)(2,1)} %make_block.1.own_info_ref.refs_0_), channel_id=1, source_target_pairs={{0,64},{32,96},{1,65},{33,97},{2,66},{34,98},{3,67},{35,99},{4,68}... | collective-permute-start | bytes 614408 | tf_op jit(solution)/shard_map/ppermute | solution.py:373
  16.6 7.8 %collective-permute-start.2 = (bf16[1,400,256]{2,1,0:T(8,128)(2,1)S(1)}, bf16[1,400,256]{2,1,0:T(8,128)(2,1)S(1)}, u32[]{:S(2)}, u32[]{:S(2)}) collective-permute-start(bf16[1,400,256]{2,1,0:T(8,128)(2,1)S(1)} %get-tuple-element.25), channel_id=1, source_target_pairs={{0,16},{16,0},{1,17},{17,1},{2,18},{18,2},{3,19},{19,3},{4,20},{20... | collective-permute-start | bytes 614408 | tf_op jit(solution)/shard_map/ppermute | solution.py:378
  17.2 18.1 %collective-permute-start.3 = (bf16[1,400,256]{2,1,0:T(8,128)(2,1)S(1)}, bf16[1,400,256]{2,1,0:T(8,128)(2,1)S(1)}, u32[]{:S(2)}, u32[]{:S(2)}) collective-permute-start(bf16[1,400,256]{2,1,0:T(8,128)(2,1)S(1)} %collective-permute-done.refs_1_), channel_id=1, source_target_pairs={{0,8},{4,12},{8,0},{12,4},{1,9},{5,13},{9,1},{13,5},{2,10},{6,14},... | collective-permute-start | bytes 614408 | tf_op jit(solution)/shard_map/ppermute | solution.py:377
  21.1 14.2 %collective-permute-start.4 = (bf16[1,400,256]{2,1,0:T(8,128)(2,1)S(1)}, bf16[1,400,256]{2,1,0:T(8,128)(2,1)S(1)}, u32[]{:S(2)}, u32[]{:S(2)}) collective-permute-start(bf16[1,400,256]{2,1,0:T(8,128)(2,1)S(1)} %collective-permute-done.refs_1_), channel_id=1, source_target_pairs={{0,4},{4,0},{8,12},{12,8},{1,5},{5,1},{9,13},{13,9},{2,6},{6,2},{1... | collective-permute-start | bytes 614408 | tf_op jit(solution)/shard_map/ppermute | solution.py:377
  22.1 13.2 %collective-permute-start.5 = (bf16[1,400,256]{2,1,0:T(8,128)(2,1)S(1)}, bf16[1,400,256]{2,1,0:T(8,128)(2,1)S(1)}, u32[]{:S(2)}, u32[]{:S(2)}) collective-permute-start(bf16[1,400,256]{2,1,0:T(8,128)(2,1)S(1)} %collective-permute-done.refs_1_), channel_id=1, source_target_pairs={{0,12},{4,8},{8,4},{12,0},{1,13},{5,9},{9,5},{13,1},{2,14},{6,10},... | collective-permute-start | bytes 614408 | tf_op jit(solution)/shard_map/ppermute | solution.py:377
  25.4 23.6 %all-to-all-start = ((bf16[32,80,128]{2,1,0:T(8,128)(2,1)}), bf16[32,80,128]{2,1,0:T(8,128)(2,1)S(1)}, u32[]{:S(2)}, u32[]{:S(2)}) async-start(bf16[32,80,128]{2,1,0:T(8,128)(2,1)} %decode_partials.1), calls=%async_computation | async-start | bytes 1310720 | tf_op jit(solution)/shard_map/all_to_all | solution.py:384
  36.3 31.4 %collective-permute-start.6 = (bf16[4,400,256]{2,1,0:T(8,128)(2,1)}, bf16[4,400,256]{2,1,0:T(8,128)(2,1)}, u32[]{:S(2)}, u32[]{:S(2)}) collective-permute-start(bf16[4,400,256]{2,1,0:T(8,128)(2,1)} %pad_maximum_fusion), channel_id=1, source_target_pairs={{0,16},{16,0},{1,17},{17,1},{2,18},{18,2},{3,19},{19,3},{4,20},{20... | collective-permute-start | bytes 2457608 | tf_op jit(solution)/shard_map/ppermute | solution.py:379
  36.5 31.2 %collective-permute-start.7 = (bf16[2,400,256]{2,1,0:T(8,128)(2,1)}, bf16[2,400,256]{2,1,0:T(8,128)(2,1)S(1)}, u32[]{:S(2)}, u32[]{:S(2)}) collective-permute-start(bf16[2,400,256]{2,1,0:T(8,128)(2,1)} %get-tuple-element.17), channel_id=1, source_target_pairs={{0,8},{4,12},{8,0},{12,4},{1,9},{5,13},{9,1},{13,5},{2,10},{6,14},... | collective-permute-start | bytes 1228808 | tf_op jit(solution)/shard_map/ppermute | solution.py:382
  39.8 27.9 %collective-permute-start.9 = (bf16[2,400,256]{2,1,0:T(8,128)(2,1)}, bf16[2,400,256]{2,1,0:T(8,128)(2,1)S(1)}, u32[]{:S(2)}, u32[]{:S(2)}) collective-permute-start(bf16[2,400,256]{2,1,0:T(8,128)(2,1)} %get-tuple-element.17), channel_id=1, source_target_pairs={{0,12},{4,8},{8,4},{12,0},{1,13},{5,9},{9,5},{13,1},{2,14},{6,10},... | collective-permute-start | bytes 1228808 | tf_op jit(solution)/shard_map/ppermute | solution.py:382
  41.0 26.7 %collective-permute-start.8 = (bf16[2,400,256]{2,1,0:T(8,128)(2,1)}, bf16[2,400,256]{2,1,0:T(8,128)(2,1)S(1)}, u32[]{:S(2)}, u32[]{:S(2)}) collective-permute-start(bf16[2,400,256]{2,1,0:T(8,128)(2,1)} %get-tuple-element.18), channel_id=1, source_target_pairs={{0,4},{4,0},{8,12},{12,8},{1,5},{5,1},{9,13},{13,9},{2,6},{6,2},{1... | collective-permute-start | bytes 1228808 | tf_op jit(solution)/shard_map/ppermute | solution.py:382
  50.5 35.5 %all-to-all-start.1 = ((bf16[32,4,2048]{2,1,0:T(4,128)(2,1)}), bf16[32,4,2048]{2,1,0:T(4,128)(2,1)S(1)}, u32[]{:S(2)}, u32[]{:S(2)}) async-start(bf16[32,4,2048]{2,1,0:T(4,128)(2,1)} %join_shares.1), calls=%async_computation.1 | async-start | bytes 1048576 | tf_op jit(solution)/shard_map/all_to_all | solution.py:389

commit v9 on v8

--- a/solution.py
+++ b/solution.py
@@ -132,7 +132,7 @@
                 pl.BlockSpec((STEPS, 2, 16, KV_HEADS * HEAD_DIM), lambda i, lens, me: (0, 0, me[0] // 16, 0)),
             ],
             out_specs=pl.BlockSpec((per_step, PACKED, HEAD_DIM), lambda i, *_: (i, 0, 0)),
-            scratch_shapes=[pltpu.VMEM((PER_SEQ * per_step, HEAD_DIM), jnp.float32)],
+            scratch_shapes=[pltpu.VMEM(((PER_SEQ + 1) * per_step, HEAD_DIM), jnp.float32)],
         ),
         out_shape=jax.ShapeDtypeStruct((SEQS, PACKED, HEAD_DIM), jnp.bfloat16),
         compiler_params=pltpu.CompilerParams(vmem_limit_bytes=62 * 1024 * 1024),
@@ -157,7 +157,7 @@
     acc = jnp.zeros((PER_SEQ, HEAD_DIM), jnp.float32)
     for i in range(SEQS):
         acc = acc + in_ref[i, :PER_SEQ, :].astype(jnp.float32) * columns[:PER_SEQ, i : i + 1]
-    joined[...] = acc
+    joined[:PER_SEQ, :] = acc
     heads = [joined[pl.ds(h, STEPS, stride=HEADS), :] for h in range(HEADS)]
     out = jnp.concatenate(heads, axis=1).astype(jnp.bfloat16)
     for i in range(SEQS):
@@ -170,7 +170,7 @@
         out_shape=jax.ShapeDtypeStruct((SEQS, STEPS, HEADS * HEAD_DIM), jnp.bfloat16),
         in_specs=[pl.BlockSpec(memory_space=pltpu.VMEM)],
         out_specs=pl.BlockSpec(memory_space=pltpu.VMEM),
-        scratch_shapes=[pltpu.VMEM((HEAD_DIM, HEAD_DIM), jnp.float32), pltpu.VMEM((PER_SEQ, HEAD_DIM), jnp.float32)],
+        scratch_shapes=[pltpu.VMEM((HEAD_DIM, HEAD_DIM), jnp.float32), pltpu.VMEM((PER_SEQ + HEADS, HEAD_DIM), jnp.float32)],
         compiler_params=pltpu.CompilerParams(vmem_limit_bytes=8 * 1024 * 1024),
         cost_estimate=pl.CostEstimate(flops=1_000_000, bytes_accessed=1_200_000, transcendentals=4096),
         name="join_shares",

time: 87.4 us -> 87.4 us (level)
  starting transfers between devices: 45.6 us -> 38.8 us
  Pallas kernels: 35.2 us -> 42 us
    all_to_all x1, starting transfers between devices: 17.2 us -> 10.4 us  [local(): spread = lax.all_to_all(join_shares(shares), CTX, 0, 0)]
    pallas_call x2, Pallas kernels: 26.3 us -> 33.1 us  [prefill_part(): pl.pallas_call(functools.partial(prefill_kernel, sources=sources, first=f...]
  transfers between devices with their start and end apart: 12 -> 12, of which waited for: 1 -> 1; matrix products, arithmetic and copies ran while one was open for 2% -> 2% of each run, Pallas kernels for 38% -> 46%
where the time goes in v9:
time: 87.4 us; the launch traced here: 87 us
  Pallas kernels  42 us (48%)
  starting transfers between devices  38.8 us (44%)
  waiting for transfers between devices  2.39 us (3%)
  other arithmetic  2.01 us (2%)
  local copies, waits for them, and re-layouts  1.09 us (1%)
    pallas_call x2, Pallas kernels, prefill_part(): pl.pallas_call(functools.partial(prefill_kernel, sources=sources, first=f...  33.1 us
    all_to_all x1, starting transfers between devices, local(): spread = lax.all_to_all(join_shares(shares), CTX, 0, 0)  10.4 us
    all_to_all x1, starting transfers between devices, local(): shares = lax.all_to_all(shares, CTX, 0, 0)  9.83 us
    pallas_call x1, Pallas kernels, decode_partials(): pl.pallas_call(functools.partial(decode_kernel, per_step=per_step), grid_...  5.72 us
    ppermute x3, starting transfers between devices, local(): lax.ppermute(back1, 'z', [(i, i ^ k) for i in range(4)])  4.9 us
    ppermute x1, starting transfers between devices, local(): back2 = lax.ppermute(own, 'y', [(i, i + 2) for i in range(2)])  4.81 us
    ppermute x3, starting transfers between devices, local(): lax.ppermute(packs[min(k, 2)], 'z', [(i, i ^ k) for i in range(4)])  4.46 us
    ppermute x1, starting transfers between devices, local(): back1 = lax.ppermute(own, 'y', [(i, i + 1) for i in range(3)])  3.61 us
  transfers between devices with their start and end apart: 12, of which 1 were waited for; matrix products, arithmetic and copies ran while one was open for 2% of the time, Pallas kernels for 46%

profile of v9, /device:TPU:4, one launch (start us, length us, event | category | flops | bytes accessed | tf_op | source)
XLA Modules:
  0.0 87.0 jit_solution(10595152543655377512)
XLA Ops:
  0.6 1.7 %make_block.1.own_info_ref.refs_0_ = bf16[1,400,256]{2,1,0:T(8,128)(2,1)} custom-call(s32[1,192]{1,0:T(1,128)} %bitcast.6, bf16[384,256]{1,0:T(8,128)(2,1)} %bitcast.5), custom_call_target="tpu_custom_call" | custom-call | flops 1000 | bytes 400000 | tf_op jit(solution)/shard_map/make_block/pallas_call | solution.py:192
  2.3 0.0 copy-start
  2.3 3.6 %collective-permute-start = (bf16[1,400,256]{2,1,0:T(8,128)(2,1)}, bf16[1,400,256]{2,1,0:T(8,128)(2,1)S(1)}, u32[]{:S(2)}, u32[]{:S(2)}) collective-permute-start(bf16[1,400,256]{2,1,0:T(8,128)(2,1)} %make_block.1.own_info_ref.refs_0_), channel_id=1, source_target_pairs={{0,32},{32,64},{64,96},{1,33},{33,65},{65,97},{2,34},{34,66},{66,9... | collective-permute-start | bytes 614408 | tf_op jit(solution)/shard_map/ppermute | solution.py:372
  6.0 4.8 %collective-permute-start.1 = (bf16[1,400,256]{2,1,0:T(8,128)(2,1)}, bf16[1,400,256]{2,1,0:T(8,128)(2,1)S(1)}, u32[]{:S(2)}, u32[]{:S(2)}) collective-permute-start(bf16[1,400,256]{2,1,0:T(8,128)(2,1)} %make_block.1.own_info_ref.refs_0_), channel_id=1, source_target_pairs={{0,64},{32,96},{1,65},{33,97},{2,66},{34,98},{3,67},{35,99},{4,68}... | collective-permute-start | bytes 614408 | tf_op jit(solution)/shard_map/ppermute | solution.py:373
  10.8 5.7 %decode_partials.1 = bf16[32,80,128]{2,1,0:T(8,128)(2,1)} custom-call(s32[32]{0:T(128)} %len_ref.1, s32[1]{0:T(128)} %bitcast.2.me_ref, bf16[4,32,2048]{2,1,0:T(8,128)(2,1)} %q_ref.3, bf16[2,32,128,256]{3,2,1,0:T(8,128)(2,1)} %kv_ref.1, bf16[4,2,32,256]{3,2,1,0:T(8,128)(2,1)} %step_ref.1), custom_call_target="tpu_custom_call" | custom-call | flops 70000000 | bytes 5500000 | tf_op jit(solution)/shard_map/decode_partials/pallas_call | solution.py:124
  16.5 0.0 collective-permute-done.refs_1_
  16.5 0.0 collective-permute-done.1.refs_5_
  16.5 0.0 copy-done
  16.5 0.1 broadcast_select_fusion
  16.6 0.6 collective-permute-start.2
  17.2 3.9 %collective-permute-start.3 = (bf16[1,400,256]{2,1,0:T(8,128)(2,1)S(1)}, bf16[1,400,256]{2,1,0:T(8,128)(2,1)S(1)}, u32[]{:S(2)}, u32[]{:S(2)}) collective-permute-start(bf16[1,400,256]{2,1,0:T(8,128)(2,1)S(1)} %collective-permute-done.refs_1_), channel_id=1, source_target_pairs={{0,8},{4,12},{8,0},{12,4},{1,9},{5,13},{9,1},{13,5},{2,10},{6,14},... | collective-permute-start | bytes 614408 | tf_op jit(solution)/shard_map/ppermute | solution.py:377
  21.1 1.0 %collective-permute-start.4 = (bf16[1,400,256]{2,1,0:T(8,128)(2,1)S(1)}, bf16[1,400,256]{2,1,0:T(8,128)(2,1)S(1)}, u32[]{:S(2)}, u32[]{:S(2)}) collective-permute-start(bf16[1,400,256]{2,1,0:T(8,128)(2,1)S(1)} %collective-permute-done.refs_1_), channel_id=1, source_target_pairs={{0,4},{4,0},{8,12},{12,8},{1,5},{5,1},{9,13},{13,9},{2,6},{6,2},{1... | collective-permute-start | bytes 614408 | tf_op jit(solution)/shard_map/ppermute | solution.py:377
  22.1 0.0 collective-permute-start.5
  22.1 2.4 %collective-permute-done.2.refs_6_ = bf16[1,400,256]{2,1,0:T(8,128)(2,1)S(1)} collective-permute-done((bf16[1,400,256]{2,1,0:T(8,128)(2,1)S(1)}, bf16[1,400,256]{2,1,0:T(8,128)(2,1)S(1)}, u32[]{:S(2)}, u32[]{:S(2)}) %collective-permute-start.2) | collective-permute-done | bytes 204832 | tf_op jit(solution)/shard_map/ppermute | solution.py:378
  24.4 1.0 %pad_maximum_fusion.1 = (bf16[2,400,256]{2,1,0:T(8,128)(2,1)}, bf16[2,400,256]{2,1,0:T(8,128)(2,1)}) fusion(bf16[1,400,256]{2,1,0:T(8,128)(2,1)S(1)} %collective-permute-done.2.refs_6_, bf16[1,400,256]{2,1,0:T(8,128)(2,1)S(1)} %get-tuple-element.24, bf16[1,400,256]{2,1,0:T(8,128)(2,1)S(1)} %get-tuple-element.26), kind=kLoop, calls=%fused_computation.1 | loop fusion | flops 409600 | bytes 1433600 | tf_op jit(solution)/shard_map/concatenate | solution.py:380
  25.4 9.8 %all-to-all-start = ((bf16[32,80,128]{2,1,0:T(8,128)(2,1)}), bf16[32,80,128]{2,1,0:T(8,128)(2,1)S(1)}, u32[]{:S(2)}, u32[]{:S(2)}) async-start(bf16[32,80,128]{2,1,0:T(8,128)(2,1)} %decode_partials.1), calls=%async_computation | async-start | bytes 1310720 | tf_op jit(solution)/shard_map/all_to_all | solution.py:384
  35.2 0.0 collective-permute-done.3.refs_2_
  35.2 0.0 collective-permute-done.4.refs_3_
  35.3 0.0 collective-permute-done.5.refs_4_
  35.3 1.0 %pad_maximum_fusion = bf16[4,400,256]{2,1,0:T(8,128)(2,1)} fusion(bf16[1,400,256]{2,1,0:T(8,128)(2,1)S(1)} %collective-permute-done.5.refs_4_, bf16[1,400,256]{2,1,0:T(8,128)(2,1)S(1)} %collective-permute-done.4.refs_3_, bf16[1,400,256]{2,1,0:T(8,128)(2,1)S(1)} %collective-permute-done.3.refs_2_, bf16[1,400,256]{2,1,0:T(8,128)(2,1)S(1)} %collective-permute-done.refs_1_), kind=kLoop, calls=%fused_computation | loop fusion | flops 1228800 | bytes 1638400 | tf_op jit(solution)/shard_map/concatenate | solution.py:379
  36.3 0.2 collective-permute-start.6
  36.5 3.3 %collective-permute-start.7 = (bf16[2,400,256]{2,1,0:T(8,128)(2,1)}, bf16[2,400,256]{2,1,0:T(8,128)(2,1)S(1)}, u32[]{:S(2)}, u32[]{:S(2)}) collective-permute-start(bf16[2,400,256]{2,1,0:T(8,128)(2,1)} %get-tuple-element.17), channel_id=1, source_target_pairs={{0,8},{4,12},{8,0},{12,4},{1,9},{5,13},{9,1},{13,5},{2,10},{6,14},... | collective-permute-start | bytes 1228808 | tf_op jit(solution)/shard_map/ppermute | solution.py:382
  39.8 1.2 %collective-permute-start.9 = (bf16[2,400,256]{2,1,0:T(8,128)(2,1)}, bf16[2,400,256]{2,1,0:T(8,128)(2,1)S(1)}, u32[]{:S(2)}, u32[]{:S(2)}) collective-permute-start(bf16[2,400,256]{2,1,0:T(8,128)(2,1)} %get-tuple-element.17), channel_id=1, source_target_pairs={{0,12},{4,8},{8,4},{12,0},{1,13},{5,9},{9,5},{13,1},{2,14},{6,10},... | collective-permute-start | bytes 1228808 | tf_op jit(solution)/shard_map/ppermute | solution.py:382
  41.0 0.0 collective-permute-start.8
  41.0 14.8 %prefill_first.1.refs_4_ = f32[2,144,1536]{2,1,0:T(8,128)} custom-call(s32[1]{0:T(128)} %bitcast.2.me_ref, bf16[192,2048]{1,0:T(8,128)(2,1)} %q_ref.5, bf16[1,400,256]{2,1,0:T(8,128)(2,1)S(1)} %copy-done, bf16[1,400,256]{2,1,0:T(8,128)(2,1)S(1)} %copy-done, bf16[1,400,256]{2,1,0:T(8,128)(2,1)S(1)} %collective-permute-done.refs_1_, ...), custom_call_target="tpu_custom_call" | custom-call | flops 2113929216 | bytes 4000000 | tf_op jit(solution)/shard_map/prefill_first/pallas_call | solution.py:346
  55.8 0.0 all-to-all-done.in_ref
  55.8 1.5 %join_shares.1 = bf16[32,4,2048]{2,1,0:T(4,128)(2,1)} custom-call(bf16[32,80,128]{2,1,0:T(8,128)(2,1)S(1)} %all-to-all-done.in_ref), custom_call_target="tpu_custom_call" | custom-call | flops 1000000 | bytes 1200000 | tf_op jit(solution)/shard_map/join_shares/pallas_call | solution.py:168
  57.3 10.4 %all-to-all-start.1 = ((bf16[32,4,2048]{2,1,0:T(4,128)(2,1)}), bf16[32,4,2048]{2,1,0:T(4,128)(2,1)S(1)}, u32[]{:S(2)}, u32[]{:S(2)}) async-start(bf16[32,4,2048]{2,1,0:T(4,128)(2,1)} %join_shares.1), calls=%async_computation.1 | async-start | bytes 1048576 | tf_op jit(solution)/shard_map/all_to_all | solution.py:389
  67.7 0.0 collective-permute-done.7.refs_1_
  67.7 0.0 collective-permute-done.8.refs_2_
  67.7 0.0 collective-permute-done.9.refs_3_
  67.7 0.0 collective-permute-done.6.refs_0_
  67.7 18.2 %prefill_last.1 = bf16[192,2048]{1,0:T(8,128)(2,1)} custom-call(s32[1]{0:T(128)} %bitcast.2.me_ref, bf16[192,2048]{1,0:T(8,128)(2,1)} %q_ref.5, bf16[1,400,256]{2,1,0:T(8,128)(2,1)S(1)} %copy-done, bf16[4,400,256]{2,1,0:T(8,128)(2,1)} %collective-permute-done.6.refs_0_, bf16[2,400,256]{2,1,0:T(8,128)(2,1)S(1)} %collective-permute-done.7.refs_1_, ...), custom_call_target="tpu_custom_call" | custom-call | flops 3019898880 | bytes 4000000 | tf_op jit(solution)/shard_map/prefill_last/pallas_call | solution.py:346
  85.9 0.0 all-to-all-done.1
  85.9 1.1 %copy.9 = bf16[4,32,2048]{2,1,0:T(8,128)(2,1)} copy(bf16[4,32,2048]{2,0,1:T(4,128)(2,1)S(1)} %bitcast.4) | data formatting | bytes 1048576
Async XLA Ops:
  2.3 14.2 %copy-start = (bf16[1,400,256]{2,1,0:T(8,128)(2,1)S(1)}, bf16[1,400,256]{2,1,0:T(8,128)(2,1)}, u32[]{:S(2)}) copy-start(bf16[1,400,256]{2,1,0:T(8,128)(2,1)} %make_block.1.own_info_ref.refs_0_) | copy-start | bytes 614404
  2.3 14.2 %collective-permute-start = (bf16[1,400,256]{2,1,0:T(8,128)(2,1)}, bf16[1,400,256]{2,1,0:T(8,128)(2,1)S(1)}, u32[]{:S(2)}, u32[]{:S(2)}) collective-permute-start(bf16[1,400,256]{2,1,0:T(8,128)(2,1)} %make_block.1.own_info_ref.refs_0_), channel_id=1, source_target_pairs={{0,32},{32,64},{64,96},{1,33},{33,65},{65,97},{2,34},{34,66},{66,9... | collective-permute-start | bytes 614408 | tf_op jit(solution)/shard_map/ppermute | solution.py:372
  6.0 10.6 %collective-permute-start.1 = (bf16[1,400,256]{2,1,0:T(8,128)(2,1)}, bf16[1,400,256]{2,1,0:T(8,128)(2,1)S(1)}, u32[]{:S(2)}, u32[]{:S(2)}) collective-permute-start(bf16[1,400,256]{2,1,0:T(8,128)(2,1)} %make_block.1.own_info_ref.refs_0_), channel_id=1, source_target_pairs={{0,64},{32,96},{1,65},{33,97},{2,66},{34,98},{3,67},{35,99},{4,68}... | collective-permute-start | bytes 614408 | tf_op jit(solution)/shard_map/ppermute | solution.py:373
  16.6 7.8 %collective-permute-start.2 = (bf16[1,400,256]{2,1,0:T(8,128)(2,1)S(1)}, bf16[1,400,256]{2,1,0:T(8,128)(2,1)S(1)}, u32[]{:S(2)}, u32[]{:S(2)}) collective-permute-start(bf16[1,400,256]{2,1,0:T(8,128)(2,1)S(1)} %get-tuple-element.25), channel_id=1, source_target_pairs={{0,16},{16,0},{1,17},{17,1},{2,18},{18,2},{3,19},{19,3},{4,20},{20... | collective-permute-start | bytes 614408 | tf_op jit(solution)/shard_map/ppermute | solution.py:378
  17.2 18.1 %collective-permute-start.3 = (bf16[1,400,256]{2,1,0:T(8,128)(2,1)S(1)}, bf16[1,400,256]{2,1,0:T(8,128)(2,1)S(1)}, u32[]{:S(2)}, u32[]{:S(2)}) collective-permute-start(bf16[1,400,256]{2,1,0:T(8,128)(2,1)S(1)} %collective-permute-done.refs_1_), channel_id=1, source_target_pairs={{0,8},{4,12},{8,0},{12,4},{1,9},{5,13},{9,1},{13,5},{2,10},{6,14},... | collective-permute-start | bytes 614408 | tf_op jit(solution)/shard_map/ppermute | solution.py:377
  21.1 14.2 %collective-permute-start.4 = (bf16[1,400,256]{2,1,0:T(8,128)(2,1)S(1)}, bf16[1,400,256]{2,1,0:T(8,128)(2,1)S(1)}, u32[]{:S(2)}, u32[]{:S(2)}) collective-permute-start(bf16[1,400,256]{2,1,0:T(8,128)(2,1)S(1)} %collective-permute-done.refs_1_), channel_id=1, source_target_pairs={{0,4},{4,0},{8,12},{12,8},{1,5},{5,1},{9,13},{13,9},{2,6},{6,2},{1... | collective-permute-start | bytes 614408 | tf_op jit(solution)/shard_map/ppermute | solution.py:377
  22.1 13.2 %collective-permute-start.5 = (bf16[1,400,256]{2,1,0:T(8,128)(2,1)S(1)}, bf16[1,400,256]{2,1,0:T(8,128)(2,1)S(1)}, u32[]{:S(2)}, u32[]{:S(2)}) collective-permute-start(bf16[1,400,256]{2,1,0:T(8,128)(2,1)S(1)} %collective-permute-done.refs_1_), channel_id=1, source_target_pairs={{0,12},{4,8},{8,4},{12,0},{1,13},{5,9},{9,5},{13,1},{2,14},{6,10},... | collective-permute-start | bytes 614408 | tf_op jit(solution)/shard_map/ppermute | solution.py:377
  25.4 30.4 %all-to-all-start = ((bf16[32,80,128]{2,1,0:T(8,128)(2,1)}), bf16[32,80,128]{2,1,0:T(8,128)(2,1)S(1)}, u32[]{:S(2)}, u32[]{:S(2)}) async-start(bf16[32,80,128]{2,1,0:T(8,128)(2,1)} %decode_partials.1), calls=%async_computation | async-start | bytes 1310720 | tf_op jit(solution)/shard_map/all_to_all | solution.py:384
  36.3 31.4 %collective-permute-start.6 = (bf16[4,400,256]{2,1,0:T(8,128)(2,1)}, bf16[4,400,256]{2,1,0:T(8,128)(2,1)}, u32[]{:S(2)}, u32[]{:S(2)}) collective-permute-start(bf16[4,400,256]{2,1,0:T(8,128)(2,1)} %pad_maximum_fusion), channel_id=1, source_target_pairs={{0,16},{16,0},{1,17},{17,1},{2,18},{18,2},{3,19},{19,3},{4,20},{20... | collective-permute-start | bytes 2457608 | tf_op jit(solution)/shard_map/ppermute | solution.py:379
  36.5 31.2 %collective-permute-start.7 = (bf16[2,400,256]{2,1,0:T(8,128)(2,1)}, bf16[2,400,256]{2,1,0:T(8,128)(2,1)S(1)}, u32[]{:S(2)}, u32[]{:S(2)}) collective-permute-start(bf16[2,400,256]{2,1,0:T(8,128)(2,1)} %get-tuple-element.17), channel_id=1, source_target_pairs={{0,8},{4,12},{8,0},{12,4},{1,9},{5,13},{9,1},{13,5},{2,10},{6,14},... | collective-permute-start | bytes 1228808 | tf_op jit(solution)/shard_map/ppermute | solution.py:382
  39.8 27.9 %collective-permute-start.9 = (bf16[2,400,256]{2,1,0:T(8,128)(2,1)}, bf16[2,400,256]{2,1,0:T(8,128)(2,1)S(1)}, u32[]{:S(2)}, u32[]{:S(2)}) collective-permute-start(bf16[2,400,256]{2,1,0:T(8,128)(2,1)} %get-tuple-element.17), channel_id=1, source_target_pairs={{0,12},{4,8},{8,4},{12,0},{1,13},{5,9},{9,5},{13,1},{2,14},{6,10},... | collective-permute-start | bytes 1228808 | tf_op jit(solution)/shard_map/ppermute | solution.py:382
  41.0 26.7 %collective-permute-start.8 = (bf16[2,400,256]{2,1,0:T(8,128)(2,1)}, bf16[2,400,256]{2,1,0:T(8,128)(2,1)S(1)}, u32[]{:S(2)}, u32[]{:S(2)}) collective-permute-start(bf16[2,400,256]{2,1,0:T(8,128)(2,1)} %get-tuple-element.18), channel_id=1, source_target_pairs={{0,4},{4,0},{8,12},{12,8},{1,5},{5,1},{9,13},{13,9},{2,6},{6,2},{1... | collective-permute-start | bytes 1228808 | tf_op jit(solution)/shard_map/ppermute | solution.py:382
  57.3 28.7 %all-to-all-start.1 = ((bf16[32,4,2048]{2,1,0:T(4,128)(2,1)}), bf16[32,4,2048]{2,1,0:T(4,128)(2,1)S(1)}, u32[]{:S(2)}, u32[]{:S(2)}) async-start(bf16[32,4,2048]{2,1,0:T(4,128)(2,1)} %join_shares.1), calls=%async_computation.1 | async-start | bytes 1048576 | tf_op jit(solution)/shard_map/all_to_all | solution.py:389
